TPU v7x, 32 devices: a whole 2x2x4 slice. The times are simulated.
32 devices in a mesh: dp: 8 (over z, y), tensor: 4 (over x, core).
Axes of the slice: x: 2, y: 2, z: 4, core: 2. Of those that a mesh axis runs over, the one named last changes fastest.
Arguments:
- tokens: bfloat16 [16384, 1536], P(('dp', 'tensor')), may hold values from -6 to 6
- first_gain: bfloat16 [1536], P('dp'), may hold values from 0.099609375 to 1.8984375
- query_weight: bfloat16 [1536, 1536], P('dp', 'tensor'), may hold values from -0.15625 to 0.15625
- key_weight: bfloat16 [1536, 768], P('dp', 'tensor'), may hold values from -0.15625 to 0.15625
- value_weight: bfloat16 [1536, 768], P('dp', 'tensor'), may hold values from -0.15625 to 0.15625
- output_weight: bfloat16 [1536, 1536], P('tensor', 'dp'), may hold values from -1.25 to 1.25
- second_gain: bfloat16 [1536], P('dp'), may hold values from 0.099609375 to 1.8984375
- gate_weight: bfloat16 [1536, 4096], P('dp', 'tensor'), may hold values from -0.15625 to 0.15625
- up_weight: bfloat16 [1536, 4096], P('dp', 'tensor'), may hold values from -0.15625 to 0.15625
- down_weight: bfloat16 [4096, 1536], P('tensor', 'dp'), may hold values from -0.09375 to 0.09375
- cotangent: bfloat16 [16384, 1536], P(('dp', 'tensor')), may hold values from -6 to 6
Outputs:
- layer_out: bfloat16 [16384, 1536], P(('dp', 'tensor'))
- tokens_grad: bfloat16 [16384, 1536], P(('dp', 'tensor'))
- first_gain_grad: float32 [1536], P('dp')
- query_weight_grad: float32 [1536, 1536], P('dp', 'tensor')
- key_weight_grad: float32 [1536, 768], P('dp', 'tensor')
- value_weight_grad: float32 [1536, 768], P('dp', 'tensor')
- output_weight_grad: float32 [1536, 1536], P('tensor', 'dp')
- second_gain_grad: float32 [1536], P('dp')
- gate_weight_grad: float32 [1536, 4096], P('dp', 'tensor')
- up_weight_grad: float32 [1536, 4096], P('dp', 'tensor')
- down_weight_grad: float32 [4096, 1536], P('tensor', 'dp')
All inputs are finite; a program needn't handle non-finite values.
Results may differ from a plain program's by a relative error of at most 0.023.
Values may be sent and summed in bfloat16 or wider, within the bound.
A program may use at most 192 MiB of HBM per device.

v0:
```python
import jax
import jax.numpy as jnp
from jax import lax
from jax.sharding import PartitionSpec as P

HEAD = 96
LENGTH = 1024
QBLOCK = 512


norm_eps = 1e-05
rope_base = 100000.0


def angles(row_count):
    half_head = HEAD // 2
    frequency = rope_base ** (jnp.arange(half_head, dtype=jnp.float32) * (-2.0 / HEAD))
    places = (jnp.arange(row_count, dtype=jnp.int32) % LENGTH).astype(jnp.float32)
    turned = places[:, None] * frequency[None, :]
    return (jnp.cos(turned), jnp.sin(turned))


def rotate(rows, cosine_table, sine_table):
    half_head = HEAD // 2
    first_half = rows[..., :half_head]
    second_half = rows[..., half_head:]
    cosine_rows = cosine_table[:, None, :]
    sine_rows = sine_table[:, None, :]
    return jnp.concatenate(
        [
            first_half * cosine_rows - second_half * sine_rows,
            second_half * cosine_rows + first_half * sine_rows,
        ],
        axis=-1,
    )


def unrotate(rows, cosine_table, sine_table):
    half_head = HEAD // 2
    first_half = rows[..., :half_head]
    second_half = rows[..., half_head:]
    cosine_rows = cosine_table[:, None, :]
    sine_rows = sine_table[:, None, :]
    return jnp.concatenate(
        [
            first_half * cosine_rows + second_half * sine_rows,
            second_half * cosine_rows - first_half * sine_rows,
        ],
        axis=-1,
    )


def contract_rows(left_matrix, right_matrix):
    return lax.dot_general(
        left_matrix, right_matrix, (((0,), (0,)), ((), ())), preferred_element_type=jnp.float32
    )


def times_transpose(left_matrix, right_matrix):
    return lax.dot_general(
        left_matrix, right_matrix, (((1,), (1,)), ((), ())), preferred_element_type=jnp.float32
    )


def local(
    tokens,
    first_gain,
    query_weight,
    key_weight,
    value_weight,
    output_weight,
    second_gain,
    gate_weight,
    up_weight,
    down_weight,
    cotangent,
):
    shards = (
        first_gain,
        query_weight,
        key_weight,
        value_weight,
        output_weight,
        second_gain,
        gate_weight,
        up_weight,
        down_weight,
    )
    gathered = (
        lax.all_gather(first_gain, "dp", axis=0, tiled=True),
        lax.all_gather(query_weight, "dp", axis=0, tiled=True),
        lax.all_gather(key_weight, "dp", axis=0, tiled=True),
        lax.all_gather(value_weight, "dp", axis=0, tiled=True),
        lax.all_gather(output_weight, "dp", axis=1, tiled=True),
        lax.all_gather(second_gain, "dp", axis=0, tiled=True),
        lax.all_gather(gate_weight, "dp", axis=0, tiled=True),
        lax.all_gather(up_weight, "dp", axis=0, tiled=True),
        lax.all_gather(down_weight, "dp", axis=1, tiled=True),
    )
    gain_one = gathered[0].astype(jnp.float32)
    gain_two = gathered[5].astype(jnp.float32)
    activations = tokens.astype(jnp.float32)
    inverse_one = lax.rsqrt(jnp.mean(activations * activations, axis=-1, keepdims=True) + norm_eps)
    normed = lax.all_gather(
        (activations * inverse_one * gain_one).astype(jnp.bfloat16), "tensor", axis=0, tiled=True
    )
    row_count = normed.shape[0]
    local_heads = query_weight.shape[1] // HEAD
    local_groups = key_weight.shape[1] // HEAD
    group_size = local_heads // local_groups
    cosine_table, sine_table = angles(row_count)
    query_rows = jnp.dot(normed, gathered[1], preferred_element_type=jnp.float32)
    key_rows = jnp.dot(normed, gathered[2], preferred_element_type=jnp.float32)
    values = jnp.dot(normed, gathered[3], preferred_element_type=jnp.float32).astype(jnp.bfloat16)
    values = values.reshape(row_count, local_groups, HEAD)
    queries = rotate(query_rows.reshape(row_count, local_heads, HEAD), cosine_table, sine_table)
    queries = queries.astype(jnp.bfloat16).reshape(row_count, local_groups, group_size, HEAD)
    keys = rotate(key_rows.reshape(row_count, local_groups, HEAD), cosine_table, sine_table)
    keys = keys.astype(jnp.bfloat16)
    block_count = row_count // QBLOCK
    scale_factor = HEAD ** (-0.5)

    def block_scores(block_index):
        row_start = block_index * QBLOCK
        seq_start = row_start // LENGTH * LENGTH
        query_block = lax.dynamic_slice_in_dim(queries, row_start, QBLOCK, 0)
        key_block = lax.dynamic_slice_in_dim(keys, seq_start, LENGTH, 0)
        value_block = lax.dynamic_slice_in_dim(values, seq_start, LENGTH, 0)
        scores = (
            jnp.einsum("qgrd,kgd->grqk", query_block, key_block, preferred_element_type=jnp.float32)
            * scale_factor
        )
        query_place = row_start - seq_start + jnp.arange(QBLOCK, dtype=jnp.int32)
        causal = jnp.arange(LENGTH, dtype=jnp.int32)[None, :] <= query_place[:, None]
        scores = jnp.where(causal, scores, -1e30)
        return (query_block, key_block, value_block, scores)

    def attend_block(block_index):
        query_block, key_block, value_block, scores = block_scores(block_index)
        largest = jnp.max(scores, axis=-1, keepdims=True)
        exponent = jnp.exp(scores - largest)
        totals = jnp.sum(exponent, axis=-1, keepdims=True)
        softmax_rows = exponent / totals
        attended_block = jnp.einsum(
            "grqk,kgd->qgrd",
            softmax_rows.astype(jnp.bfloat16),
            value_block,
            preferred_element_type=jnp.float32,
        ).astype(jnp.bfloat16)
        return (attended_block, largest[..., 0] + jnp.log(totals[..., 0]))

    attended, log_totals = lax.map(attend_block, jnp.arange(block_count, dtype=jnp.int32))
    attended = attended.reshape(row_count, local_heads * HEAD)
    attention_terms = jnp.dot(attended, gathered[4], preferred_element_type=jnp.float32)
    hidden_state = activations + lax.psum_scatter(
        attention_terms, "tensor", scatter_dimension=0, tiled=True
    )
    inverse_two = lax.rsqrt(
        jnp.mean(hidden_state * hidden_state, axis=-1, keepdims=True) + norm_eps
    )
    normed_two = lax.all_gather(
        (hidden_state * inverse_two * gain_two).astype(jnp.bfloat16), "tensor", axis=0, tiled=True
    )
    gate_rows = jnp.dot(normed_two, gathered[6], preferred_element_type=jnp.float32)
    up_rows = jnp.dot(normed_two, gathered[7], preferred_element_type=jnp.float32)
    sigmoid_gate = jax.nn.sigmoid(gate_rows)
    inner_rows = (gate_rows * sigmoid_gate * up_rows).astype(jnp.bfloat16)
    feedforward_terms = jnp.dot(inner_rows, gathered[8], preferred_element_type=jnp.float32)
    layer_out = hidden_state + lax.psum_scatter(
        feedforward_terms.astype(jnp.bfloat16), "tensor", scatter_dimension=0, tiled=True
    ).astype(jnp.float32)
    backward_weights = (
        lax.all_gather(shards[0], "dp", axis=0, tiled=True),
        lax.all_gather(shards[1], "dp", axis=0, tiled=True),
        lax.all_gather(shards[2], "dp", axis=0, tiled=True),
        lax.all_gather(shards[3], "dp", axis=0, tiled=True),
        lax.all_gather(shards[4], "dp", axis=1, tiled=True),
        lax.all_gather(shards[5], "dp", axis=0, tiled=True),
        lax.all_gather(shards[6], "dp", axis=0, tiled=True),
        lax.all_gather(shards[7], "dp", axis=0, tiled=True),
        lax.all_gather(shards[8], "dp", axis=1, tiled=True),
    )
    out_rows = lax.all_gather(cotangent, "tensor", axis=0, tiled=True)
    down_weight_grad = contract_rows(inner_rows, out_rows)
    inner_grad = times_transpose(out_rows, backward_weights[8])
    up_grad = (inner_grad * gate_rows * sigmoid_gate).astype(jnp.bfloat16)
    gate_grad = (
        inner_grad * up_rows * sigmoid_gate * (1.0 + gate_rows * (1.0 - sigmoid_gate))
    ).astype(jnp.bfloat16)
    gate_weight_grad = contract_rows(normed_two, gate_grad)
    up_weight_grad = contract_rows(normed_two, up_grad)
    normed_two_terms = times_transpose(gate_grad, backward_weights[6]) + times_transpose(
        up_grad, backward_weights[7]
    )
    normed_two_grad = lax.psum_scatter(
        normed_two_terms.astype(jnp.bfloat16), "tensor", scatter_dimension=0, tiled=True
    ).astype(jnp.float32)
    second_gain_part = jnp.sum(normed_two_grad * hidden_state * inverse_two, axis=0)
    scaled_two = normed_two_grad * gain_two
    hidden_grad = (
        cotangent.astype(jnp.float32)
        + inverse_two * scaled_two
        - hidden_state
        * inverse_two**3
        * jnp.mean(scaled_two * hidden_state, axis=-1, keepdims=True)
    )
    branch_grad = lax.all_gather(hidden_grad.astype(jnp.bfloat16), "tensor", axis=0, tiled=True)
    output_weight_grad = contract_rows(attended, branch_grad)
    attended_grad = times_transpose(branch_grad, backward_weights[4]).astype(jnp.bfloat16)
    attended_grad = attended_grad.reshape(row_count, local_groups, group_size, HEAD)

    def attend_back(carry, block_index):
        key_total, value_total = carry
        query_block, key_block, value_block, scores = block_scores(block_index)
        row_start = block_index * QBLOCK
        seq_start = row_start // LENGTH * LENGTH
        softmax_rows = jnp.exp(scores - log_totals[block_index][..., None])
        grad_block = lax.dynamic_slice_in_dim(attended_grad, row_start, QBLOCK, 0)
        prob_grad = jnp.einsum(
            "qgrd,kgd->grqk", grad_block, value_block, preferred_element_type=jnp.float32
        )
        centre = jnp.sum(softmax_rows * prob_grad, axis=-1, keepdims=True)
        score_grad = (softmax_rows * (prob_grad - centre)).astype(jnp.bfloat16)
        query_part = (
            jnp.einsum("grqk,kgd->qgrd", score_grad, key_block, preferred_element_type=jnp.float32)
            * scale_factor
        )
        key_part = (
            jnp.einsum(
                "grqk,qgrd->kgd", score_grad, query_block, preferred_element_type=jnp.float32
            )
            * scale_factor
        )
        value_part = jnp.einsum(
            "grqk,qgrd->kgd",
            softmax_rows.astype(jnp.bfloat16),
            grad_block,
            preferred_element_type=jnp.float32,
        )
        key_total = lax.dynamic_update_slice_in_dim(
            key_total,
            lax.dynamic_slice_in_dim(key_total, seq_start, LENGTH, 0) + key_part,
            seq_start,
            0,
        )
        value_total = lax.dynamic_update_slice_in_dim(
            value_total,
            lax.dynamic_slice_in_dim(value_total, seq_start, LENGTH, 0) + value_part,
            seq_start,
            0,
        )
        return ((key_total, value_total), query_part)

    zero_rows = jnp.zeros((row_count, local_groups, HEAD), jnp.float32)
    (keys_grad, values_grad), queries_grad = lax.scan(
        attend_back, (zero_rows, zero_rows), jnp.arange(block_count, dtype=jnp.int32)
    )
    query_back = unrotate(
        queries_grad.reshape(row_count, local_heads, HEAD), cosine_table, sine_table
    )
    query_back = query_back.astype(jnp.bfloat16).reshape(row_count, local_heads * HEAD)
    key_back = unrotate(keys_grad, cosine_table, sine_table).astype(jnp.bfloat16)
    key_back = key_back.reshape(row_count, local_groups * HEAD)
    value_back = values_grad.astype(jnp.bfloat16).reshape(row_count, local_groups * HEAD)
    query_weight_grad = contract_rows(normed, query_back)
    key_weight_grad = contract_rows(normed, key_back)
    value_weight_grad = contract_rows(normed, value_back)
    normed_terms = (
        times_transpose(query_back, backward_weights[1])
        + times_transpose(key_back, backward_weights[2])
        + times_transpose(value_back, backward_weights[3])
    )
    normed_grad = lax.psum_scatter(
        normed_terms.astype(jnp.bfloat16), "tensor", scatter_dimension=0, tiled=True
    ).astype(jnp.float32)
    first_gain_part = jnp.sum(normed_grad * activations * inverse_one, axis=0)
    scaled_one = normed_grad * gain_one
    tokens_grad = (
        hidden_grad
        + inverse_one * scaled_one
        - activations * inverse_one**3 * jnp.mean(scaled_one * activations, axis=-1, keepdims=True)
    )
    summed = (
        lax.psum_scatter(
            first_gain_part.astype(jnp.bfloat16), "dp", scatter_dimension=0, tiled=True
        ).astype(jnp.float32),
        lax.psum_scatter(
            query_weight_grad.astype(jnp.bfloat16), "dp", scatter_dimension=0, tiled=True
        ).astype(jnp.float32),
        lax.psum_scatter(
            key_weight_grad.astype(jnp.bfloat16), "dp", scatter_dimension=0, tiled=True
        ).astype(jnp.float32),
        lax.psum_scatter(
            value_weight_grad.astype(jnp.bfloat16), "dp", scatter_dimension=0, tiled=True
        ).astype(jnp.float32),
        lax.psum_scatter(
            output_weight_grad.astype(jnp.bfloat16), "dp", scatter_dimension=1, tiled=True
        ).astype(jnp.float32),
        lax.psum_scatter(
            second_gain_part.astype(jnp.bfloat16), "dp", scatter_dimension=0, tiled=True
        ).astype(jnp.float32),
        lax.psum_scatter(
            gate_weight_grad.astype(jnp.bfloat16), "dp", scatter_dimension=0, tiled=True
        ).astype(jnp.float32),
        lax.psum_scatter(
            up_weight_grad.astype(jnp.bfloat16), "dp", scatter_dimension=0, tiled=True
        ).astype(jnp.float32),
        lax.psum_scatter(
            down_weight_grad.astype(jnp.bfloat16), "dp", scatter_dimension=1, tiled=True
        ).astype(jnp.float32),
    )
    gain_sums = lax.psum((summed[0], summed[5]), "tensor")
    return (
        layer_out.astype(jnp.bfloat16),
        tokens_grad.astype(jnp.bfloat16),
        gain_sums[0],
        summed[1],
        summed[2],
        summed[3],
        summed[4],
        gain_sums[1],
        summed[6],
        summed[7],
        summed[8],
    )


def solution(mesh):
    in_specs = (
        P(("dp", "tensor"), None),
        P("dp"),
        P("dp", "tensor"),
        P("dp", "tensor"),
        P("dp", "tensor"),
        P("tensor", "dp"),
        P("dp"),
        P("dp", "tensor"),
        P("dp", "tensor"),
        P("tensor", "dp"),
        P(("dp", "tensor"), None),
    )
    out_specs = (
        P(("dp", "tensor"), None),
        P(("dp", "tensor"), None),
        P("dp"),
        P("dp", "tensor"),
        P("dp", "tensor"),
        P("dp", "tensor"),
        P("tensor", "dp"),
        P("dp"),
        P("dp", "tensor"),
        P("dp", "tensor"),
        P("tensor", "dp"),
    )
    return jax.shard_map(local, mesh=mesh, in_specs=in_specs, out_specs=out_specs, check_vma=False)
```

profile of v0, /device:TPU:0, one launch (start us, length us, event | category | flops | bytes accessed | tf_op | source)
XLA Modules:
  0.0 1355.9 jit_solution(5599474263890192128)
XLA Ops:
  13.4 23.4 %all-reduce.6 = (bf16[1536]{0:T(1024)(128)(2,1)S(1)}, bf16[1536]{0:T(1024)(128)(2,1)S(1)}) all-reduce(bf16[1536]{0:T(1024)(128)(2,1)S(1)} %dynamic-update-slice, bf16[1536]{0:T(1024)(128)(2,1)S(1)} %dynamic-update-slice.1), channel_id=1, replica_groups=mesh['dp'=8,'tensor'=4] {'dp'}, use_global_device_ids=true, to_apply=%add | all-reduce | flops 3072 | bytes 12288
  41.9 32.3 %all_gather.49 = bf16[1536,192]{1,0:T(8,128)(2,1)S(1)} all-gather(bf16[192,192]{1,0:T(8,128)(2,1)S(1)} %copy-done.31), channel_id=1, replica_groups=mesh['dp'=8,'tensor'=4] {'dp'}, dimensions={0}, use_global_device_ids=true | all-gather | bytes 663552 | tf_op jit(solution)/shard_map/all_gather | solution.py:92
  74.3 32.6 %all_gather.48 = bf16[1536,192]{1,0:T(8,128)(2,1)S(1)} all-gather(bf16[192,192]{1,0:T(8,128)(2,1)S(1)} %copy-done.32), channel_id=1, replica_groups=mesh['dp'=8,'tensor'=4] {'dp'}, dimensions={0}, use_global_device_ids=true | all-gather | bytes 663552 | tf_op jit(solution)/shard_map/all_gather | solution.py:93
  108.3 5.2 fusion.82
  113.8 14.3 %all-gather.12.cloned.1.call-done = bf16[1536,384]{1,0:T(8,128)(2,1)} async-done(((bf16[192,384]{1,0:T(8,128)(2,1)}), bf16[1536,384]{1,0:T(8,128)(2,1)}) %all-gather.12.cloned.1.call-update) | async-done | bytes 1179664 | tf_op jit(solution)/shard_map/all_gather | solution.py:91
  128.1 5.1 fusion.83
  134.0 5.9 convolution_convert_fusion.9
  140.0 40.9 %while.30 = (s32[]{:T(128)}, bf16[4,512,2,2,96]{1,4,3,2,0:T(8,128)(2,1)}, f32[4,2,2,512]{3,2,1,0:T(2,128)}, s32[4]{0:T(128)S(1)}, bf16[2048,2,96]{0,2,1:T(8,128)...) while((s32[]{:T(128)}, ...), condition=%wide.region_4.5_spmd, body=%wide.region_1.4_spmd.sunk | while | flops 831191552 | bytes 28905900 | solution.py:152
  186.0 9.8 fusion.84
  196.5 97.3 %reduce-scatter.12.cloned.1.call-done = f32[512,1536]{1,0:T(8,128)} async-done(((f32[2048,1536]{1,0:T(8,128)}), f32[512,1536]{1,0:T(8,128)}) %reduce-scatter.12.cloned.1.call-update) | async-done | bytes 3145744 | tf_op jit(solution)/shard_map/reduce_scatter | solution.py:155
  300.8 55.6 %all-gather.20.cloned.1.call-done = bf16[1536,1024]{1,0:T(8,128)(2,1)} async-done(((bf16[192,1024]{1,0:T(8,128)(2,1)}), bf16[1536,1024]{1,0:T(8,128)(2,1)}) %all-gather.20.cloned.1.call-update) | async-done | bytes 3145744 | tf_op jit(solution)/shard_map/all_gather | solution.py:97
  356.4 47.0 %all-gather.16.cloned.1.call-done = bf16[2048,1536]{1,0:T(8,128)(2,1)} async-done(((bf16[512,1536]{1,0:T(8,128)(2,1)}), bf16[2048,1536]{1,0:T(8,128)(2,1)}) %all-gather.16.cloned.1.call-update) | async-done | bytes 6291472 | tf_op jit(solution)/shard_map/all_gather | solution.py:161
  403.4 11.8 fusion.86
  415.2 50.9 %all-gather.18.cloned.1.call-done = bf16[1536,1024]{1,0:T(8,128)(2,1)} async-done(((bf16[192,1024]{1,0:T(8,128)(2,1)}), bf16[1536,1024]{1,0:T(8,128)(2,1)}) %all-gather.18.cloned.1.call-update) | async-done | bytes 3145744 | tf_op jit(solution)/shard_map/all_gather | solution.py:96
  466.1 11.7 fusion.85
  477.8 49.6 %all-gather.22.cloned.1.call-done = bf16[1024,1536]{0,1:T(8,128)(2,1)} async-done(((bf16[1024,192]{0,1:T(8,128)(2,1)}), bf16[1024,1536]{0,1:T(8,128)(2,1)}) %all-gather.22.cloned.1.call-update) | async-done | bytes 3145744 | tf_op jit(solution)/shard_map/all_gather | solution.py:98
  527.4 46.6 %all-gather.24.cloned.1.call-done = bf16[2048,1536]{1,0:T(8,128)(2,1)} async-done(((bf16[512,1536]{1,0:T(8,128)(2,1)}), bf16[2048,1536]{1,0:T(8,128)(2,1)}) %all-gather.24.cloned.1.call-update) | async-done | bytes 6291472 | tf_op jit(solution)/shard_map/all_gather | solution.py:183
  574.0 18.5 %multiply_convert_fusion = (bf16[2048,1024]{1,0:T(8,128)(2,1)}, bf16[2048,1024]{1,0:T(8,128)(2,1)S(1)}, bf16[2048,1024]{1,0:T(8,128)(2,1)}) fusion(f32[2048,1024]{1,0:T(8,128)} %fusion.85, f32[2048,1024]{1,0:T(8,128)} %fusion.86, bf16[2048,1536]{1,0:T(8,128)(2,1)} %all-gather.24.cloned.1.call-done, bf16[1024,1536]{0,1:T(8,128)(2,1)} %all-gather.22.cloned.1.call-done), kind=kOutput, calls=%fused_computation.67 | convolution fusion | flops 6476005376 | bytes 38797312 | tf_op jit(solution)/shard_map/dot_general | solution.py:60
  592.5 9.8 fusion.87
  602.3 12.1 add_convert_fusion.1
  614.5 58.5 %reduce-scatter.16.cloned.1.call-done = bf16[512,1536]{1,0:T(8,128)(2,1)} async-done(((bf16[2048,1536]{1,0:T(8,128)(2,1)}), bf16[512,1536]{1,0:T(8,128)(2,1)}) %reduce-scatter.16.cloned.1.call-update) | async-done | bytes 1572880 | tf_op jit(solution)/shard_map/reduce_scatter | solution.py:195
  678.9 11.3 convolution_convert_fusion.1
  690.2 11.3 convolution_convert_fusion.2
  701.6 11.5 convolution_convert_fusion.3
  713.2 12.2 all-gather.26.cloned.1.call-done
  725.4 6.7 convolution_convert_fusion.6
  733.6 146.3 %while.31 = (s32[]{:T(128)}, f32[2048,2,96]{0,2,1:T(8,128)S(1)}, f32[2048,2,96]{0,2,1:T(8,128)}, f32[4,512,2,2,96]{1,0,4,3,2:T(4,128)}, s32[4]{0:T(128)S(1)}, /*...) while((s32[]{:T(128)}, f32[2048,2,96]{0,2,1:T(8,128)S(1)}, ...), condition=%wide.region_12.13_spmd, body=%wide.region_10.12_spmd.sunk | while | flops 2046032384 | bytes 93778528 | solution.py:255
  754.0 16.1 %dynamic_update_slice.46 = f32[4,512,2,2,96]{1,0,4,3,2:T(4,128)} dynamic-update-slice(f32[4,512,2,2,96]{1,0,4,3,2:T(4,128)} %get-tuple-element.487, f32[1,512,2,2,96]{1,0,4,3,2:T(1,128)S(1)} %copy.58, s32[]{:T(128)S(6)} %copy.79, s32[]{:T(128)} %constant.183.clone.1..sunk.1, s32[]{:T(128)} %constant.183.clone.1..sunk.1, s32[]{:T(128)} %constant.183.clone.1..sunk.1, s32[]{:T(128)} %constant.183.clone.1..sunk.1) | dynamic-update-slice | bytes 1572868 | tf_op jit(solution)/shard_map/while/body/jit(dynamic_update_index_in_dim)/dynamic_update_slice | solution.py:255
  790.6 16.1 %dynamic_update_slice.46 = f32[4,512,2,2,96]{1,0,4,3,2:T(4,128)} dynamic-update-slice(f32[4,512,2,2,96]{1,0,4,3,2:T(4,128)} %get-tuple-element.487, f32[1,512,2,2,96]{1,0,4,3,2:T(1,128)S(1)} %copy.58, s32[]{:T(128)S(6)} %copy.79, s32[]{:T(128)} %constant.183.clone.1..sunk.1, s32[]{:T(128)} %constant.183.clone.1..sunk.1, s32[]{:T(128)} %constant.183.clone.1..sunk.1, s32[]{:T(128)} %constant.183.clone.1..sunk.1) | dynamic-update-slice | bytes 1572868 | tf_op jit(solution)/shard_map/while/body/jit(dynamic_update_index_in_dim)/dynamic_update_slice | solution.py:255
  827.1 16.1 %dynamic_update_slice.46 = f32[4,512,2,2,96]{1,0,4,3,2:T(4,128)} dynamic-update-slice(f32[4,512,2,2,96]{1,0,4,3,2:T(4,128)} %get-tuple-element.487, f32[1,512,2,2,96]{1,0,4,3,2:T(1,128)S(1)} %copy.58, s32[]{:T(128)S(6)} %copy.79, s32[]{:T(128)} %constant.183.clone.1..sunk.1, s32[]{:T(128)} %constant.183.clone.1..sunk.1, s32[]{:T(128)} %constant.183.clone.1..sunk.1, s32[]{:T(128)} %constant.183.clone.1..sunk.1) | dynamic-update-slice | bytes 1572868 | tf_op jit(solution)/shard_map/while/body/jit(dynamic_update_index_in_dim)/dynamic_update_slice | solution.py:255
  863.7 16.2 %dynamic_update_slice.46 = f32[4,512,2,2,96]{1,0,4,3,2:T(4,128)} dynamic-update-slice(f32[4,512,2,2,96]{1,0,4,3,2:T(4,128)} %get-tuple-element.487, f32[1,512,2,2,96]{1,0,4,3,2:T(1,128)S(1)} %copy.58, s32[]{:T(128)S(6)} %copy.79, s32[]{:T(128)} %constant.183.clone.1..sunk.1, s32[]{:T(128)} %constant.183.clone.1..sunk.1, s32[]{:T(128)} %constant.183.clone.1..sunk.1, s32[]{:T(128)} %constant.183.clone.1..sunk.1) | dynamic-update-slice | bytes 1572868 | tf_op jit(solution)/shard_map/while/body/jit(dynamic_update_index_in_dim)/dynamic_update_slice | solution.py:255
  881.2 5.8 convolution_convert_fusion.8
  887.7 5.8 convolution_convert_fusion.7
  893.6 7.3 convolution_convert_fusion.4
  901.0 5.4 reshape.195
  915.2 7.8 fusion.89
  922.9 6.6 fusion.88
  929.5 12.2 add_convert_fusion
  943.7 11.0 convolution_convert_fusion
  961.5 62.4 %reduce-scatter.22.cloned.1.call-done = bf16[192,192]{1,0:T(8,128)(2,1)} async-done(((bf16[1536,192]{1,0:T(8,128)(2,1)}), bf16[192,192]{1,0:T(8,128)(2,1)}) %reduce-scatter.22.cloned.1.call-update) | async-done | bytes 73744 | tf_op jit(solution)/shard_map/reduce_scatter | solution.py:290
  1025.5 63.1 %reduce-scatter.24.cloned.1.call-done = bf16[192,192]{1,0:T(8,128)(2,1)} async-done(((bf16[1536,192]{1,0:T(8,128)(2,1)}), bf16[192,192]{1,0:T(8,128)(2,1)}) %reduce-scatter.24.cloned.1.call-update) | async-done | bytes 73744 | tf_op jit(solution)/shard_map/reduce_scatter | solution.py:293
  1090.2 65.1 %reduce-scatter.26.cloned.1.call-done = bf16[384,192]{0,1:T(8,128)(2,1)} async-done(((bf16[384,1536]{0,1:T(8,128)(2,1)}), bf16[384,192]{0,1:T(8,128)(2,1)}) %reduce-scatter.26.cloned.1.call-update) | async-done | bytes 147472 | tf_op jit(solution)/shard_map/reduce_scatter | solution.py:296
  1156.9 65.6 %reduce-scatter.20.cloned.1.call-done = bf16[192,384]{1,0:T(8,128)(2,1)} async-done(((bf16[1536,384]{1,0:T(8,128)(2,1)}), bf16[192,384]{1,0:T(8,128)(2,1)}) %reduce-scatter.20.cloned.1.call-update) | async-done | bytes 147472 | tf_op jit(solution)/shard_map/reduce_scatter | solution.py:287
  1224.2 58.4 %reduce-scatter.18.cloned.1.call-done = bf16[512,1536]{1,0:T(8,128)(2,1)} async-done(((bf16[2048,1536]{1,0:T(8,128)(2,1)}), bf16[512,1536]{1,0:T(8,128)(2,1)}) %reduce-scatter.18.cloned.1.call-update) | async-done | bytes 1572880 | tf_op jit(solution)/shard_map/reduce_scatter | solution.py:273
  1285.6 21.7 %all-reduce.5 = (bf16[1536]{0:T(1024)(128)(2,1)S(1)}, bf16[1536]{0:T(1024)(128)(2,1)S(1)}) all-reduce(bf16[1536]{0:T(1024)(128)(2,1)S(1)} %get-tuple-element.237, bf16[1536]{0:T(1024)(128)(2,1)S(1)} %copy-done.41), channel_id=6, replica_groups=mesh['dp'=8,'tensor'=4] {'dp'}, use_global_device_ids=true, to_apply=%region_16.17.clone | all-reduce | flops 3072 | bytes 12288
  1307.4 6.7 all-reduce.4
  1314.1 29.4 %reduce-scatter.14.cloned.1.call-done = bf16[512,1536]{1,0:T(8,128)(2,1)} async-done(((bf16[2048,1536]{1,0:T(8,128)(2,1)}), bf16[512,1536]{1,0:T(8,128)(2,1)}) %reduce-scatter.14.cloned.1.call-update) | async-done | bytes 1572880 | tf_op jit(solution)/shard_map/reduce_scatter | solution.py:169
  1343.5 5.4 fusion.63
  (284 shorter events, 170.1 us)
Async XLA Ops:
  7.2 101.1 %all-gather.10.cloned.1.call-start = ((), (), s32[]{:S(2)}) async-start(), calls=%async_computation.11 | async-start | bytes 7864320 | tf_op jit(solution)/shard_map/all_gather | solution.py:104
  7.2 34.7 %copy-start.31 = (bf16[192,192]{1,0:T(8,128)(2,1)S(1)}, bf16[192,192]{1,0:T(8,128)(2,1)}, u32[]{:S(2)}) copy-start(bf16[192,192]{1,0:T(8,128)(2,1)} %param.18) | copy-start | bytes 221188
  9.1 65.2 %copy-start.32 = (bf16[192,192]{1,0:T(8,128)(2,1)S(1)}, bf16[192,192]{1,0:T(8,128)(2,1)}, u32[]{:S(2)}) copy-start(bf16[192,192]{1,0:T(8,128)(2,1)} %param.19) | copy-start | bytes 221188
  9.7 64.6 %copy-start.35 = (f32[512]{0:T(512)}, f32[512]{0:T(512)S(1)}, u32[]{:S(2)}) copy-start(f32[512]{0:T(512)S(1)} %get-tuple-element.301) | copy-start | bytes 6148
  40.4 87.8 %all-gather.12.cloned.1.call-start = ((), (), s32[]{:S(2)}) async-start(), calls=%async_computation.12 | async-start | bytes 1327104 | tf_op jit(solution)/shard_map/all_gather | solution.py:91
  41.1 144.9 %all-gather.14.cloned.1.call-start = ((), (), s32[]{:S(2)}) async-start(), calls=%async_computation.13 | async-start | bytes 1327104 | tf_op jit(solution)/shard_map/all_gather | solution.py:94
  41.8 252.0 %reduce-scatter.12.cloned.1.call-start = ((), (), s32[]{:S(2)}) async-start(), calls=%async_computation.14 | async-start | bytes 15728640 | tf_op jit(solution)/shard_map/reduce_scatter | solution.py:155
  74.3 39.3 %copy-start.11 = (bf16[1536,192]{1,0:T(8,128)(2,1)}, bf16[1536,192]{1,0:T(8,128)(2,1)S(1)}, u32[]{:S(2)}) copy-start(bf16[1536,192]{1,0:T(8,128)(2,1)S(1)} %all_gather.49) | copy-start | bytes 1769476
  106.8 27.2 %copy-start.20 = (bf16[1536,192]{1,0:T(8,128)(2,1)}, bf16[1536,192]{1,0:T(8,128)(2,1)S(1)}, u32[]{:S(2)}) copy-start(bf16[1536,192]{1,0:T(8,128)(2,1)S(1)} %all_gather.48) | copy-start | bytes 1769476
  108.3 25.0 %copy-start.7 = (f32[2048,48]{0,1:T(8,128)}, f32[2048,48]{0,1:T(8,128)S(1)}, u32[]{:S(2)}) copy-start(f32[2048,48]{0,1:T(8,128)S(1)} %get-tuple-element.298) | copy-start | bytes 1179652
  108.3 25.0 %copy-start.9 = (f32[2048,48]{0,1:T(8,128)}, f32[2048,48]{0,1:T(8,128)S(1)}, u32[]{:S(2)}) copy-start(f32[2048,48]{0,1:T(8,128)S(1)} %get-tuple-element.299) | copy-start | bytes 1179652
  195.9 160.5 %all-gather.20.cloned.1.call-start = ((), (), s32[]{:S(2)}) async-start(), calls=%async_computation.17 | async-start | bytes 3538944 | tf_op jit(solution)/shard_map/all_gather | solution.py:97
  196.5 206.9 %all-gather.16.cloned.1.call-start = ((), (), s32[]{:S(2)}) async-start(), calls=%async_computation.15 | async-start | bytes 7864320 | tf_op jit(solution)/shard_map/all_gather | solution.py:161
  196.5 479.6 %copy-start.27 = (f32[1536]{0:T(1024)}, f32[1536]{0:T(1024)S(1)}, u32[]{:S(2)}) copy-start(f32[1536]{0:T(1024)S(1)} %convert_element_type.199) | copy-start | bytes 18436
  296.7 379.5 %copy-start = (f32[512,1536]{1,0:T(8,128)}, f32[512,1536]{1,0:T(8,128)S(1)}, u32[]{:S(2)}) copy-start(f32[512,1536]{1,0:T(8,128)S(1)} %get-tuple-element.280) | copy-start | bytes 9437188
  296.7 379.4 %copy-start.33 = (f32[512]{0:T(512)}, f32[512]{0:T(512)S(1)}, u32[]{:S(2)}) copy-start(f32[512]{0:T(512)S(1)} %get-tuple-element.303) | copy-start | bytes 6148
  296.7 379.4 %copy-start.37 = (f32[512]{0:T(512)}, f32[512]{0:T(512)S(1)}, u32[]{:S(2)}) copy-start(f32[512]{0:T(512)S(1)} %get-tuple-element.302) | copy-start | bytes 6148
  298.5 167.6 %all-gather.18.cloned.1.call-start = ((), (), s32[]{:S(2)}) async-start(), calls=%async_computation.16 | async-start | bytes 3538944 | tf_op jit(solution)/shard_map/all_gather | solution.py:96
  299.2 228.1 %all-gather.22.cloned.1.call-start = ((), (), s32[]{:S(2)}) async-start(), calls=%async_computation.18 | async-start | bytes 3538944 | tf_op jit(solution)/shard_map/all_gather | solution.py:98
  300.0 274.0 %all-gather.24.cloned.1.call-start = ((), (), s32[]{:S(2)}) async-start(), calls=%async_computation.20 | async-start | bytes 7864320 | tf_op jit(solution)/shard_map/all_gather | solution.py:183
  300.7 372.3 %reduce-scatter.16.cloned.1.call-start = ((), (), s32[]{:S(2)}) async-start(), calls=%async_computation.21 | async-start | bytes 7864320 | tf_op jit(solution)/shard_map/reduce_scatter | solution.py:195
  574.0 18.5 %copy-start.45 = (bf16[1536,1024]{1,0:T(8,128)(2,1)S(1)}, bf16[1536,1024]{1,0:T(8,128)(2,1)}, u32[]{:S(2)}) copy-start(bf16[1536,1024]{1,0:T(8,128)(2,1)} %all-gather.18.cloned.1.call-done) | copy-start | bytes 9437188
  592.5 9.9 copy-start.46
  592.5 9.9 copy-start.44
  592.5 9.8 copy-start.47
  614.5 110.9 %all-gather.26.cloned.1.call-start = ((), (), s32[]{:S(2)}) async-start(), calls=%async_computation.22 | async-start | bytes 7864320 | tf_op jit(solution)/shard_map/all_gather | solution.py:207
  678.8 276.5 %reduce-scatter.32.cloned.1.call-start = ((), (), s32[]{:S(2)}) async-start(), calls=%async_computation.30 | async-start | bytes 3538944 | tf_op jit(solution)/shard_map/reduce_scatter | solution.py:308
  690.2 267.2 %reduce-scatter.30.cloned.1.call-start = ((), (), s32[]{:S(2)}) async-start(), calls=%async_computation.29 | async-start | bytes 3538944 | tf_op jit(solution)/shard_map/reduce_scatter | solution.py:305
  701.5 257.9 %reduce-scatter.28.cloned.1.call-start = ((), (), s32[]{:S(2)}) async-start(), calls=%async_computation.28 | async-start | bytes 3538944 | tf_op jit(solution)/shard_map/reduce_scatter | solution.py:302
  713.1 12.3 copy-start.26
  713.1 310.8 %reduce-scatter.22.cloned.1.call-start = ((), (), s32[]{:S(2)}) async-start(), calls=%async_computation.25 | async-start | bytes 884736 | tf_op jit(solution)/shard_map/reduce_scatter | solution.py:290
  733.5 146.3 %copy-start.8 = (f32[2048,48]{0,1:T(8,128)S(1)}, f32[2048,48]{0,1:T(8,128)}, u32[]{:S(2)}) copy-start(f32[2048,48]{0,1:T(8,128)} %copy-done.7) | copy-start | bytes 1179652
  887.1 201.5 %reduce-scatter.24.cloned.1.call-start = ((), (), s32[]{:S(2)}) async-start(), calls=%async_computation.26 | async-start | bytes 884736 | tf_op jit(solution)/shard_map/reduce_scatter | solution.py:293
  893.5 261.7 %reduce-scatter.26.cloned.1.call-start = ((), (), s32[]{:S(2)}) async-start(), calls=%async_computation.27 | async-start | bytes 1327104 | tf_op jit(solution)/shard_map/reduce_scatter | solution.py:296
  900.9 321.6 %reduce-scatter.20.cloned.1.call-start = ((), (), s32[]{:S(2)}) async-start(), calls=%async_computation.24 | async-start | bytes 1327104 | tf_op jit(solution)/shard_map/reduce_scatter | solution.py:287
  901.0 9.4 slice-start
  914.9 8.0 copy-start.15
  914.9 367.6 %reduce-scatter.18.cloned.1.call-start = ((), (), s32[]{:S(2)}) async-start(), calls=%async_computation.23 | async-start | bytes 7864320 | tf_op jit(solution)/shard_map/reduce_scatter | solution.py:273
  941.7 401.7 %reduce-scatter.14.cloned.1.call-start = ((), (), s32[]{:S(2)}) async-start(), calls=%async_computation.19 | async-start | bytes 7864320 | tf_op jit(solution)/shard_map/reduce_scatter | solution.py:169
  954.7 327.9 %copy-start.30 = (f32[1536]{0:T(1024)S(1)}, f32[1536]{0:T(1024)}, u32[]{:S(2)}) copy-start(f32[1536]{0:T(1024)} %copy-done.29) | copy-start | bytes 18436
  954.7 327.9 %copy-start.36 = (f32[512]{0:T(512)S(1)}, f32[512]{0:T(512)}, u32[]{:S(2)}) copy-start(f32[512]{0:T(512)} %copy-done.35) | copy-start | bytes 6148
  959.3 326.3 %copy-start.41 = (bf16[1536]{0:T(1024)(128)(2,1)S(1)}, bf16[1536]{0:T(1024)(128)(2,1)}, u32[]{:S(2)}) copy-start(bf16[1536]{0:T(1024)(128)(2,1)} %get-tuple-element.235) | copy-start | bytes 9220
  959.3 384.2 %copy-start.1 = (f32[512,1536]{1,0:T(8,128)S(1)}, f32[512,1536]{1,0:T(8,128)}, u32[]{:S(2)}) copy-start(f32[512,1536]{1,0:T(8,128)} %copy-done) | copy-start | bytes 9437188
  959.3 384.2 %copy-start.28 = (f32[1536]{0:T(1024)S(1)}, f32[1536]{0:T(1024)}, u32[]{:S(2)}) copy-start(f32[1536]{0:T(1024)} %copy-done.27) | copy-start | bytes 18436
  959.3 384.2 %copy-start.34 = (f32[512]{0:T(512)S(1)}, f32[512]{0:T(512)}, u32[]{:S(2)}) copy-start(f32[512]{0:T(512)} %copy-done.33) | copy-start | bytes 6148
  959.3 384.2 %copy-start.38 = (f32[512]{0:T(512)S(1)}, f32[512]{0:T(512)}, u32[]{:S(2)}) copy-start(f32[512]{0:T(512)} %copy-done.37) | copy-start | bytes 6148
  959.3 384.2 %copy-start.40 = (f32[512]{0:T(512)S(1)}, f32[512]{0:T(512)}, u32[]{:S(2)}) copy-start(f32[512]{0:T(512)} %copy-done.39) | copy-start | bytes 6148
  959.3 384.2 %copy-start.42 = (f32[512]{0:T(512)S(1)}, f32[512]{0:T(512)}, u32[]{:S(2)}) copy-start(f32[512]{0:T(512)} %get-tuple-element.300) | copy-start | bytes 6148
  (31 other events, 119.5 us)
Sparse Core Ops, SparseCore 0:
  40.5 43.6 all-gather.9
  86.3 41.7 all-gather.11
  130.3 39.8 all-gather.13
  196.0 97.7 reduce-scatter.11
  295.9 60.4 all-gather.19
  358.4 44.9 all-gather.15
  405.6 60.4 all-gather.17
  468.3 59.0 all-gather.21
  528.9 44.9 all-gather.23
  614.6 58.3 reduce-scatter.15
  679.0 46.3 all-gather.25
  729.2 74.3 reduce-scatter.31
  807.6 73.5 reduce-scatter.29
  885.1 73.5 reduce-scatter.27
  962.2 61.6 reduce-scatter.21
  1027.1 61.4 reduce-scatter.23
  1092.2 63.0 reduce-scatter.25
  1159.4 63.0 reduce-scatter.19
  1225.2 57.2 reduce-scatter.17
  1284.9 58.5 reduce-scatter.13
where the time goes:
time: 1370 us; the launch traced here: 1360 us
  waiting for transfers between devices  780 us (57%)
  matrix products  266 us (19%)
  blocking collectives  117 us (9%)
  local copies, waits for them, and re-layouts  94.7 us (7%)
  other arithmetic  66.5 us (5%)
  between operations  16.4 us (1%)
  loops' own time  14.2 us (1%)
    reduce_scatter x1, waiting for transfers between devices, local(): lax.psum_scatter(attention_terms, 'tensor', scatter_dimension=0, tiled=True)  97.3 us
    dot_general x7, matrix products, times_transpose(): lax.dot_general(left_matrix, right_matrix, (((1,), (1,)), ((), ())), pref...  73.7 us
    dynamic_update_slice x8, local copies, waits for them, and re-layouts, local(): lax.scan(attend_back, (zero_rows, zero_rows), jnp.arange(block_count, dty...  67.8 us
    reduce_scatter x1, waiting for transfers between devices, local(): lax.psum_scatter(query_weight_grad.astype(jnp.bfloat16), 'dp', scatter_di...  65.6 us
    reduce_scatter x1, waiting for transfers between devices, local(): lax.psum_scatter(output_weight_grad.astype(jnp.bfloat16), 'dp', scatter_d...  65.1 us
    reduce_scatter x1, waiting for transfers between devices, local(): lax.psum_scatter(value_weight_grad.astype(jnp.bfloat16), 'dp', scatter_di...  63.1 us
    reduce_scatter x1, waiting for transfers between devices, local(): lax.psum_scatter(key_weight_grad.astype(jnp.bfloat16), 'dp', scatter_dime...  62.4 us
    reduce_scatter x1, waiting for transfers between devices, local(): lax.psum_scatter(normed_two_terms.astype(jnp.bfloat16), 'tensor', scatter...  58.5 us
  transfers between devices with their start and end apart: 20, of which 15 were waited for; matrix products, arithmetic and copies ran while one was open for 26% of the time, Pallas kernels for 0%

commit v1 on v0

v1 whole, which is shorter than its diff:
```python
import functools

import jax
import jax.numpy as jnp
import numpy as np
from jax import lax
from jax.experimental import pallas as pl
from jax.experimental.pallas import tpu as pltpu
from jax.sharding import PartitionSpec as P

HEAD = 96
LENGTH = 1024
LANES = 128
QB = 256
norm_eps = 1e-05
rope_base = 100000.0


def rope_tables():
    half = HEAD // 2
    freq = rope_base ** (np.arange(half, dtype=np.float64) * (-2.0 / HEAD))
    turned = np.arange(LENGTH, dtype=np.float64)[:, None] * freq[None, :]
    cos = np.zeros((LENGTH, LANES), np.float32); sin = np.zeros((LENGTH, LANES), np.float32)
    cos[:, :half] = np.cos(turned); cos[:, 64:64+half] = np.cos(turned)
    sin[:, :half] = -np.sin(turned); sin[:, 64:64+half] = np.sin(turned)
    return cos, sin

def spread(heads, rotary):
    e = np.zeros((heads * HEAD, heads * LANES), np.float32)
    for h in range(heads):
        for i in range(HEAD):
            lane = i if (not rotary[h] or i < 48) else i + 16
            e[h * HEAD + i, h * LANES + lane] = 1
    return e

def dot(a, b, dims=((1,), (0,))):
    return lax.dot_general(a, b, (dims, ((), ())), preferred_element_type=jnp.float32)

C2 = float(HEAD ** -0.5 * np.log2(np.e))

def fwd_kernel(normed, weight, spread_ref, cos_ref, sin_ref, qkv_ref, att_ref, lse_ref):
    w = dot(weight[...], spread_ref[...]).astype(jnp.bfloat16)
    rows = dot(normed[...], w)
    cos = cos_ref[...]; sin = sin_ref[...]
    def rot(u):
        return (u * cos + pltpu.roll(u, 64, 1) * sin).astype(jnp.bfloat16)
    qkv_ref[:, 0:128] = rot(rows[:, 0:128])
    qkv_ref[:, 128:256] = rot(rows[:, 128:256])
    qkv_ref[:, 256:384] = rot(rows[:, 256:384])
    qkv_ref[:, 384:512] = rows[:, 384:512].astype(jnp.bfloat16)
    vt = qkv_ref[:, 384:512].T
    for r in range(2):
        for i in range(LENGTH // QB):
            kk = (i + 1) * QB
            q = qkv_ref[i * QB:kk, r * 128:r * 128 + 128]
            s = dot(qkv_ref[:kk, 256:384], q, ((1,), (1,)))
            key_place = lax.broadcasted_iota(jnp.int32, (QB, QB), 0)
            query_place = lax.broadcasted_iota(jnp.int32, (QB, QB), 1)
            last = jnp.where(key_place <= query_place, s[kk - QB:], -1e30)
            s = jnp.concatenate([s[:kk - QB], last], axis=0) if i else last
            top = jnp.max(s, axis=0, keepdims=True)
            e = jnp.exp2((s - top) * C2)
            total = jnp.sum(e, axis=0, keepdims=True)
            o = dot(vt[:, :kk], e.astype(jnp.bfloat16))
            o = o / total
            att_ref[i * QB:kk, r * 128:r * 128 + 128] = o.T.astype(jnp.bfloat16)
            lse_ref[0, r, pl.ds(i * QB, QB)] = (top * C2 + jnp.log2(total))[0]

def attend_fwd(normed, weight):
    groups = weight.shape[1] // 384
    cos, sin = rope_tables()
    e = jnp.asarray(spread(4, (1, 1, 1, 0)), jnp.bfloat16)
    whole = lambda g: (0, 0)
    return pl.pallas_call(
        fwd_kernel, grid=(groups,),
        in_specs=[pl.BlockSpec((LENGTH, weight.shape[0]), whole), pl.BlockSpec((weight.shape[0], 384), lambda g: (0, g)),
                  pl.BlockSpec((384, 512), whole), pl.BlockSpec((LENGTH, LANES), whole), pl.BlockSpec((LENGTH, LANES), whole)],
        out_specs=[pl.BlockSpec((LENGTH, 512), lambda g: (0, g)), pl.BlockSpec((LENGTH, 256), lambda g: (0, g)),
                   pl.BlockSpec((1, 2, LENGTH), lambda g: (g, 0, 0))],
        out_shape=[jax.ShapeDtypeStruct((LENGTH, 512 * groups), jnp.bfloat16), jax.ShapeDtypeStruct((LENGTH, 256 * groups), jnp.bfloat16),
                   jax.ShapeDtypeStruct((groups, 2, LENGTH), jnp.float32)],
        compiler_params=pltpu.CompilerParams(vmem_limit_bytes=40 * 2**20),
        cost_estimate=pl.CostEstimate(flops=groups * 2 * 10**9 * 3, bytes_accessed=10 * 2**20, transcendentals=groups * 2**21),
        name="attend_forward",
    )(normed, weight, e, jnp.asarray(cos), jnp.asarray(sin))

def bwd_kernel(qkv_ref, att_ref, grad_ref, lse_ref, spread_ref, cos_ref, sin_ref, out_ref, dk_ref, dv_ref, dq_ref):
    kt = qkv_ref[:, 256:384].T
    cos = cos_ref[...]; sin = sin_ref[...]
    scale = HEAD ** -0.5
    def unrot(u):
        return (u * cos - pltpu.roll(u, 64, 1) * sin).astype(jnp.bfloat16)
    for r in range(2):
        prod = grad_ref[:, r * 128:r * 128 + 128].astype(jnp.float32) * att_ref[:, r * 128:r * 128 + 128].astype(jnp.float32)
        delta = jnp.sum(prod.T, axis=0, keepdims=True)
        for i in reversed(range(LENGTH // QB)):
            kk = (i + 1) * QB
            q = qkv_ref[i * QB:kk, r * 128:r * 128 + 128]
            g = grad_ref[i * QB:kk, r * 128:r * 128 + 128]
            s = dot(qkv_ref[:kk, 256:384], q, ((1,), (1,)))
            p = jnp.exp2(s * C2 - lse_ref[0, r:r + 1, i * QB:kk])
            key_place = lax.broadcasted_iota(jnp.int32, (QB, QB), 0)
            query_place = lax.broadcasted_iota(jnp.int32, (QB, QB), 1)
            last = jnp.where(key_place <= query_place, p[kk - QB:], 0.0)
            p = jnp.concatenate([p[:kk - QB], last], axis=0) if i else last
            dp = dot(qkv_ref[:kk, 384:512], g, ((1,), (1,)))
            ds = (p * (dp - delta[:, i * QB:kk])).astype(jnp.bfloat16)
            dk = dot(ds, q)
            dv = dot(p.astype(jnp.bfloat16), g)
            if r == 0 and i == LENGTH // QB - 1:
                dk_ref[...] = dk
                dv_ref[...] = dv
            else:
                dk_ref[:kk] += dk
                dv_ref[:kk] += dv
            dq = dot(kt[:, :kk], ds)
            dq_ref[i * QB:kk, r * 128:r * 128 + 128] = dq.T
    rows = jnp.concatenate([unrot(dq_ref[:, :128] * scale), unrot(dq_ref[:, 128:] * scale), unrot(dk_ref[...] * scale), dv_ref[...].astype(jnp.bfloat16)], axis=1)
    out_ref[...] = dot(rows, spread_ref[...], ((1,), (1,))).astype(jnp.bfloat16)

def attend_bwd(qkv, att, grad, lse):
    groups = qkv.shape[1] // 512
    cos, sin = rope_tables()
    e = jnp.asarray(spread(4, (1, 1, 1, 0)), jnp.bfloat16)
    whole = lambda g: (0, 0)
    return pl.pallas_call(
        bwd_kernel, grid=(groups,),
        in_specs=[pl.BlockSpec((LENGTH, 512), lambda g: (0, g)), pl.BlockSpec((LENGTH, 256), lambda g: (0, g)), pl.BlockSpec((LENGTH, 256), lambda g: (0, g)),
                  pl.BlockSpec((1, 2, LENGTH), lambda g: (g, 0, 0)),
                  pl.BlockSpec((384, 512), whole), pl.BlockSpec((LENGTH, LANES), whole), pl.BlockSpec((LENGTH, LANES), whole)],
        out_specs=pl.BlockSpec((LENGTH, 384), lambda g: (0, g)),
        out_shape=jax.ShapeDtypeStruct((LENGTH, 384 * groups), jnp.bfloat16),
        scratch_shapes=[pltpu.VMEM((LENGTH, LANES), jnp.float32), pltpu.VMEM((LENGTH, LANES), jnp.float32), pltpu.VMEM((LENGTH, 256), jnp.float32)],
        compiler_params=pltpu.CompilerParams(vmem_limit_bytes=40 * 2**20),
        cost_estimate=pl.CostEstimate(flops=groups * 4 * 10**9 * 3, bytes_accessed=10 * 2**20, transcendentals=groups * 2**21),
        name="attend_backward",
    )(qkv, att, grad, lse, e, jnp.asarray(cos), jnp.asarray(sin))


def swap_core(v):
    return lax.ppermute(v, "tensor", [(t, t ^ 1) for t in range(4)])


def swap_chip(v):
    return lax.ppermute(v, "tensor", [(t, t ^ 2) for t in range(4)])


class Ring:
    def __init__(self, size):
        self.size = size
        self.half = size // 2
        order = list(range(0, size, 2)) + list(range(size - 1, 0, -2))
        self.forward = [(order[i], order[(i + 1) % size]) for i in range(size)]
        self.backward = [(b, a) for a, b in self.forward]
        own = lax.axis_index("dp")
        self.place = jnp.where(own % 2 == 0, own // 2, size - 1 - own // 2)

    def index(self, step):
        place = (self.place + step + self.size) % self.size
        return jnp.where(place < self.half, 2 * place, 2 * (self.size - 1 - place) + 1)

    def up(self, v):
        return lax.ppermute(v, "dp", self.forward)

    def down(self, v):
        return lax.ppermute(v, "dp", self.backward)

    def gather(self, shard, passed=False):
        rows, columns = shard.shape
        parts = [(0, shard)]
        others = []
        if passed:
            others.append((0, swap_chip(shard)))
        up = down = shard
        for step in range(1, self.half):
            up, down = self.up(up), self.down(down)
            parts += [(-step, up), (step, down)]
            if passed:
                both = swap_chip(jnp.concatenate([up, down], axis=0))
                others += [(-step, both[:rows]), (step, both[rows:])]
        cut = rows // 2
        last = jnp.concatenate([self.up(up[:cut]), self.down(down[cut:])], axis=0)
        parts.append((self.half, last))
        if passed:
            others.append((self.half, swap_chip(last)))

        def lay(pieces):
            whole = jnp.zeros((self.size * rows, columns), shard.dtype)
            for step, piece in pieces:
                whole = lax.dynamic_update_slice(whole, piece, (self.index(step) * rows, 0))
            return whole

        return (lay(parts), lay(others)) if passed else lay(parts)

    def scatter(self, take):
        far = take(self.index(self.half))
        cut = far.shape[0] // 2
        up, down = self.up(far[:cut]), self.down(far[cut:])
        for step in range(self.half - 1, 0, -1):
            ahead = take(self.index(step)).astype(jnp.float32)
            behind = take(self.index(-step)).astype(jnp.float32)
            if step == self.half - 1:
                ahead = jnp.concatenate([ahead[:cut] + up.astype(jnp.float32), ahead[cut:]], axis=0)
                behind = jnp.concatenate([behind[:cut], behind[cut:] + down.astype(jnp.float32)], axis=0)
            else:
                ahead = ahead + up.astype(jnp.float32)
                behind = behind + down.astype(jnp.float32)
            up, down = self.up(ahead.astype(jnp.bfloat16)), self.down(behind.astype(jnp.bfloat16))
        own = take(self.index(0)).astype(jnp.float32)
        return own + up.astype(jnp.float32) + down.astype(jnp.float32)


def gather_gains(gains, size):
    own = lax.axis_index("dp")
    whole = jnp.zeros((size,) + gains.shape, gains.dtype)
    whole = lax.dynamic_update_slice(whole, gains[None], (own, 0, 0))
    for step in range(1, size):
        piece = lax.ppermute(gains, "dp", [(i, (i + step) % size) for i in range(size)])
        whole = lax.dynamic_update_slice(whole, piece[None], ((own - step + size) % size, 0, 0))
    return whole


def times(left, right):
    return dot(left, right)


def times_transpose(left, right):
    return dot(left, right, ((1,), (1,)))


def contract_rows(left, right):
    return dot(left, right, ((0,), (0,)))


def local(
    dp_size,
    tokens,
    first_gain,
    query_weight,
    key_weight,
    value_weight,
    output_weight,
    second_gain,
    gate_weight,
    up_weight,
    down_weight,
    cotangent,
):
    ring = Ring(dp_size)
    half_rows = tokens.shape[0]
    core = lax.axis_index("tensor") % 2
    bf16, f32 = jnp.bfloat16, jnp.float32

    def pair(own, other):
        return jnp.where(
            core == 0,
            jnp.concatenate([own, other], axis=0),
            jnp.concatenate([other, own], axis=0),
        )

    def mine(rows):
        return lax.dynamic_slice_in_dim(rows, core * half_rows, half_rows, 0)

    def theirs(rows):
        return lax.dynamic_slice_in_dim(rows, (1 - core) * half_rows, half_rows, 0)

    groups = key_weight.shape[1] // HEAD
    packs = []
    for group in range(groups):
        packs.append(query_weight[:, group * 2 * HEAD : (group + 1) * 2 * HEAD])
        packs.append(key_weight[:, group * HEAD : (group + 1) * HEAD])
        packs.append(value_weight[:, group * HEAD : (group + 1) * HEAD])
    attend_shard = jnp.concatenate(packs, axis=1)
    output_shard = output_weight.T
    feed_shard = jnp.concatenate([gate_weight, up_weight, down_weight.T], axis=1)
    hidden_units = gate_weight.shape[1]

    gains = gather_gains(jnp.stack([first_gain, second_gain]), dp_size)
    gain_one = gains[:, 0].reshape(1, -1).astype(f32)
    gain_two = gains[:, 1].reshape(1, -1).astype(f32)

    activations = tokens.astype(f32)
    inverse_one = lax.rsqrt(jnp.mean(activations * activations, axis=-1, keepdims=True) + norm_eps)
    normed_own = (activations * inverse_one * gain_one).astype(bf16)
    normed = pair(normed_own, swap_core(normed_own))

    attend_own, attend_other = ring.gather(attend_shard, passed=True)
    output_shard, attend_own_late = lax.optimization_barrier((output_shard, attend_own))
    output_both = ring.gather(jnp.concatenate([output_shard, swap_chip(output_shard)], axis=1))
    output_both_late, feed_shard = lax.optimization_barrier((output_both, feed_shard))
    feed = ring.gather(feed_shard)
    gate_up = feed[:, : 2 * hidden_units]
    down_turned = feed[:, 2 * hidden_units :]

    qkv_own, attended_own, log_own = attend_fwd(normed, attend_own)
    qkv_other, attended_other, log_other = attend_fwd(normed, attend_other)
    heads = output_both.shape[1] // HEAD
    spread_heads = jnp.asarray(spread(heads, (0,) * heads), bf16)
    output_spread = times(output_both, spread_heads).astype(bf16)
    attended = jnp.concatenate([attended_own, attended_other], axis=1)
    attention_terms = times_transpose(attended, output_spread).astype(bf16)
    hidden_state = (
        activations
        + mine(attention_terms).astype(f32)
        + swap_core(theirs(attention_terms)).astype(f32)
    )
    inverse_two = lax.rsqrt(
        jnp.mean(hidden_state * hidden_state, axis=-1, keepdims=True) + norm_eps
    )
    normed_two_own = (hidden_state * inverse_two * gain_two).astype(bf16)

    def spread_rows(own):
        across = swap_chip(own)
        return pair(own, swap_core(own)), pair(across, swap_core(across))

    def gather_rows(near, far):
        near_sum = mine(near).astype(f32) + swap_core(theirs(near)).astype(f32)
        far_sum = mine(far).astype(f32) + swap_core(theirs(far)).astype(f32)
        return near_sum + swap_chip(far_sum.astype(bf16)).astype(f32)

    cot_near, cot_far = spread_rows(cotangent)
    two_near, two_far = spread_rows(normed_two_own)

    def feed_forward(two, cot):
        both = times(two, gate_up)
        gate, up = both[:, :hidden_units], both[:, hidden_units:]
        inner_grad = times(cot, down_turned)
        sigmoid = jax.nn.sigmoid(gate)
        inner = (gate * sigmoid * up).astype(bf16)
        up_grad = (inner_grad * gate * sigmoid).astype(bf16)
        gate_grad = (inner_grad * up * sigmoid * (1.0 + gate * (1.0 - sigmoid))).astype(bf16)
        return inner, jnp.concatenate([gate_grad, up_grad], axis=1)

    inner_near, grad_near = feed_forward(two_near, cot_near)
    inner_far, grad_far = feed_forward(two_far, cot_far)
    two_terms_far = times_transpose(grad_far, gate_up).astype(bf16)
    two_terms_near = times_transpose(grad_near, gate_up).astype(bf16)
    out_far = times_transpose(inner_far, down_turned).astype(bf16)
    out_near = times_transpose(inner_near, down_turned).astype(bf16)
    normed_two_grad = gather_rows(two_terms_near, two_terms_far)
    layer_out = (hidden_state + gather_rows(out_near, out_far)).astype(bf16)

    down_grad = contract_rows(
        jnp.concatenate([cot_near, cot_far], axis=0),
        jnp.concatenate([inner_near, inner_far], axis=0),
    ).astype(bf16)
    gate_up_grad = contract_rows(
        jnp.concatenate([two_near, two_far], axis=0),
        jnp.concatenate([grad_near, grad_far], axis=0),
    ).astype(bf16)
    shard_rows = first_gain.shape[0]

    def part(whole):
        return lambda index: lax.dynamic_slice_in_dim(whole, index * shard_rows, shard_rows, 0)

    down_sum = ring.scatter(part(down_grad))
    gate_up_sum = ring.scatter(part(gate_up_grad))

    scaled_two = normed_two_grad * gain_two
    hidden_grad = (
        cotangent.astype(f32)
        + inverse_two * scaled_two
        - hidden_state
        * inverse_two**3
        * jnp.mean(scaled_two * hidden_state, axis=-1, keepdims=True)
    )
    branch_own = hidden_grad.astype(bf16)
    branch = pair(branch_own, swap_core(branch_own))
    attended_grad = times(branch, output_spread).astype(bf16)
    width = attended_own.shape[1]
    other_back = attend_bwd(qkv_other, attended_other, attended_grad[:, width:], log_other)
    own_back = attend_bwd(qkv_own, attended_own, attended_grad[:, :width], log_own)

    attended_close = times_transpose(attended, spread_heads).astype(bf16)
    output_grad = contract_rows(branch, attended_close).astype(bf16)
    columns = output_shard.shape[1]
    output_grad = output_grad[:, :columns].astype(f32) + swap_chip(output_grad[:, columns:]).astype(
        f32
    )
    output_sum = ring.scatter(part(output_grad.astype(bf16)))

    other_grad = swap_chip(contract_rows(normed, other_back).astype(bf16))
    own_grad = contract_rows(normed, own_back)
    attend_grad = (own_grad + other_grad.astype(f32)).astype(bf16)
    attend_sum = ring.scatter(part(attend_grad))

    normed_terms = (
        times_transpose(own_back, attend_own) + times_transpose(other_back, attend_other)
    ).astype(bf16)
    normed_grad = mine(normed_terms).astype(f32) + swap_core(theirs(normed_terms)).astype(f32)
    scaled_one = normed_grad * gain_one
    tokens_grad = (
        hidden_grad
        + inverse_one * scaled_one
        - activations * inverse_one**3 * jnp.mean(scaled_one * activations, axis=-1, keepdims=True)
    ).astype(bf16)

    gain_sums = jnp.stack(
        [
            jnp.sum(attend_sum * attend_shard.astype(f32), axis=1) / first_gain.astype(f32),
            jnp.sum(gate_up_sum * feed_shard[:, : 2 * hidden_units].astype(f32), axis=1)
            / second_gain.astype(f32),
        ]
    )
    gain_sums = gain_sums + swap_core(gain_sums)
    gain_sums = gain_sums + swap_chip(gain_sums)

    block = 4 * HEAD
    query_grad = jnp.concatenate(
        [attend_sum[:, g * block : g * block + 2 * HEAD] for g in range(groups)], axis=1
    )
    key_grad = jnp.concatenate(
        [attend_sum[:, g * block + 2 * HEAD : g * block + 3 * HEAD] for g in range(groups)], axis=1
    )
    value_grad = jnp.concatenate(
        [attend_sum[:, g * block + 3 * HEAD : (g + 1) * block] for g in range(groups)], axis=1
    )
    return (
        layer_out,
        tokens_grad,
        gain_sums[0],
        query_grad,
        key_grad,
        value_grad,
        output_sum.T,
        gain_sums[1],
        gate_up_sum[:, :hidden_units],
        gate_up_sum[:, hidden_units:],
        down_sum.T,
    )


def solution(mesh):
    in_specs = (
        P(("dp", "tensor"), None),
        P("dp"),
        P("dp", "tensor"),
        P("dp", "tensor"),
        P("dp", "tensor"),
        P("tensor", "dp"),
        P("dp"),
        P("dp", "tensor"),
        P("dp", "tensor"),
        P("tensor", "dp"),
        P(("dp", "tensor"), None),
    )
    out_specs = (
        P(("dp", "tensor"), None),
        P(("dp", "tensor"), None),
        P("dp"),
        P("dp", "tensor"),
        P("dp", "tensor"),
        P("dp", "tensor"),
        P("tensor", "dp"),
        P("dp"),
        P("dp", "tensor"),
        P("dp", "tensor"),
        P("tensor", "dp"),
    )
    body = functools.partial(local, mesh.shape["dp"])
    return jax.shard_map(body, mesh=mesh, in_specs=in_specs, out_specs=out_specs, check_vma=False)
```

time: 1370 us -> 670 us (0.49)
  waiting for transfers between devices: 780 us -> 310 us
  matrix products: 266 us -> 134 us
  blocking collectives: 117 us -> 0 us
  starting transfers between devices: 1.39 us -> 98.3 us
  local copies, waits for them, and re-layouts: 94.7 us -> 33.1 us
  Pallas kernels: 0 us -> 43.9 us
  other arithmetic: 66.5 us -> 39.6 us
  loops' own time: 14.2 us -> 0 us
  between operations: 16.4 us -> 2.62 us
    reduce_scatter x11 -> x0, waiting for transfers between devices: 500 us -> none  [the longest x1 97.3 us: local(): lax.psum_scatter(attention_terms, 'tensor', scatter_dimension=0, tiled=True)]
    ppermute x0 -> x89, waiting for transfers between devices: none -> 310 us  [the longest x13 133 us: swap_chip(): return lax.ppermute(v, 'tensor', [(t, t ^ 2) for t in range(4)])]
    all_gather x9 -> x0, waiting for transfers between devices: 276 us -> none  [the longest x1 55.6 us: local(): lax.all_gather(up_weight, 'dp', axis=0, tiled=True)]
    dot_general x49 -> x19, matrix products: 266 us -> 134 us  [dot(): lax.dot_general(a, b, (dims, ((), ())), preferred_element_type=jnp.float32)]
    ppermute x0 -> x89, starting transfers between devices: none -> 98.3 us  [the longest x28 36.4 us: down(): return lax.ppermute(v, 'dp', self.backward)]
    all_gather x2 -> x0, blocking collectives: 64.9 us -> none  [the longest x1 32.6 us: local(): lax.all_gather(value_weight, 'dp', axis=0, tiled=True)]
    dynamic_update_slice x8 -> x37, local copies, waits for them, and re-layouts: 67.8 us -> 5.51 us  [the longest x30 5.44 us: lay(): whole = lax.dynamic_update_slice(whole, piece, (self.index(step) * rows, 0))]
    unnamed x2 -> x0, blocking collectives: 45 us -> none
  transfers between devices with their start and end apart: 20 -> 89, of which waited for: 15 -> 42; matrix products, arithmetic and copies ran while one was open for 26% -> 27% of each run, Pallas kernels for 0% -> 7%
where the time goes in v1:
time: 670 us; the launch traced here: 662 us
  waiting for transfers between devices  310 us (46%)
  matrix products  134 us (20%)
  starting transfers between devices  98.3 us (15%)
  Pallas kernels  43.9 us (7%)
  other arithmetic  39.6 us (6%)
  local copies, waits for them, and re-layouts  33.1 us (5%)
    dot_general x19, matrix products, dot(): lax.dot_general(a, b, (dims, ((), ())), preferred_element_type=jnp.float32)  134 us
    ppermute x13, waiting for transfers between devices, swap_chip(): return lax.ppermute(v, 'tensor', [(t, t ^ 2) for t in range(4)])  133 us
    ppermute x28, waiting for transfers between devices, up(): return lax.ppermute(v, 'dp', self.forward)  124 us
    ppermute x28, waiting for transfers between devices, down(): return lax.ppermute(v, 'dp', self.backward)  41.3 us
    ppermute x28, starting transfers between devices, down(): return lax.ppermute(v, 'dp', self.backward)  36.4 us
    ppermute x28, starting transfers between devices, up(): return lax.ppermute(v, 'dp', self.forward)  34.7 us
    pallas_call x2, Pallas kernels, attend_fwd(): pl.pallas_call(fwd_kernel, grid=(groups,), in_specs=[pl.BlockSpec((LENGTH...  25.8 us
    ppermute x13, starting transfers between devices, swap_chip(): return lax.ppermute(v, 'tensor', [(t, t ^ 2) for t in range(4)])  18.5 us
  transfers between devices with their start and end apart: 89, of which 42 were waited for; matrix products, arithmetic and copies ran while one was open for 27% of the time, Pallas kernels for 7%

profile of v1, /device:TPU:0, one launch (start us, length us, event | category | flops | bytes accessed | tf_op | source)
XLA Modules:
  0.0 661.8 jit_solution(5004436662280629998)
XLA Ops:
  3.1 3.0 collective-permute-start.16
  14.4 3.2 collective-permute-done
  19.8 3.4 collective-permute-done.2
  37.9 6.8 %collective-permute-done.10 = bf16[192,768]{1,0:T(8,128)(2,1)S(1)} collective-permute-done((bf16[192,768]{1,0:T(8,128)(2,1)S(1)}, bf16[192,768]{1,0:T(8,128)(2,1)S(1)}, u32[]{:S(2)}, u32[]{:S(2)}) %collective-permute-start.10) | collective-permute-done | bytes 294944 | tf_op jit(solution)/shard_map/ppermute | solution.py:163
  46.9 6.1 collective-permute-done.12
  62.6 19.9 %collective-permute-done.21 = bf16[192,384]{1,0:T(8,128)(2,1)S(1)} collective-permute-done((bf16[192,384]{1,0:T(8,128)(2,1)S(1)}, bf16[192,384]{1,0:T(8,128)(2,1)S(1)}, u32[]{:S(2)}, u32[]{:S(2)}) %collective-permute-start.21) | collective-permute-done | bytes 147488 | tf_op jit(solution)/shard_map/ppermute | solution.py:145
  84.9 4.4 collective-permute-done.22
  93.9 34.7 %collective-permute-done.20 = bf16[192,768]{1,0:T(8,128)(2,1)S(1)} collective-permute-done((bf16[192,768]{1,0:T(8,128)(2,1)S(1)}, bf16[192,768]{1,0:T(8,128)(2,1)S(1)}, u32[]{:S(2)}, u32[]{:S(2)}) %collective-permute-start.20) | collective-permute-done | bytes 294944 | tf_op jit(solution)/shard_map/ppermute | solution.py:145
  132.4 12.9 %attend_forward.2 = (bf16[1024,1024]{1,0:T(8,128)(2,1)S(1)}, bf16[1024,512]{1,0:T(8,128)(2,1)S(1)}, f32[2,2,1024]{2,1,0:T(2,128)S(1)}) custom-call(bf16[1024,1536]{1,0:T(8,128)(2,1)S(1)} %maximum_select_fusion.normed, bf16[1536,768]{1,0:T(8,128)(2,1)S(1)} %constant_dynamic-update-slice_fusion.16.weight, bf16[384,512]{1,0:T(8,128)(2,1)S(1)} %copy-done.10, ...), custom_call_target="tpu_custom_call" | custom-call | flops 12000000000 | bytes 10485760 | tf_op jit(solution)/shard_map/attend_forward/pallas_call | solution.py:74
  148.9 12.9 %attend_forward.3 = (bf16[1024,1024]{1,0:T(8,128)(2,1)S(1)}, bf16[1024,512]{1,0:T(8,128)(2,1)S(1)}, f32[2,2,1024]{2,1,0:T(2,128)S(1)}) custom-call(bf16[1024,1536]{1,0:T(8,128)(2,1)S(1)} %maximum_select_fusion.normed, bf16[1536,768]{1,0:T(8,128)(2,1)S(1)} %constant_dynamic-update-slice_fusion.14.weight, bf16[384,512]{1,0:T(8,128)(2,1)S(1)} %copy-done.10, ...), custom_call_target="tpu_custom_call" | custom-call | flops 12000000000 | bytes 10485760 | tf_op jit(solution)/shard_map/attend_forward/pallas_call | solution.py:74
  164.2 3.0 collective-permute-done.28
  170.5 3.7 convolution_convert_fusion.3
  180.9 4.5 maximum_select_fusion.3
  188.2 18.8 %collective-permute-done.32 = bf16[192,3072]{1,0:T(8,128)(2,1)} collective-permute-done((bf16[192,3072]{1,0:T(8,128)(2,1)}, bf16[192,3072]{1,0:T(8,128)(2,1)}, u32[]{:S(2)}, u32[]{:S(2)}) %collective-permute-start.32) | collective-permute-done | bytes 1179680 | tf_op jit(solution)/shard_map/ppermute | solution.py:163
  218.0 16.1 %collective-permute-done.34 = bf16[192,3072]{1,0:T(8,128)(2,1)S(1)} collective-permute-done((bf16[192,3072]{1,0:T(8,128)(2,1)}, bf16[192,3072]{1,0:T(8,128)(2,1)S(1)}, u32[]{:S(2)}, u32[]{:S(2)}) %collective-permute-start.34) | collective-permute-done | bytes 1179680 | tf_op jit(solution)/shard_map/ppermute | solution.py:163
  238.3 11.3 %collective-permute-done.41 = bf16[512,1536]{1,0:T(8,128)(2,1)S(1)} collective-permute-done((bf16[512,1536]{1,0:T(8,128)(2,1)S(1)}, bf16[512,1536]{1,0:T(8,128)(2,1)S(1)}, u32[]{:S(2)}, u32[]{:S(2)}) %collective-permute-start.41) | collective-permute-done | bytes 1572896 | tf_op jit(solution)/shard_map/ppermute | solution.py:145
  250.5 9.7 %collective-permute-done.36 = bf16[192,3072]{1,0:T(8,128)(2,1)S(1)} collective-permute-done((bf16[192,3072]{1,0:T(8,128)(2,1)S(1)}, bf16[192,3072]{1,0:T(8,128)(2,1)S(1)}, u32[]{:S(2)}, u32[]{:S(2)}) %collective-permute-start.36) | collective-permute-done | bytes 1179680 | tf_op jit(solution)/shard_map/ppermute | solution.py:163
  263.0 9.9 %collective-permute-done.38 = bf16[96,3072]{1,0:T(8,128)(2,1)S(1)} collective-permute-done((bf16[96,3072]{1,0:T(8,128)(2,1)S(1)}, bf16[96,3072]{1,0:T(8,128)(2,1)S(1)}, u32[]{:S(2)}, u32[]{:S(2)}) %collective-permute-start.38) | collective-permute-done | bytes 589856 | tf_op jit(solution)/shard_map/ppermute | solution.py:163
  274.4 8.9 %fusion.33 = f32[1024,2048]{1,0:T(8,128)} fusion(bf16[1024,1536]{1,0:T(8,128)(2,1)S(1)} %maximum_select_fusion.1, bf16[1536,3072]{1,0:T(8,128)(2,1)S(1)} %maximum_dynamic-update-slice_fusion), kind=kOutput, calls=%fused_computation.46 | convolution fusion | flops 6442450944 | bytes 17825792 | tf_op jit(solution)/shard_map/dot_general | solution.py:37
  283.3 9.1 %multiply_convert_fusion.3 = (bf16[1024,1024]{1,0:T(8,128)(2,1)}, bf16[1024,1024]{1,0:T(8,128)(2,1)}, bf16[1024,1024]{1,0:T(8,128)(2,1)}) fusion(f32[1024,2048]{1,0:T(8,128)} %fusion.33, bf16[1024,1536]{1,0:T(8,128)(2,1)S(1)} %copy-done.30, bf16[1536,3072]{1,0:T(8,128)(2,1)S(1)} %maximum_dynamic-update-slice_fusion), kind=kOutput, calls=%fused_computation.37 | convolution fusion | flops 3238002688 | bytes 20971520 | tf_op jit(solution)/shard_map/dot_general | solution.py:37
  292.5 8.5 %fusion.40 = bf16[1024,1536]{1,0:T(8,128)(2,1)S(1)} fusion(bf16[1536,3072]{1,0:T(8,128)(2,1)S(1)} %maximum_dynamic-update-slice_fusion, bf16[1024,1024]{1,0:T(8,128)(2,1)} %get-tuple-element.40, bf16[1024,1024]{1,0:T(8,128)(2,1)} %get-tuple-element.39), kind=kOutput, calls=%fused_computation.49 | convolution fusion | flops 6452412416 | bytes 13631488 | tf_op jit(solution)/shard_map/dot_general | solution.py:37
  304.2 3.7 convolution_convert_fusion.2
  310.3 8.9 %fusion.31 = f32[1024,2048]{1,0:T(8,128)} fusion(bf16[1024,1536]{1,0:T(8,128)(2,1)S(1)} %maximum_select_fusion.2, bf16[1536,3072]{1,0:T(8,128)(2,1)S(1)} %maximum_dynamic-update-slice_fusion), kind=kOutput, calls=%fused_computation.44 | convolution fusion | flops 6442450944 | bytes 17825792 | tf_op jit(solution)/shard_map/dot_general | solution.py:37
  319.2 9.1 %multiply_convert_fusion.1 = (bf16[1024,1024]{1,0:T(8,128)(2,1)}, bf16[1024,1024]{1,0:T(8,128)(2,1)}, bf16[1024,1024]{1,0:T(8,128)(2,1)S(1)}) fusion(f32[1024,2048]{1,0:T(8,128)} %fusion.31, bf16[1024,1536]{1,0:T(8,128)(2,1)S(1)} %maximum_select_fusion.4, bf16[1536,3072]{1,0:T(8,128)(2,1)S(1)} %maximum_dynamic-update-slice_fusion), kind=kOutput, calls=%fused_computation.35 | convolution fusion | flops 3238002688 | bytes 20971520 | tf_op jit(solution)/shard_map/dot_general | solution.py:37
  328.3 8.2 %fusion.45 = bf16[1536,1024]{1,0:T(8,128)(2,1)} fusion(bf16[1024,1024]{1,0:T(8,128)(2,1)S(1)} %get-tuple-element.44, bf16[1024,1024]{1,0:T(8,128)(2,1)S(1)} %copy-done.60, bf16[1024,1536]{1,0:T(8,128)(2,1)S(1)} %maximum_select_fusion.4, bf16[1024,1536]{1,0:T(8,128)(2,1)S(1)} %copy-done.30), kind=kOutput, calls=%fused_computation.50 | convolution fusion | flops 6464995328 | bytes 13631488 | tf_op jit(solution)/shard_map/dot_general | solution.py:37
  336.5 4.9 convolution_convert_fusion.1
  341.4 8.1 %fusion.35 = bf16[1024,1536]{1,0:T(8,128)(2,1)} fusion(bf16[1536,3072]{1,0:T(8,128)(2,1)S(1)} %maximum_dynamic-update-slice_fusion, bf16[1024,1024]{1,0:T(8,128)(2,1)S(1)} %copy-done.62, bf16[1024,1024]{1,0:T(8,128)(2,1)S(1)} %copy-done.61), kind=kOutput, calls=%fused_computation.48 | convolution fusion | flops 6452412416 | bytes 13631488 | tf_op jit(solution)/shard_map/dot_general | solution.py:37
  349.5 20.6 %fusion.8 = bf16[1536,2048]{1,0:T(8,128)(2,1)} fusion(bf16[1024,1024]{1,0:T(8,128)(2,1)} %get-tuple-element.42, bf16[1024,1024]{1,0:T(8,128)(2,1)} %get-tuple-element.41, bf16[1024,1024]{1,0:T(8,128)(2,1)} %get-tuple-element.40, bf16[1024,1024]{1,0:T(8,128)(2,1)} %get-tuple-element.39, bf16[1024,1536]{1,0:T(8,128)(2,1)} %copy-done.33, ...), kind=kOutput, calls=%fused_computation.8 | convolution fusion | flops 12934184960 | bytes 20971520 | tf_op jit(solution)/shard_map/dot_general | solution.py:37
  378.8 4.7 collective-permute-done.62
  389.0 16.7 %collective-permute-done.63 = bf16[192,2048]{1,0:T(8,128)(2,1)S(1)} collective-permute-done((bf16[192,2048]{1,0:T(8,128)(2,1)S(1)}, bf16[192,2048]{1,0:T(8,128)(2,1)S(1)}, u32[]{:S(2)}, u32[]{:S(2)}) %collective-permute-start.63) | collective-permute-done | bytes 786464 | tf_op jit(solution)/shard_map/ppermute | solution.py:163
  406.4 5.9 collective-permute-done.82
  414.9 10.8 %collective-permute-done.67 = bf16[192,2048]{1,0:T(8,128)(2,1)S(1)} collective-permute-done((bf16[192,2048]{1,0:T(8,128)(2,1)S(1)}, bf16[192,2048]{1,0:T(8,128)(2,1)S(1)}, u32[]{:S(2)}, u32[]{:S(2)}) %collective-permute-start.67) | collective-permute-done | bytes 786464 | tf_op jit(solution)/shard_map/ppermute | solution.py:166
  427.7 5.1 collective-permute-done.64
  440.2 10.8 %collective-permute-done.68 = bf16[192,2048]{1,0:T(8,128)(2,1)S(1)} collective-permute-done((bf16[192,2048]{1,0:T(8,128)(2,1)S(1)}, bf16[192,2048]{1,0:T(8,128)(2,1)S(1)}, u32[]{:S(2)}, u32[]{:S(2)}) %collective-permute-start.68) | collective-permute-done | bytes 786464 | tf_op jit(solution)/shard_map/ppermute | solution.py:166
  453.8 16.3 %collective-permute-done.50 = bf16[512,1536]{1,0:T(8,128)(2,1)S(1)} collective-permute-done((bf16[512,1536]{1,0:T(8,128)(2,1)S(1)}, bf16[512,1536]{1,0:T(8,128)(2,1)S(1)}, u32[]{:S(2)}, u32[]{:S(2)}) %collective-permute-start.50) | collective-permute-done | bytes 1572896 | tf_op jit(solution)/shard_map/ppermute | solution.py:145
  474.5 22.7 %collective-permute-done.44 = bf16[512,1536]{1,0:T(8,128)(2,1)S(1)} collective-permute-done((bf16[512,1536]{1,0:T(8,128)(2,1)S(1)}, bf16[512,1536]{1,0:T(8,128)(2,1)S(1)}, u32[]{:S(2)}, u32[]{:S(2)}) %collective-permute-start.44) | collective-permute-done | bytes 1572896 | tf_op jit(solution)/shard_map/ppermute | solution.py:145
  497.3 5.2 fusion.77
  502.6 3.5 collective-permute-start.88
  508.8 6.4 collective-permute-done.88
  519.1 12.1 %convolution_convert_fusion.4 = bf16[1536,768]{1,0:T(8,128)(2,1)} fusion(f32[1024,768]{1,0:T(8,128)} %fusion.88, bf16[1024,512]{1,0:T(8,128)(2,1)} %copy-done.12, bf16[768,512]{1,0:T(8,128)(2,1)} %constant.292, bf16[512,1536]{1,0:T(8,128)(2,1)} %collective-permute-done.51, bf16[512,1536]{1,0:T(8,128)(2,1)} %copy-done.39, pred[]{:T(512)S(6)} %eq.85), kind=kOutput, calls=%fused_computation.55 | convolution fusion | flops 3238133760 | bytes 10485761 | tf_op jit(solution)/shard_map/dot_general | solution.py:37
  534.2 7.2 %convolution_convert_fusion.6 = bf16[1024,1024]{1,0:T(8,128)(2,1)S(1)} fusion(bf16[1536,1024]{1,0:T(8,128)(2,1)} %copy-done.58, bf16[512,1536]{1,0:T(8,128)(2,1)} %collective-permute-done.51, bf16[512,1536]{1,0:T(8,128)(2,1)} %copy-done.39, pred[]{:T(512)S(6)} %eq.85), kind=kOutput, calls=%fused_computation.91 | convolution fusion | flops 3236429824 | bytes 8388609 | tf_op jit(solution)/shard_map/dot_general | solution.py:37
  543.4 9.0 %attend_backward.3 = bf16[1024,768]{1,0:T(8,128)(2,1)S(1)} custom-call(bf16[1024,1024]{1,0:T(8,128)(2,1)S(1)} %copy-done.17, bf16[1024,512]{1,0:T(8,128)(2,1)S(1)} %copy-done.5, bf16[1024,512]{1,0:T(8,128)(2,1)S(1)} %get-tuple-element.71.grad_ref, f32[2,2,1024]{2,1,0:T(2,128)S(1)} %get-tuple-element.26.lse_ref, bf16[384,512]{1,0:T(8,128)(2,1)S(1)} %copy-done.11, ...), custom_call_target="tpu_custom_call" | custom-call | flops 24000000000 | bytes 10485760 | tf_op jit(solution)/shard_map/attend_backward/pallas_call | solution.py:126
  556.0 9.2 %attend_backward.2 = bf16[1024,768]{1,0:T(8,128)(2,1)S(1)} custom-call(bf16[1024,1024]{1,0:T(8,128)(2,1)S(1)} %copy-done.15, bf16[1024,512]{1,0:T(8,128)(2,1)S(1)} %copy-done.13, bf16[1024,512]{1,0:T(8,128)(2,1)S(1)} %get-tuple-element.70.grad_ref, f32[2,2,1024]{2,1,0:T(2,128)S(1)} %get-tuple-element.24.lse_ref, bf16[384,512]{1,0:T(8,128)(2,1)S(1)} %copy-done.11, ...), custom_call_target="tpu_custom_call" | custom-call | flops 24000000000 | bytes 10485760 | tf_op jit(solution)/shard_map/attend_backward/pallas_call | solution.py:126
  565.2 4.7 fusion.87
  569.9 4.9 add_convert_fusion
  583.8 27.0 %collective-permute-done.53 = bf16[1536,768]{1,0:T(8,128)(2,1)S(1)} collective-permute-done((bf16[1536,768]{1,0:T(8,128)(2,1)S(1)}, bf16[1536,768]{1,0:T(8,128)(2,1)S(1)}, u32[]{:S(2)}, u32[]{:S(2)}) %collective-permute-start.53) | collective-permute-done | bytes 2359328 | tf_op jit(solution)/shard_map/ppermute | solution.py:145
  634.3 4.0 collective-permute-done.56
  642.4 5.7 collective-permute-done.60
  (418 shorter events, 193.0 us)
Async XLA Ops:
  3.1 32.6 %collective-permute-start.16 = (bf16[192,768]{1,0:T(8,128)(2,1)S(1)}, bf16[192,768]{1,0:T(8,128)(2,1)S(1)}, u32[]{:S(2)}, u32[]{:S(2)}) collective-permute-start(bf16[192,768]{1,0:T(8,128)(2,1)S(1)} %concatenate.127), channel_id=1, source_target_pairs={{0,2},{1,3},{2,0},{3,1},{4,6},{5,7},{6,4},{7,5},{8,10},{9,11},{10,... | collective-permute-start | bytes 884744 | tf_op jit(solution)/shard_map/ppermute | solution.py:145
  6.1 28.9 %collective-permute-start.8 = (bf16[192,768]{1,0:T(8,128)(2,1)S(1)}, bf16[192,768]{1,0:T(8,128)(2,1)S(1)}, u32[]{:S(2)}, u32[]{:S(2)}) collective-permute-start(bf16[192,768]{1,0:T(8,128)(2,1)S(1)} %concatenate.127), channel_id=1, source_target_pairs={{0,8},{8,16},{16,24},{24,28},{28,20},{20,12},{12,4},{4,0},{1,9},{9... | collective-permute-start | bytes 884744 | tf_op jit(solution)/shard_map/ppermute | solution.py:163
  7.7 27.3 %collective-permute-start.9 = (bf16[192,768]{1,0:T(8,128)(2,1)S(1)}, bf16[192,768]{1,0:T(8,128)(2,1)S(1)}, u32[]{:S(2)}, u32[]{:S(2)}) collective-permute-start(bf16[192,768]{1,0:T(8,128)(2,1)S(1)} %concatenate.127), channel_id=1, source_target_pairs={{8,0},{16,8},{24,16},{28,24},{20,28},{12,20},{4,12},{0,4},{9,1},{1... | collective-permute-start | bytes 884744 | tf_op jit(solution)/shard_map/ppermute | solution.py:166
  29.4 151.5 %collective-permute-start.45 = (bf16[512,1536]{1,0:T(8,128)(2,1)}, bf16[512,1536]{1,0:T(8,128)(2,1)}, u32[]{:S(2)}, u32[]{:S(2)}) collective-permute-start(bf16[512,1536]{1,0:T(8,128)(2,1)} %param.34), channel_id=1, source_target_pairs={{0,1},{1,0},{2,3},{3,2},{4,5},{5,4},{6,7},{7,6},{8,9},{9,8},{10,11... | collective-permute-start | bytes 4718600 | tf_op jit(solution)/shard_map/ppermute | solution.py:141
  34.9 95.4 %collective-permute-start.7 = (bf16[512,1536]{1,0:T(8,128)(2,1)S(1)}, bf16[512,1536]{1,0:T(8,128)(2,1)S(1)}, u32[]{:S(2)}, u32[]{:S(2)}) collective-permute-start(bf16[512,1536]{1,0:T(8,128)(2,1)S(1)} %fusion.52), channel_id=1, source_target_pairs={{0,1},{1,0},{2,3},{3,2},{4,5},{5,4},{6,7},{7,6},{8,9},{9,8},{10,11... | collective-permute-start | bytes 4718600 | tf_op jit(solution)/shard_map/ppermute | solution.py:141
  35.0 20.7 %collective-permute-start.17 = (bf16[384,768]{1,0:T(8,128)(2,1)S(1)}, bf16[384,768]{1,0:T(8,128)(2,1)S(1)}, u32[]{:S(2)}, u32[]{:S(2)}) collective-permute-start(bf16[384,768]{1,0:T(8,128)(2,1)S(1)} %pad_maximum_fusion.3), channel_id=1, source_target_pairs={{0,2},{1,3},{2,0},{3,1},{4,6},{5,7},{6,4},{7,5},{8,10},{9,11},{10,... | collective-permute-start | bytes 1769480 | tf_op jit(solution)/shard_map/ppermute | solution.py:145
  53.0 30.7 %collective-permute-start.18 = (bf16[384,768]{1,0:T(8,128)(2,1)S(1)}, bf16[384,768]{1,0:T(8,128)(2,1)S(1)}, u32[]{:S(2)}, u32[]{:S(2)}) collective-permute-start(bf16[384,768]{1,0:T(8,128)(2,1)S(1)} %pad_maximum_fusion.4), channel_id=1, source_target_pairs={{0,2},{1,3},{2,0},{3,1},{4,6},{5,7},{6,4},{7,5},{8,10},{9,11},{10,... | collective-permute-start | bytes 1769480 | tf_op jit(solution)/shard_map/ppermute | solution.py:145
  59.7 32.3 %collective-permute-start.19 = (bf16[384,768]{1,0:T(8,128)(2,1)S(1)}, bf16[384,768]{1,0:T(8,128)(2,1)S(1)}, u32[]{:S(2)}, u32[]{:S(2)}) collective-permute-start(bf16[384,768]{1,0:T(8,128)(2,1)S(1)} %pad_maximum_fusion.5), channel_id=1, source_target_pairs={{0,2},{1,3},{2,0},{3,1},{4,6},{5,7},{6,4},{7,5},{8,10},{9,11},{10,... | collective-permute-start | bytes 1769480 | tf_op jit(solution)/shard_map/ppermute | solution.py:145
  61.0 21.5 %collective-permute-start.21 = (bf16[192,384]{1,0:T(8,128)(2,1)S(1)}, bf16[192,384]{1,0:T(8,128)(2,1)S(1)}, u32[]{:S(2)}, u32[]{:S(2)}) collective-permute-start(bf16[192,384]{1,0:T(8,128)(2,1)S(1)} %bitcast.49), channel_id=1, source_target_pairs={{0,2},{1,3},{2,0},{3,1},{4,6},{5,7},{6,4},{7,5},{8,10},{9,11},{10,... | collective-permute-start | bytes 442376 | tf_op jit(solution)/shard_map/ppermute | solution.py:145
  89.3 91.6 %collective-permute-start.47 = (bf16[512,1536]{1,0:T(8,128)(2,1)}, bf16[512,1536]{1,0:T(8,128)(2,1)}, u32[]{:S(2)}, u32[]{:S(2)}) collective-permute-start(bf16[512,1536]{1,0:T(8,128)(2,1)} %param.34), channel_id=1, source_target_pairs={{0,2},{1,3},{2,0},{3,1},{4,6},{5,7},{6,4},{7,5},{8,10},{9,11},{10,... | collective-permute-start | bytes 4718600 | tf_op jit(solution)/shard_map/ppermute | solution.py:145
  90.9 37.7 %collective-permute-start.20 = (bf16[192,768]{1,0:T(8,128)(2,1)S(1)}, bf16[192,768]{1,0:T(8,128)(2,1)S(1)}, u32[]{:S(2)}, u32[]{:S(2)}) collective-permute-start(bf16[192,768]{1,0:T(8,128)(2,1)S(1)} %constant_dynamic-update-slice_fusion.32), channel_id=1, source_target_pairs={{0,2},{1,3},{2,0},{3,1},{4,6},{5,7},{6,4},{7,5},{8,10},{9,11},{10,... | collective-permute-start | bytes 884744 | tf_op jit(solution)/shard_map/ppermute | solution.py:145
  92.1 54.6 %collective-permute-start.24 = (bf16[192,768]{1,0:T(8,128)(2,1)S(1)}, bf16[192,768]{1,0:T(8,128)(2,1)S(1)}, u32[]{:S(2)}, u32[]{:S(2)}) collective-permute-start(bf16[192,768]{1,0:T(8,128)(2,1)S(1)} %collective-permute-done.22), channel_id=1, source_target_pairs={{0,8},{8,16},{16,24},{24,28},{28,20},{20,12},{12,4},{4,0},{1,9},{9... | collective-permute-start | bytes 884744 | tf_op jit(solution)/shard_map/ppermute | solution.py:163
  128.5 18.5 %collective-permute-start.25 = (bf16[192,768]{1,0:T(8,128)(2,1)S(1)}, bf16[192,768]{1,0:T(8,128)(2,1)S(1)}, u32[]{:S(2)}, u32[]{:S(2)}) collective-permute-start(bf16[192,768]{1,0:T(8,128)(2,1)S(1)} %collective-permute-done.23), channel_id=1, source_target_pairs={{8,0},{16,8},{24,16},{28,24},{20,28},{12,20},{4,12},{0,4},{9,1},{1... | collective-permute-start | bytes 884744 | tf_op jit(solution)/shard_map/ppermute | solution.py:166
  177.1 31.9 %collective-permute-start.30 = (bf16[512,1536]{1,0:T(8,128)(2,1)}, bf16[512,1536]{1,0:T(8,128)(2,1)}, u32[]{:S(2)}, u32[]{:S(2)}) collective-permute-start(bf16[512,1536]{1,0:T(8,128)(2,1)} %constant_dynamic-slice_fusion.21), channel_id=1, source_target_pairs={{0,1},{1,0},{2,3},{3,2},{4,5},{5,4},{6,7},{7,6},{8,9},{9,8},{10,11... | collective-permute-start | bytes 4718600 | tf_op jit(solution)/shard_map/ppermute | solution.py:141
  178.8 28.2 %collective-permute-start.32 = (bf16[192,3072]{1,0:T(8,128)(2,1)}, bf16[192,3072]{1,0:T(8,128)(2,1)}, u32[]{:S(2)}, u32[]{:S(2)}) collective-permute-start(bf16[192,3072]{1,0:T(8,128)(2,1)} %pad_maximum_fusion), channel_id=1, source_target_pairs={{0,8},{8,16},{16,24},{24,28},{28,20},{20,12},{12,4},{4,0},{1,9},{9... | collective-permute-start | bytes 3538952 | tf_op jit(solution)/shard_map/ppermute | solution.py:163
  180.1 28.2 %collective-permute-start.33 = (bf16[192,3072]{1,0:T(8,128)(2,1)}, bf16[192,3072]{1,0:T(8,128)(2,1)}, u32[]{:S(2)}, u32[]{:S(2)}) collective-permute-start(bf16[192,3072]{1,0:T(8,128)(2,1)} %pad_maximum_fusion), channel_id=1, source_target_pairs={{8,0},{16,8},{24,16},{28,24},{20,28},{12,20},{4,12},{0,4},{9,1},{1... | collective-permute-start | bytes 3538952 | tf_op jit(solution)/shard_map/ppermute | solution.py:166
  180.9 33.4 %collective-permute-start.48 = (bf16[512,1536]{1,0:T(8,128)(2,1)}, bf16[512,1536]{1,0:T(8,128)(2,1)S(1)}, u32[]{:S(2)}, u32[]{:S(2)}) collective-permute-start(bf16[512,1536]{1,0:T(8,128)(2,1)} %collective-permute-done.47), channel_id=1, source_target_pairs={{0,1},{1,0},{2,3},{3,2},{4,5},{5,4},{6,7},{7,6},{8,9},{9,8},{10,11... | collective-permute-start | bytes 4718600 | tf_op jit(solution)/shard_map/ppermute | solution.py:141
  207.0 27.2 %collective-permute-start.34 = (bf16[192,3072]{1,0:T(8,128)(2,1)}, bf16[192,3072]{1,0:T(8,128)(2,1)S(1)}, u32[]{:S(2)}, u32[]{:S(2)}) collective-permute-start(bf16[192,3072]{1,0:T(8,128)(2,1)} %collective-permute-done.32), channel_id=1, source_target_pairs={{0,8},{8,16},{16,24},{24,28},{28,20},{20,12},{12,4},{4,0},{1,9},{9... | collective-permute-start | bytes 3538952 | tf_op jit(solution)/shard_map/ppermute | solution.py:163
  208.3 27.2 %collective-permute-start.35 = (bf16[192,3072]{1,0:T(8,128)(2,1)}, bf16[192,3072]{1,0:T(8,128)(2,1)S(1)}, u32[]{:S(2)}, u32[]{:S(2)}) collective-permute-start(bf16[192,3072]{1,0:T(8,128)(2,1)} %collective-permute-done.33), channel_id=1, source_target_pairs={{8,0},{16,8},{24,16},{28,24},{20,28},{12,20},{4,12},{0,4},{9,1},{1... | collective-permute-start | bytes 3538952 | tf_op jit(solution)/shard_map/ppermute | solution.py:166
  212.6 36.9 %collective-permute-start.31 = (bf16[512,1536]{1,0:T(8,128)(2,1)S(1)}, bf16[512,1536]{1,0:T(8,128)(2,1)S(1)}, u32[]{:S(2)}, u32[]{:S(2)}) collective-permute-start(bf16[512,1536]{1,0:T(8,128)(2,1)S(1)} %multiply_convert_fusion.6), channel_id=1, source_target_pairs={{0,1},{1,0},{2,3},{3,2},{4,5},{5,4},{6,7},{7,6},{8,9},{9,8},{10,11... | collective-permute-start | bytes 4718600 | tf_op jit(solution)/shard_map/ppermute | solution.py:141
  212.7 36.8 %collective-permute-start.41 = (bf16[512,1536]{1,0:T(8,128)(2,1)S(1)}, bf16[512,1536]{1,0:T(8,128)(2,1)S(1)}, u32[]{:S(2)}, u32[]{:S(2)}) collective-permute-start(bf16[512,1536]{1,0:T(8,128)(2,1)S(1)} %multiply_convert_fusion.6), channel_id=1, source_target_pairs={{0,2},{1,3},{2,0},{3,1},{4,6},{5,7},{6,4},{7,5},{8,10},{9,11},{10,... | collective-permute-start | bytes 4718600 | tf_op jit(solution)/shard_map/ppermute | solution.py:145
  234.2 26.1 %collective-permute-start.36 = (bf16[192,3072]{1,0:T(8,128)(2,1)S(1)}, bf16[192,3072]{1,0:T(8,128)(2,1)S(1)}, u32[]{:S(2)}, u32[]{:S(2)}) collective-permute-start(bf16[192,3072]{1,0:T(8,128)(2,1)S(1)} %collective-permute-done.34), channel_id=1, source_target_pairs={{0,8},{8,16},{16,24},{24,28},{28,20},{20,12},{12,4},{4,0},{1,9},{9... | collective-permute-start | bytes 3538952 | tf_op jit(solution)/shard_map/ppermute | solution.py:163
  235.5 26.2 %collective-permute-start.37 = (bf16[192,3072]{1,0:T(8,128)(2,1)S(1)}, bf16[192,3072]{1,0:T(8,128)(2,1)S(1)}, u32[]{:S(2)}, u32[]{:S(2)}) collective-permute-start(bf16[192,3072]{1,0:T(8,128)(2,1)S(1)} %collective-permute-done.35), channel_id=1, source_target_pairs={{8,0},{16,8},{24,16},{28,24},{20,28},{12,20},{4,12},{0,4},{9,1},{1... | collective-permute-start | bytes 3538952 | tf_op jit(solution)/shard_map/ppermute | solution.py:166
  249.5 59.8 %collective-permute-start.42 = (bf16[512,1536]{1,0:T(8,128)(2,1)S(1)}, bf16[512,1536]{1,0:T(8,128)(2,1)S(1)}, u32[]{:S(2)}, u32[]{:S(2)}) collective-permute-start(bf16[512,1536]{1,0:T(8,128)(2,1)S(1)} %collective-permute-done.41), channel_id=1, source_target_pairs={{0,1},{1,0},{2,3},{3,2},{4,5},{5,4},{6,7},{7,6},{8,9},{9,8},{10,11... | collective-permute-start | bytes 4718600 | tf_op jit(solution)/shard_map/ppermute | solution.py:141
  302.3 151.5 %collective-permute-start.46 = (bf16[512,1536]{1,0:T(8,128)(2,1)}, bf16[512,1536]{1,0:T(8,128)(2,1)}, u32[]{:S(2)}, u32[]{:S(2)}) collective-permute-start(bf16[512,1536]{1,0:T(8,128)(2,1)} %constant_dynamic-slice_fusion.18), channel_id=1, source_target_pairs={{0,1},{1,0},{2,3},{3,2},{4,5},{5,4},{6,7},{7,6},{8,9},{9,8},{10,11... | collective-permute-start | bytes 4718600 | tf_op jit(solution)/shard_map/ppermute | solution.py:141
  383.5 30.6 %collective-permute-start.49 = (bf16[512,1536]{1,0:T(8,128)(2,1)S(1)}, bf16[512,1536]{1,0:T(8,128)(2,1)S(1)}, u32[]{:S(2)}, u32[]{:S(2)}) collective-permute-start(bf16[512,1536]{1,0:T(8,128)(2,1)S(1)} %constant_dynamic-slice_fusion.17), channel_id=1, source_target_pairs={{0,1},{1,0},{2,3},{3,2},{4,5},{5,4},{6,7},{7,6},{8,9},{9,8},{10,11... | collective-permute-start | bytes 4718600 | tf_op jit(solution)/shard_map/ppermute | solution.py:141
  385.2 20.5 %collective-permute-start.63 = (bf16[192,2048]{1,0:T(8,128)(2,1)S(1)}, bf16[192,2048]{1,0:T(8,128)(2,1)S(1)}, u32[]{:S(2)}, u32[]{:S(2)}) collective-permute-start(bf16[192,2048]{1,0:T(8,128)(2,1)S(1)} %pad_maximum_fusion.1), channel_id=1, source_target_pairs={{0,8},{8,16},{16,24},{24,28},{28,20},{20,12},{12,4},{4,0},{1,9},{9... | collective-permute-start | bytes 2359304 | tf_op jit(solution)/shard_map/ppermute | solution.py:163
  387.1 47.8 %collective-permute-start.43 = (bf16[512,1536]{1,0:T(8,128)(2,1)S(1)}, bf16[512,1536]{1,0:T(8,128)(2,1)S(1)}, u32[]{:S(2)}, u32[]{:S(2)}) collective-permute-start(bf16[512,1536]{1,0:T(8,128)(2,1)S(1)} %constant_dynamic-slice_fusion.19), channel_id=1, source_target_pairs={{0,1},{1,0},{2,3},{3,2},{4,5},{5,4},{6,7},{7,6},{8,9},{9,8},{10,11... | collective-permute-start | bytes 4718600 | tf_op jit(solution)/shard_map/ppermute | solution.py:141
  387.4 24.9 %collective-permute-start.82 = (bf16[192,1024]{1,0:T(8,128)(2,1)S(1)}, bf16[192,1024]{1,0:T(8,128)(2,1)S(1)}, u32[]{:S(2)}, u32[]{:S(2)}) collective-permute-start(bf16[192,1024]{1,0:T(8,128)(2,1)S(1)} %pad_maximum_fusion.6), channel_id=1, source_target_pairs={{0,8},{8,16},{16,24},{24,28},{28,20},{20,12},{12,4},{4,0},{1,9},{9... | collective-permute-start | bytes 1179656 | tf_op jit(solution)/shard_map/ppermute | solution.py:163
  405.8 20.0 %collective-permute-start.67 = (bf16[192,2048]{1,0:T(8,128)(2,1)S(1)}, bf16[192,2048]{1,0:T(8,128)(2,1)S(1)}, u32[]{:S(2)}, u32[]{:S(2)}) collective-permute-start(bf16[192,2048]{1,0:T(8,128)(2,1)S(1)} %pad_maximum_fusion.2), channel_id=1, source_target_pairs={{8,0},{16,8},{24,16},{28,24},{20,28},{12,20},{4,12},{0,4},{9,1},{1... | collective-permute-start | bytes 2359304 | tf_op jit(solution)/shard_map/ppermute | solution.py:166
  412.3 20.5 %collective-permute-start.64 = (bf16[192,2048]{1,0:T(8,128)(2,1)S(1)}, bf16[192,2048]{1,0:T(8,128)(2,1)S(1)}, u32[]{:S(2)}, u32[]{:S(2)}) collective-permute-start(bf16[192,2048]{1,0:T(8,128)(2,1)S(1)} %add_convert_fusion.10), channel_id=1, source_target_pairs={{0,8},{8,16},{16,24},{24,28},{28,20},{20,12},{12,4},{4,0},{1,9},{9... | collective-permute-start | bytes 2359304 | tf_op jit(solution)/shard_map/ppermute | solution.py:163
  414.1 22.0 %collective-permute-start.86 = (bf16[192,1024]{1,0:T(8,128)(2,1)S(1)}, bf16[192,1024]{1,0:T(8,128)(2,1)S(1)}, u32[]{:S(2)}, u32[]{:S(2)}) collective-permute-start(bf16[192,1024]{1,0:T(8,128)(2,1)S(1)} %pad_maximum_fusion.7), channel_id=1, source_target_pairs={{8,0},{16,8},{24,16},{28,24},{20,28},{12,20},{4,12},{0,4},{9,1},{1... | collective-permute-start | bytes 1179656 | tf_op jit(solution)/shard_map/ppermute | solution.py:166
  432.8 37.3 %collective-permute-start.50 = (bf16[512,1536]{1,0:T(8,128)(2,1)S(1)}, bf16[512,1536]{1,0:T(8,128)(2,1)S(1)}, u32[]{:S(2)}, u32[]{:S(2)}) collective-permute-start(bf16[512,1536]{1,0:T(8,128)(2,1)S(1)} %add_convert_fusion.3), channel_id=1, source_target_pairs={{0,2},{1,3},{2,0},{3,1},{4,6},{5,7},{6,4},{7,5},{8,10},{9,11},{10,... | collective-permute-start | bytes 4718600 | tf_op jit(solution)/shard_map/ppermute | solution.py:145
  435.0 16.0 %collective-permute-start.68 = (bf16[192,2048]{1,0:T(8,128)(2,1)S(1)}, bf16[192,2048]{1,0:T(8,128)(2,1)S(1)}, u32[]{:S(2)}, u32[]{:S(2)}) collective-permute-start(bf16[192,2048]{1,0:T(8,128)(2,1)S(1)} %get-tuple-element.46), channel_id=1, source_target_pairs={{8,0},{16,8},{24,16},{28,24},{20,28},{12,20},{4,12},{0,4},{9,1},{1... | collective-permute-start | bytes 2359304 | tf_op jit(solution)/shard_map/ppermute | solution.py:166
  436.3 37.8 %collective-permute-start.40 = (bf16[512,1536]{1,0:T(8,128)(2,1)S(1)}, bf16[512,1536]{1,0:T(8,128)(2,1)S(1)}, u32[]{:S(2)}, u32[]{:S(2)}) collective-permute-start(bf16[512,1536]{1,0:T(8,128)(2,1)S(1)} %copy-done.40), channel_id=1, source_target_pairs={{0,1},{1,0},{2,3},{3,2},{4,5},{5,4},{6,7},{7,6},{8,9},{9,8},{10,11... | collective-permute-start | bytes 4718600 | tf_op jit(solution)/shard_map/ppermute | solution.py:141
  438.4 58.9 %collective-permute-start.44 = (bf16[512,1536]{1,0:T(8,128)(2,1)S(1)}, bf16[512,1536]{1,0:T(8,128)(2,1)S(1)}, u32[]{:S(2)}, u32[]{:S(2)}) collective-permute-start(bf16[512,1536]{1,0:T(8,128)(2,1)S(1)} %add_convert_fusion.5), channel_id=1, source_target_pairs={{0,2},{1,3},{2,0},{3,1},{4,6},{5,7},{6,4},{7,5},{8,10},{9,11},{10,... | collective-permute-start | bytes 4718600 | tf_op jit(solution)/shard_map/ppermute | solution.py:145
  451.0 51.5 %collective-permute-start.87 = (bf16[192,1024]{1,0:T(8,128)(2,1)S(1)}, bf16[192,1024]{1,0:T(8,128)(2,1)S(1)}, u32[]{:S(2)}, u32[]{:S(2)}) collective-permute-start(bf16[192,1024]{1,0:T(8,128)(2,1)S(1)} %get-tuple-element.54), channel_id=1, source_target_pairs={{8,0},{16,8},{24,16},{28,24},{20,28},{12,20},{4,12},{0,4},{9,1},{1... | collective-permute-start | bytes 1179656 | tf_op jit(solution)/shard_map/ppermute | solution.py:166
  453.7 55.1 %collective-permute-start.84 = (bf16[192,1024]{1,0:T(8,128)(2,1)S(1)}, bf16[192,1024]{1,0:T(8,128)(2,1)S(1)}, u32[]{:S(2)}, u32[]{:S(2)}) collective-permute-start(bf16[192,1024]{1,0:T(8,128)(2,1)S(1)} %get-tuple-element.53), channel_id=1, source_target_pairs={{0,8},{8,16},{16,24},{24,28},{28,20},{20,12},{12,4},{4,0},{1,9},{9... | collective-permute-start | bytes 1179656 | tf_op jit(solution)/shard_map/ppermute | solution.py:163
  470.1 46.1 %collective-permute-start.65 = (bf16[192,2048]{1,0:T(8,128)(2,1)S(1)}, bf16[192,2048]{1,0:T(8,128)(2,1)S(1)}, u32[]{:S(2)}, u32[]{:S(2)}) collective-permute-start(bf16[192,2048]{1,0:T(8,128)(2,1)S(1)} %get-tuple-element.45), channel_id=1, source_target_pairs={{0,8},{8,16},{16,24},{24,28},{28,20},{20,12},{12,4},{4,0},{1,9},{9... | collective-permute-start | bytes 2359304 | tf_op jit(solution)/shard_map/ppermute | solution.py:163
  474.1 42.1 %collective-permute-start.69 = (bf16[192,2048]{1,0:T(8,128)(2,1)S(1)}, bf16[192,2048]{1,0:T(8,128)(2,1)S(1)}, u32[]{:S(2)}, u32[]{:S(2)}) collective-permute-start(bf16[192,2048]{1,0:T(8,128)(2,1)S(1)} %add_convert_fusion.7), channel_id=1, source_target_pairs={{8,0},{16,8},{24,16},{28,24},{20,28},{12,20},{4,12},{0,4},{9,1},{1... | collective-permute-start | bytes 2359304 | tf_op jit(solution)/shard_map/ppermute | solution.py:166
  502.4 16.7 %collective-permute-start.51 = (bf16[512,1536]{1,0:T(8,128)(2,1)S(1)}, bf16[512,1536]{1,0:T(8,128)(2,1)}, u32[]{:S(2)}, u32[]{:S(2)}) collective-permute-start(bf16[512,1536]{1,0:T(8,128)(2,1)S(1)} %get-tuple-element.33), channel_id=1, source_target_pairs={{0,1},{1,0},{2,3},{3,2},{4,5},{5,4},{6,7},{7,6},{8,9},{9,8},{10,11... | collective-permute-start | bytes 4718600 | tf_op jit(solution)/shard_map/ppermute | solution.py:141
  532.6 42.2 %collective-permute-start.72 = (bf16[1536,384]{1,0:T(8,128)(2,1)S(1)}, bf16[1536,384]{1,0:T(8,128)(2,1)S(1)}, u32[]{:S(2)}, u32[]{:S(2)}) collective-permute-start(bf16[1536,384]{1,0:T(8,128)(2,1)S(1)} %slice.332), channel_id=1, source_target_pairs={{0,2},{1,3},{2,0},{3,1},{4,6},{5,7},{6,4},{7,5},{8,10},{9,11},{10,... | collective-permute-start | bytes 3538952 | tf_op jit(solution)/shard_map/ppermute | solution.py:145
  555.4 55.4 %collective-permute-start.53 = (bf16[1536,768]{1,0:T(8,128)(2,1)S(1)}, bf16[1536,768]{1,0:T(8,128)(2,1)S(1)}, u32[]{:S(2)}, u32[]{:S(2)}) collective-permute-start(bf16[1536,768]{1,0:T(8,128)(2,1)S(1)} %convolution_convert_fusion.5), channel_id=1, source_target_pairs={{0,2},{1,3},{2,0},{3,1},{4,6},{5,7},{6,4},{7,5},{8,10},{9,11},{10,... | collective-permute-start | bytes 7077896 | tf_op jit(solution)/shard_map/ppermute | solution.py:145
  577.9 55.5 %collective-permute-start.52 = (bf16[512,1536]{1,0:T(8,128)(2,1)S(1)}, bf16[512,1536]{1,0:T(8,128)(2,1)S(1)}, u32[]{:S(2)}, u32[]{:S(2)}) collective-permute-start(bf16[512,1536]{1,0:T(8,128)(2,1)S(1)} %constant_dynamic-slice_fusion.16), channel_id=1, source_target_pairs={{0,1},{1,0},{2,3},{3,2},{4,5},{5,4},{6,7},{7,6},{8,9},{9,8},{10,11... | collective-permute-start | bytes 4718600 | tf_op jit(solution)/shard_map/ppermute | solution.py:141
  581.6 41.7 %collective-permute-start.78 = (bf16[192,384]{1,0:T(8,128)(2,1)S(1)}, bf16[192,384]{1,0:T(8,128)(2,1)S(1)}, u32[]{:S(2)}, u32[]{:S(2)}) collective-permute-start(bf16[192,384]{1,0:T(8,128)(2,1)S(1)} %pad_maximum_fusion.14), channel_id=1, source_target_pairs={{8,0},{16,8},{24,16},{28,24},{20,28},{12,20},{4,12},{0,4},{9,1},{1... | collective-permute-start | bytes 442376 | tf_op jit(solution)/shard_map/ppermute | solution.py:166
  582.3 34.1 %collective-permute-start.74 = (bf16[192,384]{1,0:T(8,128)(2,1)S(1)}, bf16[192,384]{1,0:T(8,128)(2,1)S(1)}, u32[]{:S(2)}, u32[]{:S(2)}) collective-permute-start(bf16[192,384]{1,0:T(8,128)(2,1)S(1)} %pad_maximum_fusion.13), channel_id=1, source_target_pairs={{0,8},{8,16},{16,24},{24,28},{28,20},{20,12},{12,4},{4,0},{1,9},{9... | collective-permute-start | bytes 442376 | tf_op jit(solution)/shard_map/ppermute | solution.py:163
  623.4 16.8 %collective-permute-start.79 = (bf16[192,384]{1,0:T(8,128)(2,1)S(1)}, bf16[192,384]{1,0:T(8,128)(2,1)S(1)}, u32[]{:S(2)}, u32[]{:S(2)}) collective-permute-start(bf16[192,384]{1,0:T(8,128)(2,1)S(1)} %get-tuple-element.75), channel_id=1, source_target_pairs={{8,0},{16,8},{24,16},{28,24},{20,28},{12,20},{4,12},{0,4},{9,1},{1... | collective-permute-start | bytes 442376 | tf_op jit(solution)/shard_map/ppermute | solution.py:166
  626.3 25.7 %collective-permute-start.76 = (bf16[192,384]{1,0:T(8,128)(2,1)S(1)}, bf16[192,384]{1,0:T(8,128)(2,1)S(1)}, u32[]{:S(2)}, u32[]{:S(2)}) collective-permute-start(bf16[192,384]{1,0:T(8,128)(2,1)S(1)} %get-tuple-element.74), channel_id=1, source_target_pairs={{0,8},{8,16},{16,24},{24,28},{28,20},{20,12},{12,4},{4,0},{1,9},{9... | collective-permute-start | bytes 442376 | tf_op jit(solution)/shard_map/ppermute | solution.py:163
  (104 other events, 1063.9 us)

commit v2 on v1

--- a/solution.py
+++ b/solution.py
@@ -137,6 +137,214 @@
     )(qkv, att, grad, lse, e, jnp.asarray(cos), jnp.asarray(sin))
 
 
+MESH = pl.DeviceIdType.MESH
+
+
+class Places:
+    def __init__(self, size):
+        self.size = size
+        self.half = size // 2
+        self.own = lax.axis_index("dp")
+        self.tensor = lax.axis_index("tensor")
+        odd = self.own % 2
+        self.place = (1 - odd) * (self.own // 2) + odd * (size - 1 - self.own // 2)
+
+    def index(self, step):
+        place = (self.place + step + self.size) % self.size
+        late = place // self.half
+        return (1 - late) * 2 * place + late * (2 * (self.size - 1 - place) + 1)
+
+    def on_ring(self, step):
+        return (self.index(step), self.tensor)
+
+    def peer(self, step):
+        return ((self.own + step + self.size) % self.size, self.tensor)
+
+    def chip(self):
+        return (self.own, (self.tensor + 2) % 4)
+
+    def core(self):
+        return (self.own, self.tensor + 1 - 2 * (self.tensor % 2))
+
+
+def remote(source, target, send, receive, device):
+    return pltpu.make_async_remote_copy(
+        src_ref=source,
+        dst_ref=target,
+        send_sem=send,
+        recv_sem=receive,
+        device_id=device,
+        device_id_type=MESH,
+    )
+
+
+def greet(devices):
+    barrier = pltpu.get_barrier_semaphore()
+    for device in devices:
+        pl.semaphore_signal(barrier, inc=1, device_id=device, device_id_type=MESH)
+    pl.semaphore_wait(barrier, len(devices))
+
+
+class RingGather:
+    def __init__(self, places, slots, send, receive):
+        self.places, self.slots, self.send, self.receive = places, slots, send, receive
+        self.cut = slots.shape[1] // 32 * 16
+        self.sent = []
+
+    def start(self, hop, source=None):
+        places, half = self.places, self.places.half
+        for way, (step, device) in enumerate(
+            ((1 - hop, places.on_ring(1)), (hop - 1, places.on_ring(-1)))
+        ):
+            slot = places.index(step)
+            rows = slice(None)
+            if hop == half:
+                rows = pl.ds(0, self.cut) if way == 0 else pl.ds(self.cut, self.slots.shape[1] - self.cut)
+            view = self.slots.at[slot, rows]
+            copy = remote(
+                view if source is None else source.at[rows],
+                view,
+                self.send.at[way, hop - 1],
+                self.receive.at[way, hop - 1],
+                device,
+            )
+            copy.start()
+            self.sent.append(copy)
+
+    def wait(self, hop):
+        self.sent[2 * hop - 2].wait_recv()
+        self.sent[2 * hop - 1].wait_recv()
+
+    def finish(self):
+        for copy in self.sent:
+            copy.wait_send()
+
+
+def head_kernel(
+    size, tokens, gains, attend_shard, output_shard, normed, attend_own, attend_other, output_both, gain_rows,
+    gain_slots, normed_half, gain_send, gain_receive, ring_send, ring_receive, pass_send, pass_receive,
+    out_send, out_receive, across, local_sem,
+):
+    places = Places(size)
+    half, own = places.half, places.own
+    half_rows = tokens.shape[0]
+    columns = output_shard.shape[1]
+    greet([places.peer(step) for step in range(1, size)] + [places.chip(), places.core()])
+
+    ring = RingGather(places, attend_own, ring_send, ring_receive)
+    ring.start(1, attend_shard)
+    passed = []
+
+    def hand_on(step, number, source=None):
+        slot = places.index(step)
+        copy = remote(
+            attend_own.at[slot] if source is None else source, attend_other.at[slot],
+            pass_send.at[number], pass_receive.at[number], places.chip(),
+        )
+        copy.start()
+        passed.append(copy)
+
+    hand_on(0, 0, attend_shard)
+    output_pass = remote(
+        output_shard, output_both.at[own, :, pl.ds(columns, columns)], across.at[0], across.at[1], places.chip()
+    )
+    output_pass.start()
+    gain_copies = []
+    for step in range(1, size):
+        copy = remote(gains, gain_slots.at[own], gain_send.at[step - 1], gain_receive.at[step - 1], places.peer(step))
+        copy.start()
+        gain_copies.append(copy)
+    keep = pltpu.make_async_copy(attend_shard, attend_own.at[own], local_sem.at[0])
+    keep.start()
+    keep_output = pltpu.make_async_copy(output_shard, output_both.at[own, :, pl.ds(0, columns)], local_sem.at[1])
+    keep_output.start()
+    gain_slots[own] = gains[...]
+    for copy in gain_copies:
+        copy.wait_recv()
+    width = tokens.shape[1] // size
+    for index in range(size):
+        gain_rows[:, index * width : (index + 1) * width] = gain_slots[index][:, :width]
+    gain = gain_rows[0:1, :]
+    tile = 64
+
+    def norm_tile(number, carry):
+        rows = pl.ds(pl.multiple_of(number * tile, tile), tile)
+        values = tokens[rows, :].astype(jnp.float32)
+        inverse = lax.rsqrt(jnp.mean(values * values, axis=1, keepdims=True) + norm_eps)
+        normed_half[rows, :] = (values * inverse * gain).astype(jnp.bfloat16)
+        return carry
+
+    lax.fori_loop(0, half_rows // tile, norm_tile, 0)
+    core = places.tensor % 2
+    mine = pl.ds(pl.multiple_of(core * half_rows, half_rows), half_rows)
+    swap = remote(normed_half, normed.at[mine], across.at[2], across.at[3], places.core())
+    swap.start()
+    keep_normed = pltpu.make_async_copy(normed_half, normed.at[mine], local_sem.at[2])
+    keep_normed.start()
+
+    outputs = RingGather(places, output_both, out_send, out_receive)
+    for hop in range(1, half + 1):
+        ring.wait(hop)
+        if hop < half:
+            ring.start(hop + 1)
+            hand_on(-hop, 2 * hop - 1)
+            hand_on(hop, 2 * hop)
+        else:
+            hand_on(half, size - 1)
+        if hop == 1:
+            output_pass.wait()
+            keep_output.wait()
+            outputs.start(1)
+        else:
+            outputs.wait(hop - 1)
+            outputs.start(hop)
+    outputs.wait(half)
+    for copy in passed:
+        copy.wait()
+    for copy in gain_copies:
+        copy.wait_send()
+    ring.finish()
+    outputs.finish()
+    swap.wait()
+    keep.wait()
+    keep_normed.wait()
+
+
+def head(size, tokens, gains, attend_shard, output_shard):
+    half_rows, features = tokens.shape
+    rows, width = attend_shard.shape
+    columns = output_shard.shape[1]
+    vmem = pl.BlockSpec(memory_space=pltpu.VMEM)
+    anywhere = pl.BlockSpec(memory_space=pl.ANY)
+    dma = pltpu.SemaphoreType.DMA
+    half = size // 2
+    bf16 = jnp.bfloat16
+    return pl.pallas_call(
+        functools.partial(head_kernel, size),
+        in_specs=[vmem, vmem, vmem, vmem],
+        out_specs=[anywhere, anywhere, anywhere, anywhere, vmem],
+        out_shape=[
+            jax.ShapeDtypeStruct((2 * half_rows, features), bf16),
+            jax.ShapeDtypeStruct((size, rows, width), bf16),
+            jax.ShapeDtypeStruct((size, rows, width), bf16),
+            jax.ShapeDtypeStruct((size, rows, 2 * columns), bf16),
+            jax.ShapeDtypeStruct((8, features), jnp.float32),
+        ],
+        scratch_shapes=[
+            pltpu.VMEM((size,) + gains.shape, jnp.float32),
+            pltpu.VMEM((half_rows, features), bf16),
+            dma((size - 1,)), dma((size - 1,)),
+            dma((2, half)), dma((2, half)),
+            dma((size,)), dma((size,)),
+            dma((2, half)), dma((2, half)),
+            dma((4,)), dma((3,)),
+        ],
+        compiler_params=pltpu.CompilerParams(collective_id=1, has_side_effects=True, vmem_limit_bytes=24 * 2**20),
+        cost_estimate=pl.CostEstimate(flops=10**9, bytes_accessed=200 * 2**20, transcendentals=0),
+        name="head",
+    )(tokens, gains, attend_shard, output_shard)
+
+
 def swap_core(v):
     return lax.ppermute(v, "tensor", [(t, t ^ 1) for t in range(4)])
 
@@ -210,16 +418,6 @@
         return own + up.astype(jnp.float32) + down.astype(jnp.float32)
 
 
-def gather_gains(gains, size):
-    own = lax.axis_index("dp")
-    whole = jnp.zeros((size,) + gains.shape, gains.dtype)
-    whole = lax.dynamic_update_slice(whole, gains[None], (own, 0, 0))
-    for step in range(1, size):
-        piece = lax.ppermute(gains, "dp", [(i, (i + step) % size) for i in range(size)])
-        whole = lax.dynamic_update_slice(whole, piece[None], ((own - step + size) % size, 0, 0))
-    return whole
-
-
 def times(left, right):
     return dot(left, right)
 
@@ -275,19 +473,22 @@
     feed_shard = jnp.concatenate([gate_weight, up_weight, down_weight.T], axis=1)
     hidden_units = gate_weight.shape[1]
 
-    gains = gather_gains(jnp.stack([first_gain, second_gain]), dp_size)
-    gain_one = gains[:, 0].reshape(1, -1).astype(f32)
-    gain_two = gains[:, 1].reshape(1, -1).astype(f32)
-
+    lanes = LANES * pl.cdiv(first_gain.shape[0], LANES)
+    both_gains = jnp.stack([first_gain, second_gain]).astype(f32)
+    both_gains = jnp.pad(both_gains, ((0, 6), (0, lanes - first_gain.shape[0])))
+    normed, attend_own, attend_other, output_both, gain_rows = head(
+        dp_size, tokens, both_gains, attend_shard, output_shard
+    )
+    features = tokens.shape[1]
+    attend_own = attend_own.reshape(features, -1)
+    attend_other = attend_other.reshape(features, -1)
+    output_both = output_both.reshape(features, -1)
+    gain_one = gain_rows[0:1]
+    gain_two = gain_rows[1:2]
     activations = tokens.astype(f32)
     inverse_one = lax.rsqrt(jnp.mean(activations * activations, axis=-1, keepdims=True) + norm_eps)
-    normed_own = (activations * inverse_one * gain_one).astype(bf16)
-    normed = pair(normed_own, swap_core(normed_own))
-
-    attend_own, attend_other = ring.gather(attend_shard, passed=True)
-    output_shard, attend_own_late = lax.optimization_barrier((output_shard, attend_own))
-    output_both = ring.gather(jnp.concatenate([output_shard, swap_chip(output_shard)], axis=1))
-    output_both_late, feed_shard = lax.optimization_barrier((output_both, feed_shard))
+
+    normed, feed_shard, attend_own = lax.optimization_barrier((normed, feed_shard, attend_own))
     feed = ring.gather(feed_shard)
     gate_up = feed[:, : 2 * hidden_units]
     down_turned = feed[:, 2 * hidden_units :]

time: 670 us -> 607 us (0.906)
  waiting for transfers between devices: 310 us -> 228 us
  Pallas kernels: 43.9 us -> 106 us
  starting transfers between devices: 98.3 us -> 56.3 us
    pallas_call x0 -> x1, Pallas kernels: none -> 62.3 us  [head(): pl.pallas_call(functools.partial(head_kernel, size), in_specs=[vmem, vmem...]
    ppermute x13 -> x7, waiting for transfers between devices: 133 us -> 87.4 us  [swap_chip(): return lax.ppermute(v, 'tensor', [(t, t ^ 2) for t in range(4)])]
    ppermute x28 -> x20, waiting for transfers between devices: 124 us -> 101 us  [up(): return lax.ppermute(v, 'dp', self.forward)]
    ppermute x13 -> x7, starting transfers between devices: 18.5 us -> 5.07 us  [swap_chip(): return lax.ppermute(v, 'tensor', [(t, t ^ 2) for t in range(4)])]
    ppermute x7 -> x0, waiting for transfers between devices: 11.9 us -> none  [gather_gains(): lax.ppermute(gains, 'dp', [(i, (i + step) % size) for i in range(size)])]
    ppermute x28 -> x20, starting transfers between devices: 34.7 us -> 24 us  [up(): return lax.ppermute(v, 'dp', self.forward)]
    ppermute x28 -> x20, starting transfers between devices: 36.4 us -> 26.8 us  [down(): return lax.ppermute(v, 'dp', self.backward)]
    ppermute x7 -> x0, starting transfers between devices: 8.36 us -> none  [gather_gains(): lax.ppermute(gains, 'dp', [(i, (i + step) % size) for i in range(size)])]
  transfers between devices with their start and end apart: 89 -> 59, of which waited for: 42 -> 28; matrix products, arithmetic and copies ran while one was open for 27% -> 27% of each run, Pallas kernels for 7% -> 3%
where the time goes in v2:
time: 607 us; the launch traced here: 599 us
  waiting for transfers between devices  228 us (38%)
  matrix products  136 us (22%)
  Pallas kernels  106 us (17%)
  starting transfers between devices  56.3 us (9%)
  local copies, waits for them, and re-layouts  36 us (6%)
  other arithmetic  34 us (6%)
    dot_general x19, matrix products, dot(): lax.dot_general(a, b, (dims, ((), ())), preferred_element_type=jnp.float32)  136 us
    ppermute x20, waiting for transfers between devices, up(): return lax.ppermute(v, 'dp', self.forward)  101 us
    ppermute x7, waiting for transfers between devices, swap_chip(): return lax.ppermute(v, 'tensor', [(t, t ^ 2) for t in range(4)])  87.4 us
    pallas_call x1, Pallas kernels, head(): pl.pallas_call(functools.partial(head_kernel, size), in_specs=[vmem, vmem...  62.3 us
    ppermute x20, waiting for transfers between devices, down(): return lax.ppermute(v, 'dp', self.backward)  39.7 us
    ppermute x20, starting transfers between devices, down(): return lax.ppermute(v, 'dp', self.backward)  26.8 us
    pallas_call x2, Pallas kernels, attend_fwd(): pl.pallas_call(fwd_kernel, grid=(groups,), in_specs=[pl.BlockSpec((LENGTH...  26 us
    ppermute x20, starting transfers between devices, up(): return lax.ppermute(v, 'dp', self.forward)  24 us
  transfers between devices with their start and end apart: 59, of which 28 were waited for; matrix products, arithmetic and copies ran while one was open for 27% of the time, Pallas kernels for 3%

profile of v2, /device:TPU:0, one launch (start us, length us, event | category | flops | bytes accessed | tf_op | source)
XLA Modules:
  0.0 599.0 jit_solution(16406676545418173931)
XLA Ops:
  6.9 62.3 %head.1 = (bf16[1024,1536]{1,0:T(8,128)(2,1)S(1)}, bf16[8,192,768]{2,1,0:T(8,128)(2,1)S(1)}, bf16[8,192,768]{2,1,0:T(8,128)(2,1)S(1)}, bf16[8,192,768]{2,1,0:T(8,128)(2,1)S(1)}, f32[8,1536]{1,0:T(8,128)S(1)}) custom-call(bf16[512,1536]{1,0:T(8,128)(2,1)S(1)} %copy-done, f32[8,256]{1,0:T(8,128)S(1)} %fusion.71.gains, ...), custom_call_target="tpu_custom_call" | custom-call | flops 1000000000 | bytes 209715200 | tf_op jit(solution)/shard_map/head/pallas_call | solution.py:322
  73.4 12.9 %attend_forward.2 = (bf16[1024,1024]{1,0:T(8,128)(2,1)S(1)}, bf16[1024,512]{1,0:T(8,128)(2,1)S(1)}, f32[2,2,1024]{2,1,0:T(2,128)S(1)}) custom-call(bf16[1024,1536]{1,0:T(8,128)(2,1)S(1)} %get-tuple-element.27.normed, bf16[1536,768]{1,0:T(8,128)(2,1)S(1)} %bitcast.38, bf16[384,512]{1,0:T(8,128)(2,1)S(1)} %copy-done.14, f32[1024,128]{1,0:T(8,128)S(1)} %copy-done.10, ...), custom_call_target="tpu_custom_call" | custom-call | flops 12000000000 | bytes 10485760 | tf_op jit(solution)/shard_map/attend_forward/pallas_call | solution.py:74
  87.6 13.1 %attend_forward.3 = (bf16[1024,1024]{1,0:T(8,128)(2,1)S(1)}, bf16[1024,512]{1,0:T(8,128)(2,1)S(1)}, f32[2,2,1024]{2,1,0:T(2,128)S(1)}) custom-call(bf16[1024,1536]{1,0:T(8,128)(2,1)S(1)} %get-tuple-element.27.normed, bf16[1536,768]{1,0:T(8,128)(2,1)S(1)} %bitcast.36, bf16[384,512]{1,0:T(8,128)(2,1)S(1)} %copy-done.14, f32[1024,128]{1,0:T(8,128)S(1)} %copy-done.10, ...), custom_call_target="tpu_custom_call" | custom-call | flops 12000000000 | bytes 10485760 | tf_op jit(solution)/shard_map/attend_forward/pallas_call | solution.py:74
  103.0 4.8 convolution_convert_fusion
  107.9 3.7 convolution_convert_fusion.3
  120.3 22.9 %collective-permute-done.2 = bf16[192,3072]{1,0:T(8,128)(2,1)} collective-permute-done((bf16[192,3072]{1,0:T(8,128)(2,1)}, bf16[192,3072]{1,0:T(8,128)(2,1)}, u32[]{:S(2)}, u32[]{:S(2)}) %collective-permute-start.2) | collective-permute-done | bytes 1179680 | tf_op jit(solution)/shard_map/ppermute | solution.py:371
  154.1 3.4 maximum_select_fusion.2
  157.5 13.6 %collective-permute-done.4 = bf16[192,3072]{1,0:T(8,128)(2,1)S(1)} collective-permute-done((bf16[192,3072]{1,0:T(8,128)(2,1)}, bf16[192,3072]{1,0:T(8,128)(2,1)S(1)}, u32[]{:S(2)}, u32[]{:S(2)}) %collective-permute-start.4) | collective-permute-done | bytes 1179680 | tf_op jit(solution)/shard_map/ppermute | solution.py:371
  173.4 13.9 %collective-permute-done.11 = bf16[512,1536]{1,0:T(8,128)(2,1)S(1)} collective-permute-done((bf16[512,1536]{1,0:T(8,128)(2,1)S(1)}, bf16[512,1536]{1,0:T(8,128)(2,1)S(1)}, u32[]{:S(2)}, u32[]{:S(2)}) %collective-permute-start.11) | collective-permute-done | bytes 1572896 | tf_op jit(solution)/shard_map/ppermute | solution.py:353
  188.3 3.4 maximum_select_fusion.3
  191.6 6.1 %collective-permute-done.6 = bf16[192,3072]{1,0:T(8,128)(2,1)S(1)} collective-permute-done((bf16[192,3072]{1,0:T(8,128)(2,1)S(1)}, bf16[192,3072]{1,0:T(8,128)(2,1)S(1)}, u32[]{:S(2)}, u32[]{:S(2)}) %collective-permute-start.6) | collective-permute-done | bytes 1179680 | tf_op jit(solution)/shard_map/ppermute | solution.py:371
  200.3 10.8 %collective-permute-done.8 = bf16[96,3072]{1,0:T(8,128)(2,1)S(1)} collective-permute-done((bf16[96,3072]{1,0:T(8,128)(2,1)S(1)}, bf16[96,3072]{1,0:T(8,128)(2,1)S(1)}, u32[]{:S(2)}, u32[]{:S(2)}) %collective-permute-start.8) | collective-permute-done | bytes 589856 | tf_op jit(solution)/shard_map/ppermute | solution.py:371
  211.6 9.4 %fusion.33 = f32[1024,2048]{1,0:T(8,128)} fusion(bf16[1024,1536]{1,0:T(8,128)(2,1)S(1)} %maximum_select_fusion, bf16[1536,3072]{1,0:T(8,128)(2,1)S(1)} %maximum_dynamic-update-slice_fusion), kind=kOutput, calls=%fused_computation.45 | convolution fusion | flops 6442450944 | bytes 17825792 | tf_op jit(solution)/shard_map/dot_general | solution.py:37
  220.9 8.8 %multiply_convert_fusion.3 = (bf16[1024,1024]{1,0:T(8,128)(2,1)S(1)}, bf16[1024,1024]{1,0:T(8,128)(2,1)}, bf16[1024,1024]{1,0:T(8,128)(2,1)}) fusion(f32[1024,2048]{1,0:T(8,128)} %fusion.33, bf16[1024,1536]{1,0:T(8,128)(2,1)S(1)} %maximum_select_fusion.2, bf16[1536,3072]{1,0:T(8,128)(2,1)S(1)} %maximum_dynamic-update-slice_fusion), kind=kOutput, calls=%fused_computation.36 | convolution fusion | flops 3238002688 | bytes 20971520 | tf_op jit(solution)/shard_map/dot_general | solution.py:37
  229.8 9.0 %fusion.40 = bf16[1024,1536]{1,0:T(8,128)(2,1)S(1)} fusion(bf16[1536,3072]{1,0:T(8,128)(2,1)S(1)} %maximum_dynamic-update-slice_fusion, bf16[1024,1024]{1,0:T(8,128)(2,1)} %get-tuple-element.52, bf16[1024,1024]{1,0:T(8,128)(2,1)S(1)} %get-tuple-element.51), kind=kOutput, calls=%fused_computation.48 | convolution fusion | flops 6452412416 | bytes 13631488 | tf_op jit(solution)/shard_map/dot_general | solution.py:37
  241.9 3.7 convolution_convert_fusion.2
  247.9 8.9 %fusion.31 = f32[1024,2048]{1,0:T(8,128)} fusion(bf16[1024,1536]{1,0:T(8,128)(2,1)S(1)} %maximum_select_fusion.1, bf16[1536,3072]{1,0:T(8,128)(2,1)S(1)} %maximum_dynamic-update-slice_fusion), kind=kOutput, calls=%fused_computation.43 | convolution fusion | flops 6442450944 | bytes 17825792 | tf_op jit(solution)/shard_map/dot_general | solution.py:37
  256.9 9.1 %multiply_convert_fusion.1 = (bf16[1024,1024]{1,0:T(8,128)(2,1)}, bf16[1024,1024]{1,0:T(8,128)(2,1)}, bf16[1024,1024]{1,0:T(8,128)(2,1)S(1)}) fusion(f32[1024,2048]{1,0:T(8,128)} %fusion.31, bf16[1024,1536]{1,0:T(8,128)(2,1)S(1)} %maximum_select_fusion.3, bf16[1536,3072]{1,0:T(8,128)(2,1)S(1)} %maximum_dynamic-update-slice_fusion), kind=kOutput, calls=%fused_computation.34 | convolution fusion | flops 3238002688 | bytes 20971520 | tf_op jit(solution)/shard_map/dot_general | solution.py:37
  266.0 8.2 %fusion.45 = bf16[1536,1024]{1,0:T(8,128)(2,1)} fusion(bf16[1024,1024]{1,0:T(8,128)(2,1)S(1)} %get-tuple-element.56, bf16[1024,1024]{1,0:T(8,128)(2,1)S(1)} %copy-done.55, bf16[1024,1536]{1,0:T(8,128)(2,1)S(1)} %maximum_select_fusion.3, bf16[1024,1536]{1,0:T(8,128)(2,1)S(1)} %maximum_select_fusion.2), kind=kOutput, calls=%fused_computation.49 | convolution fusion | flops 6464995328 | bytes 13631488 | tf_op jit(solution)/shard_map/dot_general | solution.py:37
  274.2 5.0 convolution_convert_fusion.1
  279.1 8.2 %fusion.35 = bf16[1024,1536]{1,0:T(8,128)(2,1)} fusion(bf16[1536,3072]{1,0:T(8,128)(2,1)S(1)} %maximum_dynamic-update-slice_fusion, bf16[1024,1024]{1,0:T(8,128)(2,1)S(1)} %copy-done.58, bf16[1024,1024]{1,0:T(8,128)(2,1)S(1)} %copy-done.57), kind=kOutput, calls=%fused_computation.47 | convolution fusion | flops 6452412416 | bytes 13631488 | tf_op jit(solution)/shard_map/dot_general | solution.py:37
  287.3 20.6 %fusion.8 = bf16[1536,2048]{1,0:T(8,128)(2,1)} fusion(bf16[1024,1024]{1,0:T(8,128)(2,1)} %get-tuple-element.54, bf16[1024,1024]{1,0:T(8,128)(2,1)} %get-tuple-element.53, bf16[1024,1024]{1,0:T(8,128)(2,1)} %get-tuple-element.52, bf16[1024,1024]{1,0:T(8,128)(2,1)} %copy-done.56, bf16[1024,1536]{1,0:T(8,128)(2,1)} %copy-done.37, bf16[1024,1536]{1,0:T(8,128)(2,1)} %copy-done.36), kind=kOutput, calls=%fused_computation.8 | convolution fusion | flops 12934184960 | bytes 20971520 | tf_op jit(solution)/shard_map/dot_general | solution.py:37
  316.6 4.7 collective-permute-done.32
  326.6 16.6 %collective-permute-done.33 = bf16[192,2048]{1,0:T(8,128)(2,1)S(1)} collective-permute-done((bf16[192,2048]{1,0:T(8,128)(2,1)S(1)}, bf16[192,2048]{1,0:T(8,128)(2,1)S(1)}, u32[]{:S(2)}, u32[]{:S(2)}) %collective-permute-start.33) | collective-permute-done | bytes 786464 | tf_op jit(solution)/shard_map/ppermute | solution.py:371
  344.1 6.0 collective-permute-done.52
  352.7 10.9 %collective-permute-done.37 = bf16[192,2048]{1,0:T(8,128)(2,1)S(1)} collective-permute-done((bf16[192,2048]{1,0:T(8,128)(2,1)S(1)}, bf16[192,2048]{1,0:T(8,128)(2,1)S(1)}, u32[]{:S(2)}, u32[]{:S(2)}) %collective-permute-start.37) | collective-permute-done | bytes 786464 | tf_op jit(solution)/shard_map/ppermute | solution.py:374
  365.2 5.4 collective-permute-done.34
  374.0 3.1 collective-permute-done.53
  377.9 11.7 %collective-permute-done.38 = bf16[192,2048]{1,0:T(8,128)(2,1)S(1)} collective-permute-done((bf16[192,2048]{1,0:T(8,128)(2,1)S(1)}, bf16[192,2048]{1,0:T(8,128)(2,1)S(1)}, u32[]{:S(2)}, u32[]{:S(2)}) %collective-permute-start.38) | collective-permute-done | bytes 786464 | tf_op jit(solution)/shard_map/ppermute | solution.py:374
  392.0 15.9 %collective-permute-done.20 = bf16[512,1536]{1,0:T(8,128)(2,1)S(1)} collective-permute-done((bf16[512,1536]{1,0:T(8,128)(2,1)S(1)}, bf16[512,1536]{1,0:T(8,128)(2,1)S(1)}, u32[]{:S(2)}, u32[]{:S(2)}) %collective-permute-start.20) | collective-permute-done | bytes 1572896 | tf_op jit(solution)/shard_map/ppermute | solution.py:353
  410.9 25.9 %collective-permute-done.14 = bf16[512,1536]{1,0:T(8,128)(2,1)S(1)} collective-permute-done((bf16[512,1536]{1,0:T(8,128)(2,1)S(1)}, bf16[512,1536]{1,0:T(8,128)(2,1)S(1)}, u32[]{:S(2)}, u32[]{:S(2)}) %collective-permute-start.14) | collective-permute-done | bytes 1572896 | tf_op jit(solution)/shard_map/ppermute | solution.py:353
  436.9 5.0 fusion.80
  444.1 2.8 fusion.91
  447.0 6.7 %collective-permute-done.58 = bf16[192,1024]{1,0:T(8,128)(2,1)S(1)} collective-permute-done((bf16[192,1024]{1,0:T(8,128)(2,1)S(1)}, bf16[192,1024]{1,0:T(8,128)(2,1)S(1)}, u32[]{:S(2)}, u32[]{:S(2)}) %collective-permute-start.58) | collective-permute-done | bytes 393248 | tf_op jit(solution)/shard_map/ppermute | solution.py:374
  457.7 11.4 %convolution_convert_fusion.4 = bf16[1536,768]{1,0:T(8,128)(2,1)} fusion(f32[1024,768]{1,0:T(8,128)} %fusion.91, bf16[1024,512]{1,0:T(8,128)(2,1)S(1)} %copy-done.20, bf16[768,512]{1,0:T(8,128)(2,1)} %constant.202, bf16[512,1536]{1,0:T(8,128)(2,1)} %collective-permute-done.21, bf16[512,1536]{1,0:T(8,128)(2,1)} %copy-done.42, pred[]{:T(512)S(6)} %eq.53), kind=kOutput, calls=%fused_computation.54 | convolution fusion | flops 3238133760 | bytes 10485761 | tf_op jit(solution)/shard_map/dot_general | solution.py:37
  471.1 7.2 %convolution_convert_fusion.6 = bf16[1024,1024]{1,0:T(8,128)(2,1)S(1)} fusion(bf16[1536,1024]{1,0:T(8,128)(2,1)} %copy-done.53, bf16[512,1536]{1,0:T(8,128)(2,1)} %collective-permute-done.21, bf16[512,1536]{1,0:T(8,128)(2,1)} %copy-done.42, pred[]{:T(512)S(6)} %eq.53), kind=kOutput, calls=%fused_computation.87 | convolution fusion | flops 3236429824 | bytes 8388609 | tf_op jit(solution)/shard_map/dot_general | solution.py:37
  480.5 9.0 %attend_backward.3 = bf16[1024,768]{1,0:T(8,128)(2,1)S(1)} custom-call(bf16[1024,1024]{1,0:T(8,128)(2,1)S(1)} %copy-done.25, bf16[1024,512]{1,0:T(8,128)(2,1)S(1)} %copy-done.21, bf16[1024,512]{1,0:T(8,128)(2,1)S(1)} %get-tuple-element.82.grad_ref, f32[2,2,1024]{2,1,0:T(2,128)S(1)} %get-tuple-element.38.lse_ref, bf16[384,512]{1,0:T(8,128)(2,1)S(1)} %copy-done.15, ...), custom_call_target="tpu_custom_call" | custom-call | flops 24000000000 | bytes 10485760 | tf_op jit(solution)/shard_map/attend_backward/pallas_call | solution.py:126
  489.5 2.9 convolution_convert_fusion.5
  494.1 9.2 %attend_backward.2 = bf16[1024,768]{1,0:T(8,128)(2,1)S(1)} custom-call(bf16[1024,1024]{1,0:T(8,128)(2,1)S(1)} %copy-done.23, bf16[1024,512]{1,0:T(8,128)(2,1)S(1)} %copy-done.3, bf16[1024,512]{1,0:T(8,128)(2,1)S(1)} %get-tuple-element.83.grad_ref, f32[2,2,1024]{2,1,0:T(2,128)S(1)} %get-tuple-element.36.lse_ref, bf16[384,512]{1,0:T(8,128)(2,1)S(1)} %copy-done.15, ...), custom_call_target="tpu_custom_call" | custom-call | flops 24000000000 | bytes 10485760 | tf_op jit(solution)/shard_map/attend_backward/pallas_call | solution.py:126
  503.2 4.6 fusion.90
  507.9 4.9 add_convert_fusion
  521.4 27.3 %collective-permute-done.23 = bf16[1536,768]{1,0:T(8,128)(2,1)S(1)} collective-permute-done((bf16[1536,768]{1,0:T(8,128)(2,1)S(1)}, bf16[1536,768]{1,0:T(8,128)(2,1)S(1)}, u32[]{:S(2)}, u32[]{:S(2)}) %collective-permute-start.23) | collective-permute-done | bytes 2359328 | tf_op jit(solution)/shard_map/ppermute | solution.py:353
  548.7 2.9 add_convert_fusion.1
  555.6 2.7 collective-permute-done.24
  560.9 2.6 collective-permute-start.49
  565.6 3.1 collective-permute-done.25
  572.0 3.7 collective-permute-done.26
  579.7 5.6 collective-permute-done.30
  (300 shorter events, 123.3 us)
Async XLA Ops:
  114.6 30.7 %collective-permute-start = (bf16[512,1536]{1,0:T(8,128)(2,1)}, bf16[512,1536]{1,0:T(8,128)(2,1)}, u32[]{:S(2)}, u32[]{:S(2)}) collective-permute-start(bf16[512,1536]{1,0:T(8,128)(2,1)} %constant_dynamic-slice_fusion.21), channel_id=1, source_target_pairs={{0,1},{1,0},{2,3},{3,2},{4,5},{5,4},{6,7},{7,6},{8,9},{9,8},{10,11... | collective-permute-start | bytes 4718600 | tf_op jit(solution)/shard_map/ppermute | solution.py:349
  114.6 28.7 %collective-permute-start.2 = (bf16[192,3072]{1,0:T(8,128)(2,1)}, bf16[192,3072]{1,0:T(8,128)(2,1)}, u32[]{:S(2)}, u32[]{:S(2)}) collective-permute-start(bf16[192,3072]{1,0:T(8,128)(2,1)} %pad_maximum_fusion), channel_id=1, source_target_pairs={{0,8},{8,16},{16,24},{24,28},{28,20},{20,12},{12,4},{4,0},{1,9},{9... | collective-permute-start | bytes 3538952 | tf_op jit(solution)/shard_map/ppermute | solution.py:371
  115.1 28.7 %collective-permute-start.3 = (bf16[192,3072]{1,0:T(8,128)(2,1)}, bf16[192,3072]{1,0:T(8,128)(2,1)}, u32[]{:S(2)}, u32[]{:S(2)}) collective-permute-start(bf16[192,3072]{1,0:T(8,128)(2,1)} %pad_maximum_fusion), channel_id=1, source_target_pairs={{8,0},{16,8},{24,16},{28,24},{20,28},{12,20},{4,12},{0,4},{9,1},{1... | collective-permute-start | bytes 3538952 | tf_op jit(solution)/shard_map/ppermute | solution.py:374
  116.6 31.9 %collective-permute-start.15 = (bf16[512,1536]{1,0:T(8,128)(2,1)}, bf16[512,1536]{1,0:T(8,128)(2,1)}, u32[]{:S(2)}, u32[]{:S(2)}) collective-permute-start(bf16[512,1536]{1,0:T(8,128)(2,1)} %param.34), channel_id=1, source_target_pairs={{0,1},{1,0},{2,3},{3,2},{4,5},{5,4},{6,7},{7,6},{8,9},{9,8},{10,11... | collective-permute-start | bytes 4718600 | tf_op jit(solution)/shard_map/ppermute | solution.py:349
  116.6 37.5 %collective-permute-start.17 = (bf16[512,1536]{1,0:T(8,128)(2,1)}, bf16[512,1536]{1,0:T(8,128)(2,1)}, u32[]{:S(2)}, u32[]{:S(2)}) collective-permute-start(bf16[512,1536]{1,0:T(8,128)(2,1)} %param.34), channel_id=1, source_target_pairs={{0,2},{1,3},{2,0},{3,1},{4,6},{5,7},{6,4},{7,5},{8,10},{9,11},{10,... | collective-permute-start | bytes 4718600 | tf_op jit(solution)/shard_map/ppermute | solution.py:353
  143.3 27.8 %collective-permute-start.4 = (bf16[192,3072]{1,0:T(8,128)(2,1)}, bf16[192,3072]{1,0:T(8,128)(2,1)S(1)}, u32[]{:S(2)}, u32[]{:S(2)}) collective-permute-start(bf16[192,3072]{1,0:T(8,128)(2,1)} %collective-permute-done.2), channel_id=1, source_target_pairs={{0,8},{8,16},{16,24},{24,28},{28,20},{20,12},{12,4},{4,0},{1,9},{9... | collective-permute-start | bytes 3538952 | tf_op jit(solution)/shard_map/ppermute | solution.py:371
  143.8 27.8 %collective-permute-start.5 = (bf16[192,3072]{1,0:T(8,128)(2,1)}, bf16[192,3072]{1,0:T(8,128)(2,1)S(1)}, u32[]{:S(2)}, u32[]{:S(2)}) collective-permute-start(bf16[192,3072]{1,0:T(8,128)(2,1)} %collective-permute-done.3), channel_id=1, source_target_pairs={{8,0},{16,8},{24,16},{28,24},{20,28},{12,20},{4,12},{0,4},{9,1},{1... | collective-permute-start | bytes 3538952 | tf_op jit(solution)/shard_map/ppermute | solution.py:374
  148.4 38.9 %collective-permute-start.1 = (bf16[512,1536]{1,0:T(8,128)(2,1)S(1)}, bf16[512,1536]{1,0:T(8,128)(2,1)S(1)}, u32[]{:S(2)}, u32[]{:S(2)}) collective-permute-start(bf16[512,1536]{1,0:T(8,128)(2,1)S(1)} %multiply_convert_fusion.6), channel_id=1, source_target_pairs={{0,1},{1,0},{2,3},{3,2},{4,5},{5,4},{6,7},{7,6},{8,9},{9,8},{10,11... | collective-permute-start | bytes 4718600 | tf_op jit(solution)/shard_map/ppermute | solution.py:349
  148.5 38.8 %collective-permute-start.11 = (bf16[512,1536]{1,0:T(8,128)(2,1)S(1)}, bf16[512,1536]{1,0:T(8,128)(2,1)S(1)}, u32[]{:S(2)}, u32[]{:S(2)}) collective-permute-start(bf16[512,1536]{1,0:T(8,128)(2,1)S(1)} %multiply_convert_fusion.6), channel_id=1, source_target_pairs={{0,2},{1,3},{2,0},{3,1},{4,6},{5,7},{6,4},{7,5},{8,10},{9,11},{10,... | collective-permute-start | bytes 4718600 | tf_op jit(solution)/shard_map/ppermute | solution.py:353
  154.1 34.2 %collective-permute-start.18 = (bf16[512,1536]{1,0:T(8,128)(2,1)}, bf16[512,1536]{1,0:T(8,128)(2,1)S(1)}, u32[]{:S(2)}, u32[]{:S(2)}) collective-permute-start(bf16[512,1536]{1,0:T(8,128)(2,1)} %collective-permute-done.17), channel_id=1, source_target_pairs={{0,1},{1,0},{2,3},{3,2},{4,5},{5,4},{6,7},{7,6},{8,9},{9,8},{10,11... | collective-permute-start | bytes 4718600 | tf_op jit(solution)/shard_map/ppermute | solution.py:349
  171.1 26.7 %collective-permute-start.6 = (bf16[192,3072]{1,0:T(8,128)(2,1)S(1)}, bf16[192,3072]{1,0:T(8,128)(2,1)S(1)}, u32[]{:S(2)}, u32[]{:S(2)}) collective-permute-start(bf16[192,3072]{1,0:T(8,128)(2,1)S(1)} %collective-permute-done.4), channel_id=1, source_target_pairs={{0,8},{8,16},{16,24},{24,28},{28,20},{20,12},{12,4},{4,0},{1,9},{9... | collective-permute-start | bytes 3538952 | tf_op jit(solution)/shard_map/ppermute | solution.py:371
  171.6 26.8 %collective-permute-start.7 = (bf16[192,3072]{1,0:T(8,128)(2,1)S(1)}, bf16[192,3072]{1,0:T(8,128)(2,1)S(1)}, u32[]{:S(2)}, u32[]{:S(2)}) collective-permute-start(bf16[192,3072]{1,0:T(8,128)(2,1)S(1)} %collective-permute-done.5), channel_id=1, source_target_pairs={{8,0},{16,8},{24,16},{28,24},{20,28},{12,20},{4,12},{0,4},{9,1},{1... | collective-permute-start | bytes 3538952 | tf_op jit(solution)/shard_map/ppermute | solution.py:374
  187.3 59.7 %collective-permute-start.12 = (bf16[512,1536]{1,0:T(8,128)(2,1)S(1)}, bf16[512,1536]{1,0:T(8,128)(2,1)S(1)}, u32[]{:S(2)}, u32[]{:S(2)}) collective-permute-start(bf16[512,1536]{1,0:T(8,128)(2,1)S(1)} %collective-permute-done.11), channel_id=1, source_target_pairs={{0,1},{1,0},{2,3},{3,2},{4,5},{5,4},{6,7},{7,6},{8,9},{9,8},{10,11... | collective-permute-start | bytes 4718600 | tf_op jit(solution)/shard_map/ppermute | solution.py:349
  197.8 13.2 %collective-permute-start.8 = (bf16[96,3072]{1,0:T(8,128)(2,1)S(1)}, bf16[96,3072]{1,0:T(8,128)(2,1)S(1)}, u32[]{:S(2)}, u32[]{:S(2)}) collective-permute-start(bf16[96,3072]{1,0:T(8,128)(2,1)S(1)} %slice.262), channel_id=1, source_target_pairs={{0,8},{8,16},{16,24},{24,28},{28,20},{20,12},{12,4},{4,0},{1,9},{9... | collective-permute-start | bytes 1769480 | tf_op jit(solution)/shard_map/ppermute | solution.py:371
  198.5 12.9 %collective-permute-start.9 = (bf16[96,3072]{1,0:T(8,128)(2,1)S(1)}, bf16[96,3072]{1,0:T(8,128)(2,1)S(1)}, u32[]{:S(2)}, u32[]{:S(2)}) collective-permute-start(bf16[96,3072]{1,0:T(8,128)(2,1)S(1)} %slice.263), channel_id=1, source_target_pairs={{8,0},{16,8},{24,16},{28,24},{20,28},{12,20},{4,12},{0,4},{9,1},{1... | collective-permute-start | bytes 1769480 | tf_op jit(solution)/shard_map/ppermute | solution.py:374
  240.0 151.5 %collective-permute-start.16 = (bf16[512,1536]{1,0:T(8,128)(2,1)}, bf16[512,1536]{1,0:T(8,128)(2,1)S(1)}, u32[]{:S(2)}, u32[]{:S(2)}) collective-permute-start(bf16[512,1536]{1,0:T(8,128)(2,1)} %constant_dynamic-slice_fusion.18), channel_id=1, source_target_pairs={{0,1},{1,0},{2,3},{3,2},{4,5},{5,4},{6,7},{7,6},{8,9},{9,8},{10,11... | collective-permute-start | bytes 4718600 | tf_op jit(solution)/shard_map/ppermute | solution.py:349
  309.5 11.8 %collective-permute-start.32 = (bf16[96,2048]{1,0:T(8,128)(2,1)S(1)}, bf16[96,2048]{1,0:T(8,128)(2,1)S(1)}, u32[]{:S(2)}, u32[]{:S(2)}) collective-permute-start(bf16[96,2048]{1,0:T(8,128)(2,1)S(1)} %get-tuple-element.61), channel_id=1, source_target_pairs={{0,8},{8,16},{16,24},{24,28},{28,20},{20,12},{12,4},{4,0},{1,9},{9... | collective-permute-start | bytes 1179656 | tf_op jit(solution)/shard_map/ppermute | solution.py:371
  310.8 11.5 %collective-permute-start.36 = (bf16[96,2048]{1,0:T(8,128)(2,1)S(1)}, bf16[96,2048]{1,0:T(8,128)(2,1)S(1)}, u32[]{:S(2)}, u32[]{:S(2)}) collective-permute-start(bf16[96,2048]{1,0:T(8,128)(2,1)S(1)} %get-tuple-element.63), channel_id=1, source_target_pairs={{8,0},{16,8},{24,16},{28,24},{20,28},{12,20},{4,12},{0,4},{9,1},{1... | collective-permute-start | bytes 1179656 | tf_op jit(solution)/shard_map/ppermute | solution.py:374
  312.9 11.7 %collective-permute-start.51 = (bf16[96,1024]{1,0:T(8,128)(2,1)S(1)}, bf16[96,1024]{1,0:T(8,128)(2,1)S(1)}, u32[]{:S(2)}, u32[]{:S(2)}) collective-permute-start(bf16[96,1024]{1,0:T(8,128)(2,1)S(1)} %get-tuple-element.69), channel_id=1, source_target_pairs={{0,8},{8,16},{16,24},{24,28},{28,20},{20,12},{12,4},{4,0},{1,9},{9... | collective-permute-start | bytes 589832 | tf_op jit(solution)/shard_map/ppermute | solution.py:371
  314.2 10.5 %collective-permute-start.55 = (bf16[96,1024]{1,0:T(8,128)(2,1)S(1)}, bf16[96,1024]{1,0:T(8,128)(2,1)S(1)}, u32[]{:S(2)}, u32[]{:S(2)}) collective-permute-start(bf16[96,1024]{1,0:T(8,128)(2,1)S(1)} %get-tuple-element.71), channel_id=1, source_target_pairs={{8,0},{16,8},{24,16},{28,24},{20,28},{12,20},{4,12},{0,4},{9,1},{1... | collective-permute-start | bytes 589832 | tf_op jit(solution)/shard_map/ppermute | solution.py:374
  321.3 30.2 %collective-permute-start.19 = (bf16[512,1536]{1,0:T(8,128)(2,1)S(1)}, bf16[512,1536]{1,0:T(8,128)(2,1)S(1)}, u32[]{:S(2)}, u32[]{:S(2)}) collective-permute-start(bf16[512,1536]{1,0:T(8,128)(2,1)S(1)} %constant_dynamic-slice_fusion.17), channel_id=1, source_target_pairs={{0,1},{1,0},{2,3},{3,2},{4,5},{5,4},{6,7},{7,6},{8,9},{9,8},{10,11... | collective-permute-start | bytes 4718600 | tf_op jit(solution)/shard_map/ppermute | solution.py:349
  322.6 20.5 %collective-permute-start.33 = (bf16[192,2048]{1,0:T(8,128)(2,1)S(1)}, bf16[192,2048]{1,0:T(8,128)(2,1)S(1)}, u32[]{:S(2)}, u32[]{:S(2)}) collective-permute-start(bf16[192,2048]{1,0:T(8,128)(2,1)S(1)} %pad_maximum_fusion.1), channel_id=1, source_target_pairs={{0,8},{8,16},{16,24},{24,28},{28,20},{20,12},{12,4},{4,0},{1,9},{9... | collective-permute-start | bytes 2359304 | tf_op jit(solution)/shard_map/ppermute | solution.py:371
  324.5 47.3 %collective-permute-start.13 = (bf16[512,1536]{1,0:T(8,128)(2,1)S(1)}, bf16[512,1536]{1,0:T(8,128)(2,1)S(1)}, u32[]{:S(2)}, u32[]{:S(2)}) collective-permute-start(bf16[512,1536]{1,0:T(8,128)(2,1)S(1)} %constant_dynamic-slice_fusion.19), channel_id=1, source_target_pairs={{0,1},{1,0},{2,3},{3,2},{4,5},{5,4},{6,7},{7,6},{8,9},{9,8},{10,11... | collective-permute-start | bytes 4718600 | tf_op jit(solution)/shard_map/ppermute | solution.py:349
  324.8 25.3 %collective-permute-start.52 = (bf16[192,1024]{1,0:T(8,128)(2,1)S(1)}, bf16[192,1024]{1,0:T(8,128)(2,1)S(1)}, u32[]{:S(2)}, u32[]{:S(2)}) collective-permute-start(bf16[192,1024]{1,0:T(8,128)(2,1)S(1)} %pad_maximum_fusion.3), channel_id=1, source_target_pairs={{0,8},{8,16},{16,24},{24,28},{28,20},{20,12},{12,4},{4,0},{1,9},{9... | collective-permute-start | bytes 1179656 | tf_op jit(solution)/shard_map/ppermute | solution.py:371
  343.2 20.5 %collective-permute-start.37 = (bf16[192,2048]{1,0:T(8,128)(2,1)S(1)}, bf16[192,2048]{1,0:T(8,128)(2,1)S(1)}, u32[]{:S(2)}, u32[]{:S(2)}) collective-permute-start(bf16[192,2048]{1,0:T(8,128)(2,1)S(1)} %pad_maximum_fusion.2), channel_id=1, source_target_pairs={{8,0},{16,8},{24,16},{28,24},{20,28},{12,20},{4,12},{0,4},{9,1},{1... | collective-permute-start | bytes 2359304 | tf_op jit(solution)/shard_map/ppermute | solution.py:374
  350.1 20.5 %collective-permute-start.34 = (bf16[192,2048]{1,0:T(8,128)(2,1)S(1)}, bf16[192,2048]{1,0:T(8,128)(2,1)S(1)}, u32[]{:S(2)}, u32[]{:S(2)}) collective-permute-start(bf16[192,2048]{1,0:T(8,128)(2,1)S(1)} %add_convert_fusion.10), channel_id=1, source_target_pairs={{0,8},{8,16},{16,24},{24,28},{28,20},{20,12},{12,4},{4,0},{1,9},{9... | collective-permute-start | bytes 2359304 | tf_op jit(solution)/shard_map/ppermute | solution.py:371
  351.5 22.4 %collective-permute-start.56 = (bf16[192,1024]{1,0:T(8,128)(2,1)S(1)}, bf16[192,1024]{1,0:T(8,128)(2,1)S(1)}, u32[]{:S(2)}, u32[]{:S(2)}) collective-permute-start(bf16[192,1024]{1,0:T(8,128)(2,1)S(1)} %pad_maximum_fusion.4), channel_id=1, source_target_pairs={{8,0},{16,8},{24,16},{28,24},{20,28},{12,20},{4,12},{0,4},{9,1},{1... | collective-permute-start | bytes 1179656 | tf_op jit(solution)/shard_map/ppermute | solution.py:374
  363.6 13.5 %collective-permute-start.53 = (bf16[192,1024]{1,0:T(8,128)(2,1)S(1)}, bf16[192,1024]{1,0:T(8,128)(2,1)S(1)}, u32[]{:S(2)}, u32[]{:S(2)}) collective-permute-start(bf16[192,1024]{1,0:T(8,128)(2,1)S(1)} %add_convert_fusion.14), channel_id=1, source_target_pairs={{0,8},{8,16},{16,24},{24,28},{28,20},{20,12},{12,4},{4,0},{1,9},{9... | collective-permute-start | bytes 1179656 | tf_op jit(solution)/shard_map/ppermute | solution.py:371
  370.6 37.3 %collective-permute-start.20 = (bf16[512,1536]{1,0:T(8,128)(2,1)S(1)}, bf16[512,1536]{1,0:T(8,128)(2,1)S(1)}, u32[]{:S(2)}, u32[]{:S(2)}) collective-permute-start(bf16[512,1536]{1,0:T(8,128)(2,1)S(1)} %add_convert_fusion.3), channel_id=1, source_target_pairs={{0,2},{1,3},{2,0},{3,1},{4,6},{5,7},{6,4},{7,5},{8,10},{9,11},{10,... | collective-permute-start | bytes 4718600 | tf_op jit(solution)/shard_map/ppermute | solution.py:353
  371.8 17.8 %collective-permute-start.38 = (bf16[192,2048]{1,0:T(8,128)(2,1)S(1)}, bf16[192,2048]{1,0:T(8,128)(2,1)S(1)}, u32[]{:S(2)}, u32[]{:S(2)}) collective-permute-start(bf16[192,2048]{1,0:T(8,128)(2,1)S(1)} %get-tuple-element.58), channel_id=1, source_target_pairs={{8,0},{16,8},{24,16},{28,24},{20,28},{12,20},{4,12},{0,4},{9,1},{1... | collective-permute-start | bytes 2359304 | tf_op jit(solution)/shard_map/ppermute | solution.py:374
  373.9 36.2 %collective-permute-start.10 = (bf16[512,1536]{1,0:T(8,128)(2,1)S(1)}, bf16[512,1536]{1,0:T(8,128)(2,1)S(1)}, u32[]{:S(2)}, u32[]{:S(2)}) collective-permute-start(bf16[512,1536]{1,0:T(8,128)(2,1)S(1)} %copy-done.43), channel_id=1, source_target_pairs={{0,1},{1,0},{2,3},{3,2},{4,5},{5,4},{6,7},{7,6},{8,9},{9,8},{10,11... | collective-permute-start | bytes 4718600 | tf_op jit(solution)/shard_map/ppermute | solution.py:349
  377.1 59.8 %collective-permute-start.14 = (bf16[512,1536]{1,0:T(8,128)(2,1)S(1)}, bf16[512,1536]{1,0:T(8,128)(2,1)S(1)}, u32[]{:S(2)}, u32[]{:S(2)}) collective-permute-start(bf16[512,1536]{1,0:T(8,128)(2,1)S(1)} %add_convert_fusion.5), channel_id=1, source_target_pairs={{0,2},{1,3},{2,0},{3,1},{4,6},{5,7},{6,4},{7,5},{8,10},{9,11},{10,... | collective-permute-start | bytes 4718600 | tf_op jit(solution)/shard_map/ppermute | solution.py:353
  389.6 52.3 %collective-permute-start.57 = (bf16[192,1024]{1,0:T(8,128)(2,1)S(1)}, bf16[192,1024]{1,0:T(8,128)(2,1)S(1)}, u32[]{:S(2)}, u32[]{:S(2)}) collective-permute-start(bf16[192,1024]{1,0:T(8,128)(2,1)S(1)} %get-tuple-element.66), channel_id=1, source_target_pairs={{8,0},{16,8},{24,16},{28,24},{20,28},{12,20},{4,12},{0,4},{9,1},{1... | collective-permute-start | bytes 1179656 | tf_op jit(solution)/shard_map/ppermute | solution.py:374
  391.5 55.5 %collective-permute-start.54 = (bf16[192,1024]{1,0:T(8,128)(2,1)S(1)}, bf16[192,1024]{1,0:T(8,128)(2,1)S(1)}, u32[]{:S(2)}, u32[]{:S(2)}) collective-permute-start(bf16[192,1024]{1,0:T(8,128)(2,1)S(1)} %get-tuple-element.65), channel_id=1, source_target_pairs={{0,8},{8,16},{16,24},{24,28},{28,20},{20,12},{12,4},{4,0},{1,9},{9... | collective-permute-start | bytes 1179656 | tf_op jit(solution)/shard_map/ppermute | solution.py:371
  407.9 46.8 %collective-permute-start.35 = (bf16[192,2048]{1,0:T(8,128)(2,1)S(1)}, bf16[192,2048]{1,0:T(8,128)(2,1)S(1)}, u32[]{:S(2)}, u32[]{:S(2)}) collective-permute-start(bf16[192,2048]{1,0:T(8,128)(2,1)S(1)} %get-tuple-element.57), channel_id=1, source_target_pairs={{0,8},{8,16},{16,24},{24,28},{28,20},{20,12},{12,4},{4,0},{1,9},{9... | collective-permute-start | bytes 2359304 | tf_op jit(solution)/shard_map/ppermute | solution.py:371
  410.1 44.6 %collective-permute-start.39 = (bf16[192,2048]{1,0:T(8,128)(2,1)S(1)}, bf16[192,2048]{1,0:T(8,128)(2,1)S(1)}, u32[]{:S(2)}, u32[]{:S(2)}) collective-permute-start(bf16[192,2048]{1,0:T(8,128)(2,1)S(1)} %add_convert_fusion.7), channel_id=1, source_target_pairs={{8,0},{16,8},{24,16},{28,24},{20,28},{12,20},{4,12},{0,4},{9,1},{1... | collective-permute-start | bytes 2359304 | tf_op jit(solution)/shard_map/ppermute | solution.py:374
  441.9 15.8 %collective-permute-start.21 = (bf16[512,1536]{1,0:T(8,128)(2,1)S(1)}, bf16[512,1536]{1,0:T(8,128)(2,1)}, u32[]{:S(2)}, u32[]{:S(2)}) collective-permute-start(bf16[512,1536]{1,0:T(8,128)(2,1)S(1)} %get-tuple-element.47), channel_id=1, source_target_pairs={{0,1},{1,0},{2,3},{3,2},{4,5},{5,4},{6,7},{7,6},{8,9},{9,8},{10,11... | collective-permute-start | bytes 4718600 | tf_op jit(solution)/shard_map/ppermute | solution.py:349
  442.1 11.6 %collective-permute-start.58 = (bf16[192,1024]{1,0:T(8,128)(2,1)S(1)}, bf16[192,1024]{1,0:T(8,128)(2,1)S(1)}, u32[]{:S(2)}, u32[]{:S(2)}) collective-permute-start(bf16[192,1024]{1,0:T(8,128)(2,1)S(1)} %add_convert_fusion.11), channel_id=1, source_target_pairs={{8,0},{16,8},{24,16},{28,24},{20,28},{12,20},{4,12},{0,4},{9,1},{1... | collective-permute-start | bytes 1179656 | tf_op jit(solution)/shard_map/ppermute | solution.py:374
  470.5 42.3 %collective-permute-start.42 = (bf16[1536,384]{1,0:T(8,128)(2,1)S(1)}, bf16[1536,384]{1,0:T(8,128)(2,1)S(1)}, u32[]{:S(2)}, u32[]{:S(2)}) collective-permute-start(bf16[1536,384]{1,0:T(8,128)(2,1)S(1)} %slice.280), channel_id=1, source_target_pairs={{0,2},{1,3},{2,0},{3,1},{4,6},{5,7},{6,4},{7,5},{8,10},{9,11},{10,... | collective-permute-start | bytes 3538952 | tf_op jit(solution)/shard_map/ppermute | solution.py:353
  492.5 56.2 %collective-permute-start.23 = (bf16[1536,768]{1,0:T(8,128)(2,1)S(1)}, bf16[1536,768]{1,0:T(8,128)(2,1)S(1)}, u32[]{:S(2)}, u32[]{:S(2)}) collective-permute-start(bf16[1536,768]{1,0:T(8,128)(2,1)S(1)} %convolution_convert_fusion.5), channel_id=1, source_target_pairs={{0,2},{1,3},{2,0},{3,1},{4,6},{5,7},{6,4},{7,5},{8,10},{9,11},{10,... | collective-permute-start | bytes 7077896 | tf_op jit(solution)/shard_map/ppermute | solution.py:353
  515.5 55.4 %collective-permute-start.22 = (bf16[512,1536]{1,0:T(8,128)(2,1)S(1)}, bf16[512,1536]{1,0:T(8,128)(2,1)S(1)}, u32[]{:S(2)}, u32[]{:S(2)}) collective-permute-start(bf16[512,1536]{1,0:T(8,128)(2,1)S(1)} %constant_dynamic-slice_fusion.16), channel_id=1, source_target_pairs={{0,1},{1,0},{2,3},{3,2},{4,5},{5,4},{6,7},{7,6},{8,9},{9,8},{10,11... | collective-permute-start | bytes 4718600 | tf_op jit(solution)/shard_map/ppermute | solution.py:349
  519.2 41.6 %collective-permute-start.48 = (bf16[192,384]{1,0:T(8,128)(2,1)S(1)}, bf16[192,384]{1,0:T(8,128)(2,1)S(1)}, u32[]{:S(2)}, u32[]{:S(2)}) collective-permute-start(bf16[192,384]{1,0:T(8,128)(2,1)S(1)} %pad_maximum_fusion.11), channel_id=1, source_target_pairs={{8,0},{16,8},{24,16},{28,24},{20,28},{12,20},{4,12},{0,4},{9,1},{1... | collective-permute-start | bytes 442376 | tf_op jit(solution)/shard_map/ppermute | solution.py:374
  519.9 34.0 %collective-permute-start.44 = (bf16[192,384]{1,0:T(8,128)(2,1)S(1)}, bf16[192,384]{1,0:T(8,128)(2,1)S(1)}, u32[]{:S(2)}, u32[]{:S(2)}) collective-permute-start(bf16[192,384]{1,0:T(8,128)(2,1)S(1)} %pad_maximum_fusion.10), channel_id=1, source_target_pairs={{0,8},{8,16},{16,24},{24,28},{28,20},{20,12},{12,4},{4,0},{1,9},{9... | collective-permute-start | bytes 442376 | tf_op jit(solution)/shard_map/ppermute | solution.py:371
  558.7 10.0 %collective-permute-start.25 = (bf16[192,768]{1,0:T(8,128)(2,1)S(1)}, bf16[192,768]{1,0:T(8,128)(2,1)S(1)}, u32[]{:S(2)}, u32[]{:S(2)}) collective-permute-start(bf16[192,768]{1,0:T(8,128)(2,1)S(1)} %pad_maximum_fusion.5), channel_id=1, source_target_pairs={{0,8},{8,16},{16,24},{24,28},{28,20},{20,12},{12,4},{4,0},{1,9},{9... | collective-permute-start | bytes 884744 | tf_op jit(solution)/shard_map/ppermute | solution.py:371
  560.9 16.7 %collective-permute-start.49 = (bf16[192,384]{1,0:T(8,128)(2,1)S(1)}, bf16[192,384]{1,0:T(8,128)(2,1)S(1)}, u32[]{:S(2)}, u32[]{:S(2)}) collective-permute-start(bf16[192,384]{1,0:T(8,128)(2,1)S(1)} %get-tuple-element.87), channel_id=1, source_target_pairs={{8,0},{16,8},{24,16},{28,24},{20,28},{12,20},{4,12},{0,4},{9,1},{1... | collective-permute-start | bytes 442376 | tf_op jit(solution)/shard_map/ppermute | solution.py:374
  563.5 26.2 %collective-permute-start.46 = (bf16[192,384]{1,0:T(8,128)(2,1)S(1)}, bf16[192,384]{1,0:T(8,128)(2,1)S(1)}, u32[]{:S(2)}, u32[]{:S(2)}) collective-permute-start(bf16[192,384]{1,0:T(8,128)(2,1)S(1)} %get-tuple-element.86), channel_id=1, source_target_pairs={{0,8},{8,16},{16,24},{24,28},{28,20},{20,12},{12,4},{4,0},{1,9},{9... | collective-permute-start | bytes 442376 | tf_op jit(solution)/shard_map/ppermute | solution.py:371
  577.6 12.0 %collective-permute-start.50 = (bf16[192,384]{1,0:T(8,128)(2,1)S(1)}, bf16[192,384]{1,0:T(8,128)(2,1)S(1)}, u32[]{:S(2)}, u32[]{:S(2)}) collective-permute-start(bf16[192,384]{1,0:T(8,128)(2,1)S(1)} %add_convert_fusion.23), channel_id=1, source_target_pairs={{8,0},{16,8},{24,16},{28,24},{20,28},{12,20},{4,12},{0,4},{9,1},{1... | collective-permute-start | bytes 442376 | tf_op jit(solution)/shard_map/ppermute | solution.py:374
  578.3 12.2 %collective-permute-start.27 = (bf16[192,768]{1,0:T(8,128)(2,1)S(1)}, bf16[192,768]{1,0:T(8,128)(2,1)S(1)}, u32[]{:S(2)}, u32[]{:S(2)}) collective-permute-start(bf16[192,768]{1,0:T(8,128)(2,1)S(1)} %get-tuple-element.74), channel_id=1, source_target_pairs={{0,8},{8,16},{16,24},{24,28},{28,20},{20,12},{12,4},{4,0},{1,9},{9... | collective-permute-start | bytes 884744 | tf_op jit(solution)/shard_map/ppermute | solution.py:371
  (70 other events, 773.5 us)

commit v3 on v2

v3 whole, which is shorter than its diff:
```python
import functools

import jax
import jax.numpy as jnp
import numpy as np
from jax import lax
from jax.experimental import pallas as pl
from jax.experimental.pallas import tpu as pltpu
from jax.sharding import PartitionSpec as P

HEAD = 96
LENGTH = 1024
LANES = 128
QB = 256
norm_eps = 1e-05
rope_base = 100000.0


def rope_tables():
    half = HEAD // 2
    freq = rope_base ** (np.arange(half, dtype=np.float64) * (-2.0 / HEAD))
    turned = np.arange(LENGTH, dtype=np.float64)[:, None] * freq[None, :]
    cos = np.zeros((LENGTH, LANES), np.float32); sin = np.zeros((LENGTH, LANES), np.float32)
    cos[:, :half] = np.cos(turned); cos[:, 64:64+half] = np.cos(turned)
    sin[:, :half] = -np.sin(turned); sin[:, 64:64+half] = np.sin(turned)
    return cos, sin

def spread(heads, rotary):
    e = np.zeros((heads * HEAD, heads * LANES), np.float32)
    for h in range(heads):
        for i in range(HEAD):
            lane = i if (not rotary[h] or i < 48) else i + 16
            e[h * HEAD + i, h * LANES + lane] = 1
    return e

def dot(a, b, dims=((1,), (0,))):
    return lax.dot_general(a, b, (dims, ((), ())), preferred_element_type=jnp.float32)

C2 = float(HEAD ** -0.5 * np.log2(np.e))


MESH = pl.DeviceIdType.MESH


class Places:
    def __init__(self, size):
        self.size = size
        self.half = size // 2
        self.own = lax.axis_index("dp")
        self.tensor = lax.axis_index("tensor")
        self.side = self.tensor % 2
        odd = self.own % 2
        self.place = (1 - odd) * (self.own // 2) + odd * (size - 1 - self.own // 2)

    def index(self, step):
        place = (self.place + step + self.size) % self.size
        late = place // self.half
        return (1 - late) * 2 * place + late * (2 * (self.size - 1 - place) + 1)

    def on_ring(self, step):
        return (self.index(step), self.tensor)

    def peer(self, step):
        return ((self.own + step + self.size) % self.size, self.tensor)

    def chip(self):
        return (self.own, (self.tensor + 2) % 4)

    def core(self):
        return (self.own, self.tensor + 1 - 2 * self.side)


def remote(source, target, send, receive, device):
    return pltpu.make_async_remote_copy(
        src_ref=source,
        dst_ref=target,
        send_sem=send,
        recv_sem=receive,
        device_id=device,
        device_id_type=MESH,
    )


def greet(devices):
    barrier = pltpu.get_barrier_semaphore()
    for device in devices:
        pl.semaphore_signal(barrier, inc=1, device_id=device, device_id_type=MESH)
    pl.semaphore_wait(barrier, len(devices))


class RingGather:
    def __init__(self, places, slots, send, receive):
        self.places, self.slots, self.send, self.receive = places, slots, send, receive
        self.cut = slots.shape[1] // 32 * 16
        self.sent = []

    def start(self, hop, source=None):
        places, half = self.places, self.places.half
        for way, (step, device) in enumerate(
            ((1 - hop, places.on_ring(1)), (hop - 1, places.on_ring(-1)))
        ):
            slot = places.index(step)
            rows = pl.ds(0, self.slots.shape[1])
            if hop == half:
                rows = (pl.ds(0, self.cut), pl.ds(self.cut, self.slots.shape[1] - self.cut))[way]
            view = self.slots.at[slot, rows]
            copy = remote(
                view if source is None else source.at[rows],
                view,
                self.send.at[way, hop - 1],
                self.receive.at[way, hop - 1],
                device,
            )
            copy.start()
            self.sent.append(copy)

    def wait(self, hop):
        self.sent[2 * hop - 2].wait_recv()
        self.sent[2 * hop - 1].wait_recv()

    def finish(self):
        for copy in self.sent:
            copy.wait_send()


class Spread:
    def __init__(self, places, own, slots, send, receive):
        self.places, self.slots, self.send, self.receive = places, slots, send, receive
        near, far = slots.at[places.side], slots.at[2 + places.side]
        self.chip = remote(own, far, send.at[0], receive.at[0], places.chip())
        self.core = remote(own, near, send.at[1], receive.at[1], places.core())
        self.far = far

    def start(self):
        self.chip.start()
        self.core.start()

    def pass_on(self):
        self.chip.wait_recv()
        self.last = remote(self.far, self.far, self.send.at[2], self.receive.at[2], self.places.core())
        self.last.start()

    def finish(self):
        self.chip.wait_send()
        self.core.wait()
        self.last.wait()


def begin_kernel(
    size, tokens, cotangent, gains, attend_shard, output_shard, feed_shard, cos_ref, sin_ref, rotary_spread,
    plain_spread,
    normed, weights, output_spread, qkv_ref, att_ref, log_ref, hidden, two_slots, cot_slots, feed, gain_rows,
    gain_slots, output_both, terms, received, two_own, gain_send, gain_receive, ring_send, ring_receive,
    pass_send, pass_receive, out_send, out_receive, feed_send, feed_receive, across, two_send, two_receive,
    cot_send, cot_receive, local_sem,
):
    bf16, f32 = jnp.bfloat16, jnp.float32
    places = Places(size)
    half, own = places.half, places.own
    half_rows = tokens.shape[0]
    columns = output_shard.shape[1]
    width = attend_shard.shape[1]
    greet([places.peer(step) for step in range(1, size)] + [places.chip(), places.core()])

    def own_side(slot):
        return weights.at[slot, :, pl.ds(0, width)]

    def other_side(slot):
        return weights.at[slot, :, pl.ds(width, width)]

    ring = RingGather(places, weights.at[:, :, pl.ds(0, width)], ring_send, ring_receive)
    ring.start(1, attend_shard)
    passed = []

    def hand_on(step, number, source=None):
        slot = places.index(step)
        copy = remote(
            own_side(slot) if source is None else source, other_side(slot),
            pass_send.at[number], pass_receive.at[number], places.chip(),
        )
        copy.start()
        passed.append(copy)

    hand_on(0, 0, attend_shard)
    output_pass = remote(
        output_shard, output_both.at[own, :, pl.ds(columns, columns)], across.at[0], across.at[1], places.chip()
    )
    output_pass.start()
    gain_copies = []
    for step in range(1, size):
        copy = remote(gains, gain_slots.at[own], gain_send.at[step - 1], gain_receive.at[step - 1], places.peer(step))
        copy.start()
        gain_copies.append(copy)
    near = cot_slots.at[places.side]
    keep = [
        pltpu.make_async_copy(attend_shard, own_side(own), local_sem.at[0]),
        pltpu.make_async_copy(output_shard, output_both.at[own, :, pl.ds(0, columns)], local_sem.at[1]),
        pltpu.make_async_copy(feed_shard, feed.at[own], local_sem.at[2]),
        pltpu.make_async_copy(cotangent, near, local_sem.at[3]),
    ]
    for copy in keep:
        copy.start()
    gain_slots[own] = gains[...]
    for copy in gain_copies:
        copy.wait_recv()
    part = tokens.shape[1] // size
    for index in range(size):
        gain_rows[:, index * part : (index + 1) * part] = gain_slots[index][:, :part]
    tile = 64
    mine_start = places.side * half_rows

    def norm_tile(number, carry):
        rows = pl.ds(pl.multiple_of(number * tile, tile), tile)
        values = tokens[rows, :].astype(f32)
        inverse = lax.rsqrt(jnp.mean(values * values, axis=1, keepdims=True) + norm_eps)
        target = pl.ds(pl.multiple_of(mine_start + number * tile, tile), tile)
        normed[target, :] = (values * inverse * gain_rows[0:1, :]).astype(bf16)
        return carry

    lax.fori_loop(0, half_rows // tile, norm_tile, 0)
    mine = pl.ds(pl.multiple_of(mine_start, half_rows), half_rows)
    swap = remote(normed.at[mine], normed.at[mine], across.at[2], across.at[3], places.core())
    swap.start()

    for hop in range(1, half + 1):
        ring.wait(hop)
        if hop < half:
            ring.start(hop + 1)
            hand_on(-hop, 2 * hop - 1)
            hand_on(hop, 2 * hop)
        else:
            hand_on(half, size - 1)
    outputs = RingGather(places, output_both, out_send, out_receive)
    output_pass.wait()
    for copy in keep:
        copy.wait()
    outputs.start(1)
    swap.wait()

    def attend(group):
        lanes = pl.ds(group * 4 * HEAD, 4 * HEAD)
        weight = weights[:, :, lanes].reshape(tokens.shape[1], 4 * HEAD)
        weight = dot(weight, rotary_spread[...]).astype(bf16)
        rows = dot(normed[...], weight)
        cos, sin = cos_ref[...], sin_ref[...]
        base = group * 4 * LANES

        def rot(u):
            return (u * cos + pltpu.roll(u, 64, 1) * sin).astype(bf16)

        for head in range(3):
            lane = head * LANES
            qkv_ref[:, base + lane : base + lane + LANES] = rot(rows[:, lane : lane + LANES])
        qkv_ref[:, base + 3 * LANES : base + 4 * LANES] = rows[:, 3 * LANES :].astype(bf16)
        turned = qkv_ref[:, base + 3 * LANES : base + 4 * LANES].T
        key_place = lax.broadcasted_iota(jnp.int32, (QB, QB), 0)
        query_place = lax.broadcasted_iota(jnp.int32, (QB, QB), 1)
        for head in range(2):
            for block in range(LENGTH // QB):
                first, last = block * QB, (block + 1) * QB
                query = qkv_ref[first:last, base + head * LANES : base + (head + 1) * LANES]
                key = qkv_ref[:last, base + 2 * LANES : base + 3 * LANES]
                score = dot(key, query, ((1,), (1,)))
                edge = jnp.where(key_place <= query_place, score[first:], -1e30)
                score = jnp.concatenate([score[:first], edge], axis=0) if block else edge
                top = jnp.max(score, axis=0, keepdims=True)
                weight = jnp.exp2((score - top) * C2)
                total = jnp.sum(weight, axis=0, keepdims=True)
                result = dot(turned[:, :last], weight.astype(bf16)) / total
                lane = group * 2 * LANES + head * LANES
                att_ref[first:last, lane : lane + LANES] = result.T.astype(bf16)
                log_ref[group, head, pl.ds(first, QB)] = (top * C2 + jnp.log2(total))[0]

    attend(0)
    outputs.wait(1)
    outputs.start(2)
    attend(1)
    for hop in range(2, half + 1):
        outputs.wait(hop)
        if hop < half:
            outputs.start(hop + 1)
    ring_feed = RingGather(places, feed, feed_send, feed_receive)
    ring_feed.start(1, feed_shard)
    for copy in passed:
        copy.wait()
    cot = Spread(places, cotangent, cot_slots, cot_send, cot_receive)
    cot.start()
    attend(2)
    attend(3)
    ring_feed.wait(1)
    ring_feed.start(2)

    heads_width = columns // HEAD * LANES
    out_rows = output_shard.shape[0]

    def spread_slot(number, carry):
        rows = pl.ds(pl.multiple_of(number * out_rows, out_rows), out_rows)
        for side in range(2):
            value = dot(output_both[number, :, side * columns : (side + 1) * columns], plain_spread[...])
            output_spread[rows, side * heads_width : (side + 1) * heads_width] = value.astype(bf16)
        return carry

    lax.fori_loop(0, size, spread_slot, 0)
    big = 256

    def theirs_tile(number, carry):
        start = (1 - places.side) * half_rows + number * big
        rows = pl.ds(pl.multiple_of(start, big), big)
        value = dot(att_ref[rows, :], output_spread[...], ((1,), (1,)))
        terms[pl.ds(pl.multiple_of(number * big, big), big), :] = value.astype(bf16)
        return carry

    lax.fori_loop(0, half_rows // big, theirs_tile, 0)
    sum_swap = remote(terms, received, across.at[4], across.at[5], places.core())
    sum_swap.start()

    def mine_tile(number, carry):
        rows = pl.ds(pl.multiple_of(mine_start + number * big, big), big)
        value = dot(att_ref[rows, :], output_spread[...], ((1,), (1,)))
        here = pl.ds(pl.multiple_of(number * big, big), big)
        hidden[here, :] = value + tokens[here, :].astype(f32)
        return carry

    lax.fori_loop(0, half_rows // big, mine_tile, 0)
    sum_swap.wait()

    def second_tile(number, carry):
        rows = pl.ds(pl.multiple_of(number * tile, tile), tile)
        values = hidden[rows, :] + received[rows, :].astype(f32)
        hidden[rows, :] = values
        inverse = lax.rsqrt(jnp.mean(values * values, axis=1, keepdims=True) + norm_eps)
        two_own[rows, :] = (values * inverse * gain_rows[1:2, :]).astype(bf16)
        return carry

    lax.fori_loop(0, half_rows // tile, second_tile, 0)
    two = Spread(places, two_own, two_slots, two_send, two_receive)
    two.start()
    keep_two = pltpu.make_async_copy(two_own, two_slots.at[places.side], local_sem.at[4])
    keep_two.start()
    ring_feed.wait(2)
    ring_feed.start(3)
    cot.pass_on()
    for hop in range(3, half + 1):
        ring_feed.wait(hop)
        if hop < half:
            ring_feed.start(hop + 1)
    two.pass_on()
    cot.finish()
    two.finish()
    keep_two.wait()
    for copy in gain_copies:
        copy.wait_send()
    ring.finish()
    outputs.finish()
    ring_feed.finish()


def begin(size, tokens, cotangent, gains, attend_shard, output_shard, feed_shard):
    half_rows, features = tokens.shape
    rows, width = attend_shard.shape
    columns = output_shard.shape[1]
    heads_width = columns // HEAD * LANES
    groups = 2 * width // (4 * HEAD)
    vmem = pl.BlockSpec(memory_space=pltpu.VMEM)
    anywhere = pl.BlockSpec(memory_space=pl.ANY)
    dma = pltpu.SemaphoreType.DMA
    half = size // 2
    bf16, f32 = jnp.bfloat16, jnp.float32
    cos, sin = rope_tables()
    shape = jax.ShapeDtypeStruct
    return pl.pallas_call(
        functools.partial(begin_kernel, size),
        in_specs=[vmem] * 10,
        out_specs=[vmem, vmem, vmem, vmem, vmem, vmem, vmem, anywhere, anywhere, anywhere, vmem],
        out_shape=[
            shape((2 * half_rows, features), bf16),
            shape((size, rows, 2 * width), bf16),
            shape((features, 2 * heads_width), bf16),
            shape((LENGTH, groups * 4 * LANES), bf16),
            shape((LENGTH, groups * 2 * LANES), bf16),
            shape((groups, 2, LENGTH), f32),
            shape((half_rows, features), f32),
            shape((4, half_rows, features), bf16),
            shape((4, half_rows, features), bf16),
            shape((size,) + feed_shard.shape, bf16),
            shape((8, features), f32),
        ],
        scratch_shapes=[
            pltpu.VMEM((size,) + gains.shape, f32),
            pltpu.VMEM((size, rows, 2 * columns), bf16),
            pltpu.VMEM((half_rows, features), bf16),
            pltpu.VMEM((half_rows, features), bf16),
            pltpu.VMEM((half_rows, features), bf16),
            dma((size - 1,)), dma((size - 1,)),
            dma((2, half)), dma((2, half)),
            dma((size,)), dma((size,)),
            dma((2, half)), dma((2, half)),
            dma((2, half)), dma((2, half)),
            dma((6,)),
            dma((3,)), dma((3,)),
            dma((3,)), dma((3,)),
            dma((5,)),
        ],
        compiler_params=pltpu.CompilerParams(collective_id=1, has_side_effects=True, vmem_limit_bytes=56 * 2**20),
        cost_estimate=pl.CostEstimate(flops=10**10, bytes_accessed=400 * 2**20, transcendentals=0),
        name="begin",
    )(
        tokens, cotangent, gains, attend_shard, output_shard, feed_shard, jnp.asarray(cos), jnp.asarray(sin),
        jnp.asarray(spread(4, (1, 1, 1, 0)), bf16), jnp.asarray(spread(columns // HEAD, (0,) * 4), bf16),
    )


class RingScatter:
    def __init__(self, places, partial, received, send, receive):
        self.places, self.partial, self.received = places, partial, received
        self.send, self.receive = send, receive
        self.rows = received.shape[2]
        self.cut = self.rows // 32 * 16
        self.sent = []

    def start(self, hop):
        places = self.places
        for way in range(2):
            rows = pl.ds(0, self.rows)
            if hop == 1:
                rows = (pl.ds(0, self.cut), pl.ds(self.cut, self.rows - self.cut))[way]
                source = self.partial(places.index(places.half)).at[rows]
            else:
                source = self.received.at[way, hop - 2]
            copy = remote(
                source,
                self.received.at[way, hop - 1, rows],
                self.send.at[way, hop - 1],
                self.receive.at[way, hop - 1],
                places.on_ring(1 - 2 * way),
            )
            copy.start()
            self.sent.append(copy)

    def wait(self, hop):
        self.sent[2 * hop - 2].wait_recv()
        self.sent[2 * hop - 1].wait_recv()

    def add(self, hop):
        distance = self.places.half - hop
        for way in range(2):
            own = self.partial(self.places.index(distance * (1 - 2 * way)))
            here = self.received.at[way, hop - 1]
            first, last = 0, self.rows // 16
            if hop == 1:
                first, last = ((0, self.cut // 16), (self.cut // 16, last))[way]
                start, count = ((self.cut, self.rows - self.cut), (0, self.cut))[way]
                here[start : start + count, :] = own[start : start + count, :]

            def tile(number, carry, own=own, here=here):
                rows = pl.ds(pl.multiple_of(number * 16, 16), 16)
                here[rows, :] = (here[rows, :].astype(jnp.float32) + own[rows, :].astype(jnp.float32)).astype(jnp.bfloat16)
                return carry

            lax.fori_loop(first, last, tile, 0)

    def total(self, rows):
        half = self.places.half
        own = self.partial(self.places.index(0))
        return (
            own[rows, :].astype(jnp.float32)
            + self.received[0, half - 1, rows, :].astype(jnp.float32)
            + self.received[1, half - 1, rows, :].astype(jnp.float32)
        )

    def finish(self):
        for copy in self.sent:
            copy.wait_send()


def finish_kernel(
    size, tokens_hbm, hidden_hbm, branch_own, normed_hbm, weights_hbm, output_hbm, qkv_hbm, att_hbm, feed_grad,
    second_part, log_ref, gain_rows, attend_shard, cos_ref, sin_ref, rotary_spread, plain_spread,
    tokens_grad, attend_sum, output_sum, feed_sum, gain_sum,
    branch, grad_ref, back, dq_ref, dk_ref, dv_ref, own_grad, other_grad, crossed, ring_got, output_grad, output_got,
    feed_got, feed_own, terms, got_terms, output_across, gain_parts,
    normed, weights, output_spread, qkv_two, att_ref, tokens, hidden_grad, load_sem,
    ring_send, ring_receive, out_send, out_receive, feed_send, feed_receive, cross_send, cross_receive, across,
    feed_sem, gain_send, gain_receive,
):
    bf16, f32 = jnp.bfloat16, jnp.float32
    places = Places(size)
    half, own = places.half, places.own
    half_rows, features = tokens_hbm.shape
    rows = attend_shard.shape[0]
    width = attend_shard.shape[1]
    span = 4 * HEAD
    diagonal = (own, 3 - places.tensor)
    greet([places.on_ring(1), places.on_ring(-1), places.chip(), places.core(), diagonal])

    def feed_slot(number):
        return feed_grad.at[pl.ds(pl.multiple_of(number * rows, rows), rows)]

    big = 256
    group_order = (2, 3, 0, 1)

    def qkv_load(number):
        lanes = pl.ds(group_order[number] * 4 * LANES, 4 * LANES)
        return pltpu.make_async_copy(qkv_hbm.at[:, lanes], qkv_two.at[number % 2], load_sem.at[number])

    def row_loads(number):
        here = pl.ds(number * big, big)
        return (
            pltpu.make_async_copy(tokens_hbm.at[here], tokens, load_sem.at[4]),
            pltpu.make_async_copy(hidden_hbm.at[here], hidden_grad, load_sem.at[5]),
        )

    mine = pl.ds(pl.multiple_of(places.side * half_rows, half_rows), half_rows)
    fetch = {
        "branch": pltpu.make_async_copy(branch_own, branch.at[mine], load_sem.at[6]),
        "output": pltpu.make_async_copy(output_hbm, output_spread, load_sem.at[7]),
        "att": pltpu.make_async_copy(att_hbm, att_ref, load_sem.at[8]),
        "normed": pltpu.make_async_copy(normed_hbm, normed, load_sem.at[9]),
        "weights": pltpu.make_async_copy(weights_hbm, weights, load_sem.at[10]),
    }
    loads = []

    def load(step, way):
        copy = pltpu.make_async_copy(feed_slot(places.index(step)), feed_own.at[way], feed_sem.at[len(loads)])
        copy.start()
        loads.append(copy)

    load(half, 0)
    swap = remote(branch_own, branch.at[mine], across.at[0], across.at[1], places.core())
    swap.start()
    fetch["branch"].start()
    fetch["output"].start()
    qkv_loads = [qkv_load(number) for number in range(4)]
    qkv_loads[0].start()
    for name in ("att", "normed", "weights"):
        fetch[name].start()

    current = {}

    def feed_partial(number):
        return current["slot"]

    feed = RingScatter(places, feed_partial, feed_got, feed_send, feed_receive)

    def feed_step(hop):
        feed.wait(hop)
        loads[-2].wait()
        loads[-1].wait()
        distance = half - hop
        for way in range(2):
            part = feed_own.at[way]
            here = feed_got.at[way, hop - 1]
            first, last = 0, rows // 16
            if hop == 1:
                first, last = ((0, feed.cut // 16), (feed.cut // 16, last))[way]
                start, count = ((feed.cut, rows - feed.cut), (0, feed.cut))[way]
                here[start : start + count, :] = part[start : start + count, :]

            def tile(number, carry, part=part, here=here):
                place = pl.ds(pl.multiple_of(number * 16, 16), 16)
                here[place, :] = (here[place, :].astype(f32) + part[place, :].astype(f32)).astype(bf16)
                return carry

            lax.fori_loop(first, last, tile, 0)
        feed.start(hop + 1)
        if distance > 1:
            load(distance - 1, 0)
            load(1 - distance, 1)
        else:
            load(0, 0)

    loads[0].wait()
    current["slot"] = feed_own.at[0]
    feed.start(1)
    swap.wait()
    fetch["branch"].wait()
    fetch["output"].wait()
    fetch["att"].wait()
    token_rows = row_loads(0)
    for copy in token_rows:
        copy.start()

    def back_group(number, target, lane):
        group = group_order[number]
        qkv_loads[number].wait()
        if number < 3:
            qkv_loads[number + 1].start()
        qkv_ref = qkv_two.at[number % 2]
        base = 0
        for part in range(2):
            block = pl.ds(part * half_rows, half_rows)
            value = dot(branch[block, :], output_spread[:, group * 2 * LANES : (group + 1) * 2 * LANES])
            grad_ref[block, :] = value.astype(bf16)
        turned = qkv_ref[:, base + 2 * LANES : base + 3 * LANES].T
        cos, sin = cos_ref[...], sin_ref[...]
        scale = HEAD**-0.5

        def unrot(u):
            return (u * cos - pltpu.roll(u, 64, 1) * sin).astype(bf16)

        key_place = lax.broadcasted_iota(jnp.int32, (QB, QB), 0)
        query_place = lax.broadcasted_iota(jnp.int32, (QB, QB), 1)
        for head in range(2):
            lanes = slice(head * LANES, (head + 1) * LANES)
            att_lane = (2 * group + head) * LANES
            prod = grad_ref[:, lanes].astype(f32) * att_ref[:, att_lane : att_lane + LANES].astype(f32)
            delta = jnp.sum(prod.T, axis=0, keepdims=True)
            for block in reversed(range(LENGTH // QB)):
                first, last = block * QB, (block + 1) * QB
                query = qkv_ref[first:last, base + head * LANES : base + (head + 1) * LANES]
                out_grad = grad_ref[first:last, lanes]
                score = dot(qkv_ref[:last, base + 2 * LANES : base + 3 * LANES], query, ((1,), (1,)))
                prob = jnp.exp2(score * C2 - log_ref[group, head : head + 1, first:last])
                edge = jnp.where(key_place <= query_place, prob[first:], 0.0)
                prob = jnp.concatenate([prob[:first], edge], axis=0) if block else edge
                prob_grad = dot(qkv_ref[:last, base + 3 * LANES : base + 4 * LANES], out_grad, ((1,), (1,)))
                score_grad = (prob * (prob_grad - delta[:, first:last])).astype(bf16)
                key_part = dot(score_grad, query)
                value_part = dot(prob.astype(bf16), out_grad)
                if head == 0 and block == LENGTH // QB - 1:
                    dk_ref[...] = key_part
                    dv_ref[...] = value_part
                else:
                    dk_ref[:last] += key_part
                    dv_ref[:last] += value_part
                dq_ref[first:last, lanes] = dot(turned[:, :last], score_grad).T
        wide = jnp.concatenate(
            [
                unrot(dq_ref[:, :LANES] * scale),
                unrot(dq_ref[:, LANES:] * scale),
                unrot(dk_ref[...] * scale),
                dv_ref[...].astype(bf16),
            ],
            axis=1,
        )
        close_back = dot(wide, rotary_spread[...], ((1,), (1,))).astype(bf16)
        back[:, group * span : (group + 1) * span] = close_back
        if number == 0:
            fetch["normed"].wait()
        for part in range(2):
            block = slice(part * features // 2, (part + 1) * features // 2)
            value = dot(normed[:, block], close_back, ((0,), (0,))).astype(bf16)
            target[part * size // 2 : (part + 1) * size // 2, :, lane : lane + span] = value.reshape(
                size // 2, rows, span
            )

    order = [half]
    for step in range(half - 1, 0, -1):
        order += [step, -step]
    order.append(0)
    crossing = {}

    def cross(group):
        for number, step in enumerate(order):
            slot = places.index(step)
            lanes = pl.ds(group * span, span)
            copy = remote(
                other_grad.at[slot, :, lanes], crossed.at[slot, :, lanes],
                cross_send.at[group, number], cross_receive.at[group, number], places.chip(),
            )
            copy.start()
            crossing[(group, step)] = copy

    back_group(0, other_grad, 0)
    cross(0)
    for copy in feed.sent:
        copy.wait_send()
    load(half - 1, 0)
    load(1 - half, 1)
    back_group(1, other_grad, span)
    cross(1)
    feed_step(1)

    def prepare(step):
        for group in range(2):
            crossing[(group, step)].wait_recv()
        slot = places.index(step)

        def tile(number, carry):
            place = pl.ds(pl.multiple_of(number * 16, 16), 16)
            crossed[slot, place, :] = (crossed[slot, place, :].astype(f32) + own_grad[slot, place, :].astype(f32)).astype(bf16)
            return carry

        lax.fori_loop(0, rows // 16, tile, 0)

    back_group(2, own_grad, 0)
    back_group(3, own_grad, span)

    columns = output_spread.shape[1] // 2 // LANES * HEAD
    heads_width = output_spread.shape[1] // 2
    for side in range(2):
        close = dot(att_ref[:, side * heads_width : (side + 1) * heads_width], plain_spread[...], ((1,), (1,))).astype(bf16)
        for part in range(2):
            block = slice(part * features // 2, (part + 1) * features // 2)
            value = dot(branch[:, block], close, ((0,), (0,))).astype(bf16)
            output_grad[part * size // 2 : (part + 1) * size // 2, :, side * columns : (side + 1) * columns] = value.reshape(
                size // 2, rows, columns
            )
    outputs = RingScatter(places, lambda slot: output_grad.at[slot], output_got, out_send, out_receive)
    outputs.start(1)
    feed_step(2)

    whole = weights.shape[2]
    fetch["weights"].wait()

    def terms_of(block):
        return dot(back[block, :], weights[...].reshape(features, whole), ((1,), (1,)))

    def theirs_tile(number, carry):
        place = (1 - places.side) * half_rows + number * big
        value = terms_of(pl.ds(pl.multiple_of(place, big), big))
        terms[pl.ds(pl.multiple_of(number * big, big), big), :] = value.astype(bf16)
        return carry

    lax.fori_loop(0, half_rows // big, theirs_tile, 0)
    terms_swap = remote(terms, got_terms, across.at[2], across.at[3], places.core())
    terms_swap.start()
    prepare(half)
    attend = RingScatter(places, lambda slot: crossed.at[slot], ring_got, ring_send, ring_receive)
    attend.start(1)
    outputs.wait(1)
    outputs.add(1)
    outputs.start(2)
    terms_swap.wait()

    for number in range(half_rows // big):
        for copy in token_rows:
            copy.wait()
        here = slice(number * big, (number + 1) * big)
        place = places.side * half_rows + number * big
        value = terms_of(pl.ds(pl.multiple_of(place, big), big)) + got_terms[here, :].astype(f32)
        values = tokens[...].astype(f32)
        inverse = lax.rsqrt(jnp.mean(values * values, axis=1, keepdims=True) + norm_eps)
        scaled = value * gain_rows[0:1, :]
        inner = jnp.mean(scaled * values, axis=1, keepdims=True)
        result = hidden_grad[...] + inverse * scaled - values * (inverse * inverse * inverse) * inner
        tokens_grad[here, :] = result.astype(bf16)
        if number < half_rows // big - 1:
            token_rows = row_loads(number + 1)
            for copy in token_rows:
                copy.start()
    prepare(half - 1)
    prepare(1 - half)
    attend.wait(1)
    attend.add(1)
    attend.start(2)
    for hop in range(2, half + 1):
        outputs.wait(hop)
        if hop < half:
            outputs.add(hop)
            outputs.start(hop + 1)
        if hop > 2 and hop < half:
            feed_step(hop)
        if hop < half:
            prepare(half - hop)
            prepare(hop - half)
            attend.wait(hop)
            attend.add(hop)
            attend.start(hop + 1)
    prepare(0)

    def output_total(place):
        return outputs.total(place)

    def output_tile(number, carry):
        place = pl.ds(pl.multiple_of(number * 16, 16), 16)
        value = output_total(place)
        output_sum[place, :] = value[:, :columns]
        output_across[0, place, :] = value[:, columns:]
        return carry

    lax.fori_loop(0, rows // 16, output_tile, 0)
    output_swap = remote(output_across.at[0], output_across.at[1], across.at[4], across.at[5], places.chip())
    output_swap.start()
    attend.wait(half)

    def attend_tile(number, carry):
        place = pl.ds(pl.multiple_of(number * 16, 16), 16)
        value = attend.total(place)
        attend_sum[place, :] = value
        gain = jnp.sum(value * attend_shard[place, :].astype(f32), axis=1, keepdims=True)
        lane = lax.broadcasted_iota(jnp.int32, (16, LANES), 1)
        gain_parts[0, place, :] = jnp.where(lane == 0, gain, 0.0)
        return carry

    lax.fori_loop(0, rows // 16, attend_tile, 0)
    feed.wait(half)
    loads[-1].wait()
    second = pltpu.make_async_copy(second_part, feed_own.at[1], load_sem.at[11])
    second.start()
    second.wait()

    def feed_tile(number, carry):
        place = pl.ds(pl.multiple_of(number * 16, 16), 16)
        value = (
            feed_own[0, place, :].astype(f32)
            + feed_got[0, half - 1, place, :].astype(f32)
            + feed_got[1, half - 1, place, :].astype(f32)
        )
        feed_sum[place, :] = value
        gain = jnp.sum(value * feed_own[1, place, :].astype(f32), axis=1, keepdims=True)
        lane = lax.broadcasted_iota(jnp.int32, (16, LANES), 1)
        gain_parts[0, place, :] += jnp.where(lane == 1, gain, 0.0)
        return carry

    lax.fori_loop(0, rows // 16, feed_tile, 0)
    gain_copies = []
    for number, device in enumerate((places.core(), places.chip(), diagonal)):
        copy = remote(gain_parts.at[0], gain_parts.at[1 + number], gain_send.at[number], gain_receive.at[number], device)
        copy.start()
        gain_copies.append(copy)
    output_swap.wait()
    output_sum[...] += output_across[1]
    for copy in gain_copies:
        copy.wait()
    gain_sum[...] = (gain_parts[0] + gain_parts[1]) + (gain_parts[2] + gain_parts[3])
    for copy in crossing.values():
        copy.wait_send()
    outputs.finish()
    attend.finish()
    for copy in feed.sent[2:]:
        copy.wait_send()


def finish(
    size, tokens, hidden_grad, branch_own, normed, weights, output_spread, qkv, att, logs, gain_rows, feed_grad,
    attend_shard, second_part,
):
    half_rows, features = tokens.shape
    rows, width = attend_shard.shape
    columns = output_spread.shape[1] // 2 // LANES * HEAD
    feed_width = feed_grad.shape[1]
    vmem = pl.BlockSpec(memory_space=pltpu.VMEM)
    anywhere = pl.BlockSpec(memory_space=pl.ANY)
    dma = pltpu.SemaphoreType.DMA
    half = size // 2
    bf16, f32 = jnp.bfloat16, jnp.float32
    cos, sin = rope_tables()
    shape = jax.ShapeDtypeStruct
    buffer = pltpu.VMEM
    return pl.pallas_call(
        functools.partial(finish_kernel, size),
        in_specs=[anywhere] * 10 + [vmem] * 7,
        out_specs=[vmem] * 5,
        out_shape=[
            shape((half_rows, features), bf16),
            shape((rows, width), f32),
            shape((rows, columns), f32),
            shape((rows, feed_width), f32),
            shape((rows, LANES), f32),
        ],
        scratch_shapes=[
            buffer((LENGTH, features), bf16),
            buffer((LENGTH, 2 * LANES), bf16),
            buffer((LENGTH, 2 * width), bf16),
            buffer((LENGTH, 2 * LANES), f32),
            buffer((LENGTH, LANES), f32),
            buffer((LENGTH, LANES), f32),
            buffer((size, rows, width), bf16),
            buffer((size, rows, width), bf16),
            buffer((size, rows, width), bf16),
            buffer((2, half, rows, width), bf16),
            buffer((size, rows, 2 * columns), bf16),
            buffer((2, half, rows, 2 * columns), bf16),
            buffer((2, half, rows, feed_width), bf16),
            buffer((2, rows, feed_width), bf16),
            buffer((half_rows, features), bf16),
            buffer((half_rows, features), bf16),
            buffer((2, rows, columns), f32),
            buffer((4, rows, LANES), f32),
            buffer((LENGTH, features), bf16),
            buffer(weights.shape, bf16),
            buffer(output_spread.shape, bf16),
            buffer((2, LENGTH, 4 * LANES), bf16),
            buffer(att.shape, bf16),
            buffer((256, features), bf16),
            buffer((256, features), f32),
            dma((12,)),
            dma((2, half)), dma((2, half)),
            dma((2, half)), dma((2, half)),
            dma((2, half)), dma((2, half)),
            dma((2, size)), dma((2, size)),
            dma((6,)),
            dma((2 * half,)),
            dma((3,)), dma((3,)),
        ],
        compiler_params=pltpu.CompilerParams(collective_id=2, has_side_effects=True, vmem_limit_bytes=62 * 2**20),
        cost_estimate=pl.CostEstimate(flops=3 * 10**10, bytes_accessed=300 * 2**20, transcendentals=0),
        name="finish",
    )(
        tokens, hidden_grad, branch_own, normed, weights, output_spread, qkv, att, feed_grad, second_part, logs,
        gain_rows, attend_shard, jnp.asarray(cos), jnp.asarray(sin),
        jnp.asarray(spread(4, (1, 1, 1, 0)), bf16), jnp.asarray(spread(4, (0,) * 4), bf16),
    )


def swap_core(v):
    return lax.ppermute(v, "tensor", [(t, t ^ 1) for t in range(4)])


def swap_chip(v):
    return lax.ppermute(v, "tensor", [(t, t ^ 2) for t in range(4)])


class Ring:
    def __init__(self, size):
        self.size = size
        self.half = size // 2
        order = list(range(0, size, 2)) + list(range(size - 1, 0, -2))
        self.forward = [(order[i], order[(i + 1) % size]) for i in range(size)]
        self.backward = [(b, a) for a, b in self.forward]
        own = lax.axis_index("dp")
        self.place = jnp.where(own % 2 == 0, own // 2, size - 1 - own // 2)

    def index(self, step):
        place = (self.place + step + self.size) % self.size
        return jnp.where(place < self.half, 2 * place, 2 * (self.size - 1 - place) + 1)

    def up(self, v):
        return lax.ppermute(v, "dp", self.forward)

    def down(self, v):
        return lax.ppermute(v, "dp", self.backward)

    def scatter(self, take):
        far = take(self.index(self.half))
        cut = far.shape[0] // 2
        up, down = self.up(far[:cut]), self.down(far[cut:])
        for step in range(self.half - 1, 0, -1):
            ahead = take(self.index(step)).astype(jnp.float32)
            behind = take(self.index(-step)).astype(jnp.float32)
            if step == self.half - 1:
                ahead = jnp.concatenate([ahead[:cut] + up.astype(jnp.float32), ahead[cut:]], axis=0)
                behind = jnp.concatenate([behind[:cut], behind[cut:] + down.astype(jnp.float32)], axis=0)
            else:
                ahead = ahead + up.astype(jnp.float32)
                behind = behind + down.astype(jnp.float32)
            up, down = self.up(ahead.astype(jnp.bfloat16)), self.down(behind.astype(jnp.bfloat16))
        own = take(self.index(0)).astype(jnp.float32)
        return own + up.astype(jnp.float32) + down.astype(jnp.float32)


def times(left, right):
    return dot(left, right)


def times_transpose(left, right):
    return dot(left, right, ((1,), (1,)))


def contract_rows(left, right):
    return dot(left, right, ((0,), (0,)))


def local(
    dp_size,
    tokens,
    first_gain,
    query_weight,
    key_weight,
    value_weight,
    output_weight,
    second_gain,
    gate_weight,
    up_weight,
    down_weight,
    cotangent,
):
    ring = Ring(dp_size)
    half_rows = tokens.shape[0]
    core = lax.axis_index("tensor") % 2
    bf16, f32 = jnp.bfloat16, jnp.float32

    def pair(own, other):
        return jnp.where(
            core == 0,
            jnp.concatenate([own, other], axis=0),
            jnp.concatenate([other, own], axis=0),
        )

    def mine(rows):
        return lax.dynamic_slice_in_dim(rows, core * half_rows, half_rows, 0)

    def theirs(rows):
        return lax.dynamic_slice_in_dim(rows, (1 - core) * half_rows, half_rows, 0)

    groups = key_weight.shape[1] // HEAD
    packs = []
    for group in range(groups):
        packs.append(query_weight[:, group * 2 * HEAD : (group + 1) * 2 * HEAD])
        packs.append(key_weight[:, group * HEAD : (group + 1) * HEAD])
        packs.append(value_weight[:, group * HEAD : (group + 1) * HEAD])
    attend_shard = jnp.concatenate(packs, axis=1)
    output_shard = output_weight.T
    feed_shard = jnp.concatenate([gate_weight, up_weight, down_weight.T], axis=1)
    hidden_units = gate_weight.shape[1]

    lanes = LANES * pl.cdiv(first_gain.shape[0], LANES)
    both_gains = jnp.stack([first_gain, second_gain]).astype(f32)
    both_gains = jnp.pad(both_gains, ((0, 6), (0, lanes - first_gain.shape[0])))
    gate_up_shard, down_shard = feed_shard[:, : 2 * hidden_units], feed_shard[:, 2 * hidden_units :]
    (normed, weights, output_spread, qkv, attended, logs, hidden_state, two_slots, cot_slots, feed, gain_rows) = begin(
        dp_size, tokens, cotangent, both_gains, attend_shard, output_shard, feed_shard
    )
    features = tokens.shape[1]
    feed = feed.reshape(features, -1)
    gate_up = feed[:, : 2 * hidden_units]
    down_turned = feed[:, 2 * hidden_units :]
    gain_two = gain_rows[1:2]
    inverse_two = lax.rsqrt(
        jnp.mean(hidden_state * hidden_state, axis=-1, keepdims=True) + norm_eps
    )
    two_all = two_slots.reshape(-1, features)
    cot_all = cot_slots.reshape(-1, features)
    both_rows = 2 * half_rows
    two_near, two_far = two_all[:both_rows], two_all[both_rows:]
    cot_near, cot_far = cot_all[:both_rows], cot_all[both_rows:]

    def gather_rows(near, far):
        near_sum = mine(near).astype(f32) + swap_core(theirs(near)).astype(f32)
        far_sum = mine(far).astype(f32) + swap_core(theirs(far)).astype(f32)
        return near_sum + swap_chip(far_sum.astype(bf16)).astype(f32)

    def feed_forward(two, cot):
        both = times(two, gate_up)
        gate, up = both[:, :hidden_units], both[:, hidden_units:]
        inner_grad = times(cot, down_turned)
        sigmoid = jax.nn.sigmoid(gate)
        inner = (gate * sigmoid * up).astype(bf16)
        up_grad = (inner_grad * gate * sigmoid).astype(bf16)
        gate_grad = (inner_grad * up * sigmoid * (1.0 + gate * (1.0 - sigmoid))).astype(bf16)
        return inner, jnp.concatenate([gate_grad, up_grad], axis=1)

    inner_near, grad_near = feed_forward(two_near, cot_near)
    inner_far, grad_far = feed_forward(two_far, cot_far)
    two_terms_far = times_transpose(grad_far, gate_up).astype(bf16)
    two_terms_near = times_transpose(grad_near, gate_up).astype(bf16)
    out_far = times_transpose(inner_far, down_turned).astype(bf16)
    out_near = times_transpose(inner_near, down_turned).astype(bf16)
    normed_two_grad = gather_rows(two_terms_near, two_terms_far)
    layer_out = (hidden_state + gather_rows(out_near, out_far)).astype(bf16)

    down_grad = contract_rows(
        cot_all,
        jnp.concatenate([inner_near, inner_far], axis=0),
    ).astype(bf16)
    gate_up_grad = contract_rows(
        two_all,
        jnp.concatenate([grad_near, grad_far], axis=0),
    ).astype(bf16)
    shard_rows = first_gain.shape[0]

    def part(whole):
        return lambda index: lax.dynamic_slice_in_dim(whole, index * shard_rows, shard_rows, 0)

    down_sum = ring.scatter(part(down_grad))

    scaled_two = normed_two_grad * gain_two
    hidden_grad = (
        cotangent.astype(f32)
        + inverse_two * scaled_two
        - hidden_state
        * inverse_two**3
        * jnp.mean(scaled_two * hidden_state, axis=-1, keepdims=True)
    )
    branch_own = hidden_grad.astype(bf16)
    tokens_grad, attend_sum, output_sum, gate_up_sum, gain_sums = finish(
        dp_size, tokens, hidden_grad, branch_own, normed, weights, output_spread, qkv, attended, logs, gain_rows,
        gate_up_grad, attend_shard, gate_up_shard,
    )
    block = 4 * HEAD
    query_grad = jnp.concatenate(
        [attend_sum[:, g * block : g * block + 2 * HEAD] for g in range(groups)], axis=1
    )
    key_grad = jnp.concatenate(
        [attend_sum[:, g * block + 2 * HEAD : g * block + 3 * HEAD] for g in range(groups)], axis=1
    )
    value_grad = jnp.concatenate(
        [attend_sum[:, g * block + 3 * HEAD : (g + 1) * block] for g in range(groups)], axis=1
    )
    return (
        layer_out,
        tokens_grad,
        gain_sums[:, 0] / first_gain.astype(f32),
        query_grad,
        key_grad,
        value_grad,
        output_sum.T,
        gain_sums[:, 1] / second_gain.astype(f32),
        gate_up_sum[:, :hidden_units],
        gate_up_sum[:, hidden_units:],
        down_sum.T,
    )


def solution(mesh):
    in_specs = (
        P(("dp", "tensor"), None),
        P("dp"),
        P("dp", "tensor"),
        P("dp", "tensor"),
        P("dp", "tensor"),
        P("tensor", "dp"),
        P("dp"),
        P("dp", "tensor"),
        P("dp", "tensor"),
        P("tensor", "dp"),
        P(("dp", "tensor"), None),
    )
    out_specs = (
        P(("dp", "tensor"), None),
        P(("dp", "tensor"), None),
        P("dp"),
        P("dp", "tensor"),
        P("dp", "tensor"),
        P("dp", "tensor"),
        P("tensor", "dp"),
        P("dp"),
        P("dp", "tensor"),
        P("dp", "tensor"),
        P("tensor", "dp"),
    )
    body = functools.partial(local, mesh.shape["dp"])
    return jax.shard_map(body, mesh=mesh, in_specs=in_specs, out_specs=out_specs, check_vma=False)
```

time: 607 us -> 534 us (0.88)
  waiting for transfers between devices: 228 us -> 34.9 us
  Pallas kernels: 106 us -> 296 us
  starting transfers between devices: 56.3 us -> 12.2 us
  matrix products: 136 us -> 110 us
    pallas_call x5 -> x2, Pallas kernels: 106 us -> 296 us  [the longest x1 165 us: begin(): pl.pallas_call(functools.partial(begin_kernel, size), in_specs=[vmem] * 1...]
    ppermute x20 -> x4, waiting for transfers between devices: 101 us -> 6.28 us  [up(): return lax.ppermute(v, 'dp', self.forward)]
    ppermute x7 -> x2, waiting for transfers between devices: 87.4 us -> 28.6 us  [swap_chip(): return lax.ppermute(v, 'tensor', [(t, t ^ 2) for t in range(4)])]
    ppermute x20 -> x4, waiting for transfers between devices: 39.7 us -> 0.01 us  [down(): return lax.ppermute(v, 'dp', self.backward)]
    dot_general x19 -> x10, matrix products: 136 us -> 110 us  [dot(): lax.dot_general(a, b, (dims, ((), ())), preferred_element_type=jnp.float32)]
    ppermute x20 -> x4, starting transfers between devices: 26.8 us -> 3.22 us  [down(): return lax.ppermute(v, 'dp', self.backward)]
    ppermute x20 -> x4, starting transfers between devices: 24 us -> 5.67 us  [up(): return lax.ppermute(v, 'dp', self.forward)]
    select_n x4 -> x0, other arithmetic: 8.6 us -> none  [pair(): jnp.where(core == 0, jnp.concatenate([own, other], axis=0), jnp.concatena...]
  transfers between devices with their start and end apart: 59 -> 14, of which waited for: 28 -> 2; matrix products, arithmetic and copies ran while one was open for 27% -> 17% of each run, Pallas kernels for 3% -> 0%
where the time goes in v3:
time: 534 us; the launch traced here: 524 us
  Pallas kernels  296 us (55%)
  matrix products  110 us (21%)
  local copies, waits for them, and re-layouts  36.2 us (7%)
  waiting for transfers between devices  34.9 us (7%)
  other arithmetic  32.9 us (6%)
  starting transfers between devices  12.2 us (2%)
    pallas_call x1, Pallas kernels, begin(): pl.pallas_call(functools.partial(begin_kernel, size), in_specs=[vmem] * 1...  165 us
    pallas_call x1, Pallas kernels, finish(): pl.pallas_call(functools.partial(finish_kernel, size), in_specs=[anywhere...  131 us
    dot_general x10, matrix products, dot(): lax.dot_general(a, b, (dims, ((), ())), preferred_element_type=jnp.float32)  110 us
    ppermute x2, waiting for transfers between devices, swap_chip(): return lax.ppermute(v, 'tensor', [(t, t ^ 2) for t in range(4)])  28.6 us
    unnamed x60, local copies, waits for them, and re-layouts  12.6 us
  transfers between devices with their start and end apart: 14, of which 2 were waited for; matrix products, arithmetic and copies ran while one was open for 17% of the time, Pallas kernels for 0%

profile of v3, /device:TPU:0, one launch (start us, length us, event | category | flops | bytes accessed | tf_op | source)
XLA Modules:
  0.0 523.7 jit_solution(13127826622194616964)
XLA Ops:
  0.7 1.1 fusion.65
  3.1 1.1 fusion.66
  4.8 2.3 pad_maximum_fusion.feed_shard
  8.0 165.1 %begin.1 = (bf16[1024,1536]{1,0:T(8,128)(2,1)}, bf16[8,192,1536]{2,1,0:T(8,128)(2,1)}, bf16[1536,1024]{1,0:T(8,128)(2,1)}, bf16[1024,2048]{1,0:T(8,128)(2,1)}, b...) custom-call(bf16[512,1536]{1,0:T(8,128)(2,1)} %tokens_hbm.1, ...), custom_call_target="tpu_custom_call" | custom-call | flops 10000000000 | bytes 419430400 | tf_op jit(solution)/shard_map/begin/pallas_call | solution.py:371
  173.2 3.4 fusion.61
  176.6 1.2 copy-done.3
  177.8 2.3 fusion.60
  180.1 1.3 slice-done.3
  181.8 8.9 %fusion.27 = f32[1024,2048]{1,0:T(8,128)} fusion(bf16[1024,1536]{1,0:T(8,128)(2,1)S(1)} %bitcast.27, bf16[1536,3072]{1,0:T(8,128)(2,1)S(1)} %bitcast.39), kind=kOutput, calls=%fused_computation.33 | convolution fusion | flops 6442450944 | bytes 17825792 | tf_op jit(solution)/shard_map/dot_general | solution.py:37
  190.6 9.2 %fusion.25 = f32[1024,2048]{1,0:T(8,128)} fusion(bf16[1024,1536]{1,0:T(8,128)(2,1)S(1)} %bitcast.26, bf16[1536,3072]{1,0:T(8,128)(2,1)S(1)} %bitcast.40), kind=kOutput, calls=%fused_computation.31 | convolution fusion | flops 6442450944 | bytes 17825792 | tf_op jit(solution)/shard_map/dot_general | solution.py:37
  199.8 12.3 %multiply_convert_fusion.3 = (bf16[1024,1024]{1,0:T(8,128)(2,1)}, bf16[1024,1024]{1,0:T(8,128)(2,1)}, bf16[1024,1024]{1,0:T(8,128)(2,1)S(1)}) fusion(f32[1024,2048]{1,0:T(8,128)} %fusion.27, bf16[1024,1536]{1,0:T(8,128)(2,1)} %bitcast.25, bf16[1536,3072]{1,0:T(8,128)(2,1)} %bitcast.31), kind=kOutput, calls=%fused_computation.24 | convolution fusion | flops 3238002688 | bytes 20971520 | tf_op jit(solution)/shard_map/dot_general | solution.py:37
  212.2 9.0 %multiply_convert_fusion.1 = (bf16[1024,1024]{1,0:T(8,128)(2,1)}, bf16[1024,1024]{1,0:T(8,128)(2,1)}, bf16[1024,1024]{1,0:T(8,128)(2,1)S(1)}) fusion(f32[1024,2048]{1,0:T(8,128)S(1)} %copy-done.18, bf16[1024,1536]{1,0:T(8,128)(2,1)S(1)} %bitcast.24, bf16[1536,3072]{1,0:T(8,128)(2,1)} %bitcast.32), kind=kOutput, calls=%fused_computation.22 | convolution fusion | flops 3238002688 | bytes 20971520 | tf_op jit(solution)/shard_map/dot_general | solution.py:37
  221.2 7.0 %fusion.29 = bf16[1536,1024]{1,0:T(8,128)(2,1)S(1)} fusion(bf16[2048,1536]{1,0:T(8,128)(2,1)S(1)} %bitcast.23, bf16[1024,1024]{1,0:T(8,128)(2,1)S(1)} %get-tuple-element.54, bf16[1024,1024]{1,0:T(8,128)(2,1)S(1)} %get-tuple-element.53), kind=kOutput, calls=%fused_computation.35 | convolution fusion | flops 6452412416 | bytes 13631488 | tf_op jit(solution)/shard_map/dot_general | solution.py:37
  228.2 1.6 copy-done.9
  230.6 2.3 collective-permute-start.10
  233.1 6.0 %convolution_convert_fusion.1 = bf16[1024,1536]{1,0:T(8,128)(2,1)S(1)} fusion(bf16[1024,1024]{1,0:T(8,128)(2,1)} %copy-done.21, bf16[1536,3072]{1,0:T(8,128)(2,1)} %bitcast.33), kind=kOutput, calls=%fused_computation.39 | convolution fusion | flops 3222798336 | bytes 8388608 | tf_op jit(solution)/shard_map/dot_general | solution.py:37
  239.1 1.3 constant_dynamic-slice_fusion.7
  240.5 1.8 copy-done.20
  242.3 6.8 %convolution_convert_fusion = bf16[1024,1536]{1,0:T(8,128)(2,1)} fusion(bf16[1024,1024]{1,0:T(8,128)(2,1)S(1)} %copy-done.20, bf16[1536,3072]{1,0:T(8,128)(2,1)} %bitcast.34), kind=kOutput, calls=%fused_computation.38 | convolution fusion | flops 3222798336 | bytes 8388608 | tf_op jit(solution)/shard_map/dot_general | solution.py:37
  249.1 1.4 add_convert_fusion.8
  250.5 2.0 collective-permute-start.7
  252.5 2.7 constant_dynamic-slice_fusion.6
  255.4 6.3 %collective-permute-done.7 = bf16[192,1024]{1,0:T(8,128)(2,1)S(1)} collective-permute-done((bf16[192,1024]{1,0:T(8,128)(2,1)S(1)}, bf16[192,1024]{1,0:T(8,128)(2,1)S(1)}, u32[]{:S(2)}, u32[]{:S(2)}) %collective-permute-start.7) | collective-permute-done | bytes 393248 | tf_op jit(solution)/shard_map/ppermute | solution.py:920
  261.6 1.1 add_convert_fusion.6
  262.8 1.8 collective-permute-start.8
  264.5 10.1 %fusion.32 = bf16[1024,1536]{1,0:T(8,128)(2,1)S(1)} fusion(bf16[1536,3072]{1,0:T(8,128)(2,1)} %bitcast.35, bf16[1024,1024]{1,0:T(8,128)(2,1)} %get-tuple-element.52, bf16[1024,1024]{1,0:T(8,128)(2,1)} %get-tuple-element.51), kind=kOutput, calls=%fused_computation.36 | convolution fusion | flops 6452412416 | bytes 13631488 | tf_op jit(solution)/shard_map/dot_general | solution.py:37
  274.7 1.6 copy-done.7
  276.3 1.2 constant_dynamic-slice_fusion.4
  277.5 2.3 add_convert_fusion.5
  280.2 10.1 %fusion.37 = bf16[1024,1536]{1,0:T(8,128)(2,1)S(1)} fusion(bf16[1536,3072]{1,0:T(8,128)(2,1)} %bitcast.36, bf16[1024,1024]{1,0:T(8,128)(2,1)} %get-tuple-element.50, bf16[1024,1024]{1,0:T(8,128)(2,1)} %get-tuple-element.49), kind=kOutput, calls=%fused_computation.37 | convolution fusion | flops 6452412416 | bytes 13631488 | tf_op jit(solution)/shard_map/dot_general | solution.py:37
  290.3 1.7 copy-done.1
  292.0 1.2 constant_dynamic-slice_fusion.5
  293.5 1.7 collective-permute-start.9
  295.2 1.9 add_convert_fusion.3
  297.6 3.0 add_convert_fusion.2
  300.6 1.6 collective-permute-start.2
  302.2 2.9 add_convert_fusion
  305.1 1.4 collective-permute-start.5
  306.5 30.3 %fusion.8.feed_grad = bf16[1536,2048]{1,0:T(8,128)(2,1)} fusion(bf16[2048,1536]{1,0:T(8,128)(2,1)} %bitcast.20, bf16[1024,1024]{1,0:T(8,128)(2,1)} %get-tuple-element.52, bf16[1024,1024]{1,0:T(8,128)(2,1)} %get-tuple-element.51, bf16[1024,1024]{1,0:T(8,128)(2,1)S(1)} %copy-done.23, bf16[1024,1024]{1,0:T(8,128)(2,1)S(1)} %copy-done.22), kind=kOutput, calls=%fused_computation.8 | convolution fusion | flops 12921602048 | bytes 20971520 | tf_op jit(solution)/shard_map/dot_general | solution.py:37
  337.8 1.9 pad_maximum_fusion.1.second_part
  339.8 2.3 add_bitcast_fusion
  342.1 28.6 %collective-permute-done.5 = bf16[512,1536]{1,0:T(8,128)(2,1)} collective-permute-done((bf16[512,1536]{1,0:T(8,128)(2,1)}, bf16[512,1536]{1,0:T(8,128)(2,1)}, u32[]{:S(2)}, u32[]{:S(2)}) %collective-permute-start.5) | collective-permute-done | bytes 1572896 | tf_op jit(solution)/shard_map/ppermute | solution.py:902
  370.7 3.7 multiply_reduce_fusion.1
  375.4 5.8 %fusion.59 = (bf16[512,1536]{1,0:T(8,128)(2,1)}, f32[512,1536]{1,0:T(8,128)}, bf16[512,1536]{1,0:T(8,128)(2,1)}) fusion(f32[512]{0:T(512)S(1)} %broadcast_multiply_fusion, f32[512,1536]{1,0:T(8,128)S(1)} %copy-done, f32[512]{0:T(512)S(1)} %get-tuple-element.83, f32[1536]{0:T(1024)S(1)} %slice_reduce_fusion.2, bf16[512,1536]{1,0:T(8,128)(2,1)} %collective-permute-done.5, ...), kind=kLoop, calls=%fused_computation.96 | loop fusion | flops 15728640 | bytes 20459524 | tf_op jit(solution)/shard_map/convert_element_type | solution.py:1066
  381.2 131.2 %finish.1 = (bf16[512,1536]{1,0:T(8,128)(2,1)}, f32[192,768]{1,0:T(8,128)}, f32[192,384]{1,0:T(8,128)}, f32[192,2048]{1,0:T(8,128)}, f32[192,128]{1,0:T(8,128)}) custom-call(bf16[512,1536]{1,0:T(8,128)(2,1)} %tokens_hbm.1, f32[512,1536]{1,0:T(8,128)} %get-tuple-element.48.hidden_hbm, bf16[512,1536]{1,0:T(8,128)(2,1)} %get-tuple-element.47.branch_own, ...), custom_call_target="tpu_custom_call" | custom-call | flops 30000001024 | bytes 314572800 | tf_op jit(solution)/shard_map/finish/pallas_call | solution.py:841
  512.4 1.4 fusion.63
  514.9 2.7 fusion.62
  521.4 1.1 copy.42
  (92 shorter events, 13.1 us)
Async XLA Ops:
  173.1 4.6 copy-start.3
  173.1 6.9 %slice-start.2 = ((s8[9437184]{0:T(1024)(128)(4,1)}), s8[4194304]{0:T(1024)(128)(4,1)S(1)}, s32[]{:S(2)}) async-start(s8[9437184]{0:T(1024)(128)(4,1)} %bitcast.37), calls=%async_computation.2 | async-start | bytes 8388608
  173.1 8.2 %slice-start.3 = ((s8[9437184]{0:T(1024)(128)(4,1)}), s8[4194304]{0:T(1024)(128)(4,1)S(1)}, s32[]{:S(2)}) async-start(s8[9437184]{0:T(1024)(128)(4,1)} %bitcast.37), calls=%async_computation.3 | async-start | bytes 8388608
  177.8 4.0 slice-start.4
  199.8 12.3 %copy-start.18 = (f32[1024,2048]{1,0:T(8,128)S(1)}, f32[1024,2048]{1,0:T(8,128)}, u32[]{:S(2)}) copy-start(f32[1024,2048]{1,0:T(8,128)} %fusion.25) | copy-start | bytes 25165828
  199.8 21.4 %slice-start = ((s8[6291456]{0:T(1024)(128)(4,1)}), s8[4194304]{0:T(1024)(128)(4,1)S(1)}, s32[]{:S(2)}) async-start(s8[6291456]{0:T(1024)(128)(4,1)} %bitcast.21), calls=%async_computation | async-start | bytes 8388608
  212.1 9.0 %copy-start.21 = (bf16[1024,1024]{1,0:T(8,128)(2,1)}, bf16[1024,1024]{1,0:T(8,128)(2,1)S(1)}, u32[]{:S(2)}) copy-start(bf16[1024,1024]{1,0:T(8,128)(2,1)S(1)} %get-tuple-element.53) | copy-start | bytes 6291460
  212.2 9.1 %slice-start.1 = ((s8[6291456]{0:T(1024)(128)(4,1)}), s8[2097152]{0:T(1024)(128)(4,1)S(1)}, s32[]{:S(2)}) async-start(s8[6291456]{0:T(1024)(128)(4,1)} %bitcast.21), calls=%async_computation.1 | async-start | bytes 4194304
  221.2 7.0 %copy-start.19 = (bf16[1024,1024]{1,0:T(8,128)(2,1)}, bf16[1024,1024]{1,0:T(8,128)(2,1)S(1)}, u32[]{:S(2)}) copy-start(bf16[1024,1024]{1,0:T(8,128)(2,1)S(1)} %get-tuple-element.54) | copy-start | bytes 6291460
  228.2 1.6 copy-start.9
  230.6 18.5 %collective-permute-start.10 = (bf16[96,1024]{1,0:T(8,128)(2,1)}, bf16[96,1024]{1,0:T(8,128)(2,1)}, u32[]{:S(2)}, u32[]{:S(2)}) collective-permute-start(bf16[96,1024]{1,0:T(8,128)(2,1)} %get-tuple-element.65), channel_id=1, source_target_pairs={{8,0},{16,8},{24,16},{28,24},{20,28},{12,20},{4,12},{0,4},{9,1},{1... | collective-permute-start | bytes 589832 | tf_op jit(solution)/shard_map/ppermute | solution.py:923
  232.9 16.2 %collective-permute-start.6 = (bf16[96,1024]{1,0:T(8,128)(2,1)}, bf16[96,1024]{1,0:T(8,128)(2,1)}, u32[]{:S(2)}, u32[]{:S(2)}) collective-permute-start(bf16[96,1024]{1,0:T(8,128)(2,1)} %get-tuple-element.63), channel_id=1, source_target_pairs={{0,8},{8,16},{16,24},{24,28},{28,20},{20,12},{12,4},{4,0},{1,9},{9... | collective-permute-start | bytes 589832 | tf_op jit(solution)/shard_map/ppermute | solution.py:920
  239.1 10.0 %copy-start.4 = (bf16[1024,1536]{1,0:T(8,128)(2,1)}, bf16[1024,1536]{1,0:T(8,128)(2,1)S(1)}, u32[]{:S(2)}) copy-start(bf16[1024,1536]{1,0:T(8,128)(2,1)S(1)} %convolution_convert_fusion.1) | copy-start | bytes 9437188
  239.1 3.2 copy-start.20
  240.4 134.0 %collective-permute-start = (bf16[512,1536]{1,0:T(8,128)(2,1)}, bf16[512,1536]{1,0:T(8,128)(2,1)}, u32[]{:S(2)}, u32[]{:S(2)}) collective-permute-start(bf16[512,1536]{1,0:T(8,128)(2,1)} %constant_dynamic-slice_fusion.7), channel_id=1, source_target_pairs={{0,1},{1,0},{2,3},{3,2},{4,5},{5,4},{6,7},{7,6},{8,9},{9,8},{10,11... | collective-permute-start | bytes 4718600 | tf_op jit(solution)/shard_map/ppermute | solution.py:898
  250.5 11.1 %collective-permute-start.7 = (bf16[192,1024]{1,0:T(8,128)(2,1)S(1)}, bf16[192,1024]{1,0:T(8,128)(2,1)S(1)}, u32[]{:S(2)}, u32[]{:S(2)}) collective-permute-start(bf16[192,1024]{1,0:T(8,128)(2,1)S(1)} %pad_maximum_fusion.2), channel_id=1, source_target_pairs={{0,8},{8,16},{16,24},{24,28},{28,20},{20,12},{12,4},{4,0},{1,9},{9... | collective-permute-start | bytes 1179656 | tf_op jit(solution)/shard_map/ppermute | solution.py:920
  255.3 41.8 %collective-permute-start.1 = (bf16[512,1536]{1,0:T(8,128)(2,1)}, bf16[512,1536]{1,0:T(8,128)(2,1)}, u32[]{:S(2)}, u32[]{:S(2)}) collective-permute-start(bf16[512,1536]{1,0:T(8,128)(2,1)} %constant_dynamic-slice_fusion.6), channel_id=1, source_target_pairs={{0,1},{1,0},{2,3},{3,2},{4,5},{5,4},{6,7},{7,6},{8,9},{9,8},{10,11... | collective-permute-start | bytes 4718600 | tf_op jit(solution)/shard_map/ppermute | solution.py:898
  255.3 22.2 %collective-permute-start.11 = (bf16[192,1024]{1,0:T(8,128)(2,1)S(1)}, bf16[192,1024]{1,0:T(8,128)(2,1)S(1)}, u32[]{:S(2)}, u32[]{:S(2)}) collective-permute-start(bf16[192,1024]{1,0:T(8,128)(2,1)S(1)} %pad_maximum_fusion.3), channel_id=1, source_target_pairs={{8,0},{16,8},{24,16},{28,24},{20,28},{12,20},{4,12},{0,4},{9,1},{1... | collective-permute-start | bytes 1179656 | tf_op jit(solution)/shard_map/ppermute | solution.py:923
  262.8 14.8 %collective-permute-start.8 = (bf16[192,1024]{1,0:T(8,128)(2,1)S(1)}, bf16[192,1024]{1,0:T(8,128)(2,1)S(1)}, u32[]{:S(2)}, u32[]{:S(2)}) collective-permute-start(bf16[192,1024]{1,0:T(8,128)(2,1)S(1)} %add_convert_fusion.6), channel_id=1, source_target_pairs={{0,8},{8,16},{16,24},{24,28},{28,20},{20,12},{12,4},{4,0},{1,9},{9... | collective-permute-start | bytes 1179656 | tf_op jit(solution)/shard_map/ppermute | solution.py:920
  274.6 1.6 copy-start.7
  277.5 23.1 %collective-permute-start.4 = (bf16[512,1536]{1,0:T(8,128)(2,1)}, bf16[512,1536]{1,0:T(8,128)(2,1)}, u32[]{:S(2)}, u32[]{:S(2)}) collective-permute-start(bf16[512,1536]{1,0:T(8,128)(2,1)} %constant_dynamic-slice_fusion.4), channel_id=1, source_target_pairs={{0,1},{1,0},{2,3},{3,2},{4,5},{5,4},{6,7},{7,6},{8,9},{9,8},{10,11... | collective-permute-start | bytes 4718600 | tf_op jit(solution)/shard_map/ppermute | solution.py:898
  279.8 13.6 %collective-permute-start.12 = (bf16[192,1024]{1,0:T(8,128)(2,1)}, bf16[192,1024]{1,0:T(8,128)(2,1)S(1)}, u32[]{:S(2)}, u32[]{:S(2)}) collective-permute-start(bf16[192,1024]{1,0:T(8,128)(2,1)} %get-tuple-element.60), channel_id=1, source_target_pairs={{8,0},{16,8},{24,16},{28,24},{20,28},{12,20},{4,12},{0,4},{9,1},{1... | collective-permute-start | bytes 1179656 | tf_op jit(solution)/shard_map/ppermute | solution.py:923
  290.3 1.7 copy-start.1
  292.0 5.6 %copy-start.6 = (bf16[1024,1536]{1,0:T(8,128)(2,1)S(1)}, bf16[1024,1536]{1,0:T(8,128)(2,1)}, u32[]{:S(2)}) copy-start(bf16[1024,1536]{1,0:T(8,128)(2,1)} %convolution_convert_fusion) | copy-start | bytes 9437188
  293.2 48.9 %collective-permute-start.3 = (bf16[512,1536]{1,0:T(8,128)(2,1)}, bf16[512,1536]{1,0:T(8,128)(2,1)}, u32[]{:S(2)}, u32[]{:S(2)}) collective-permute-start(bf16[512,1536]{1,0:T(8,128)(2,1)} %constant_dynamic-slice_fusion.5), channel_id=1, source_target_pairs={{0,1},{1,0},{2,3},{3,2},{4,5},{5,4},{6,7},{7,6},{8,9},{9,8},{10,11... | collective-permute-start | bytes 4718600 | tf_op jit(solution)/shard_map/ppermute | solution.py:898
  293.5 8.7 %copy-start.8 = (bf16[1024,1536]{1,0:T(8,128)(2,1)S(1)}, bf16[1024,1536]{1,0:T(8,128)(2,1)}, u32[]{:S(2)}) copy-start(bf16[1024,1536]{1,0:T(8,128)(2,1)} %copy-done.7) | copy-start | bytes 9437188
  293.5 11.7 %collective-permute-start.9 = (bf16[192,1024]{1,0:T(8,128)(2,1)}, bf16[192,1024]{1,0:T(8,128)(2,1)S(1)}, u32[]{:S(2)}, u32[]{:S(2)}) collective-permute-start(bf16[192,1024]{1,0:T(8,128)(2,1)} %get-tuple-element.59), channel_id=1, source_target_pairs={{0,8},{8,16},{16,24},{24,28},{28,20},{20,12},{12,4},{4,0},{1,9},{9... | collective-permute-start | bytes 1179656 | tf_op jit(solution)/shard_map/ppermute | solution.py:920
  297.0 42.7 %collective-permute-start.13 = (bf16[192,1024]{1,0:T(8,128)(2,1)}, bf16[192,1024]{1,0:T(8,128)(2,1)}, u32[]{:S(2)}, u32[]{:S(2)}) collective-permute-start(bf16[192,1024]{1,0:T(8,128)(2,1)} %add_convert_fusion.3), channel_id=1, source_target_pairs={{8,0},{16,8},{24,16},{28,24},{20,28},{12,20},{4,12},{0,4},{9,1},{1... | collective-permute-start | bytes 1179656 | tf_op jit(solution)/shard_map/ppermute | solution.py:923
  300.6 5.9 %copy-start.22 = (bf16[1024,1024]{1,0:T(8,128)(2,1)S(1)}, bf16[1024,1024]{1,0:T(8,128)(2,1)}, u32[]{:S(2)}) copy-start(bf16[1024,1024]{1,0:T(8,128)(2,1)} %get-tuple-element.49) | copy-start | bytes 6291460
  300.6 5.9 %copy-start.23 = (bf16[1024,1024]{1,0:T(8,128)(2,1)S(1)}, bf16[1024,1024]{1,0:T(8,128)(2,1)}, u32[]{:S(2)}) copy-start(bf16[1024,1024]{1,0:T(8,128)(2,1)} %get-tuple-element.50) | copy-start | bytes 6291460
  300.6 73.8 %collective-permute-start.2 = (bf16[512,1536]{1,0:T(8,128)(2,1)}, bf16[512,1536]{1,0:T(8,128)(2,1)}, u32[]{:S(2)}, u32[]{:S(2)}) collective-permute-start(bf16[512,1536]{1,0:T(8,128)(2,1)} %add_convert_fusion.2), channel_id=1, source_target_pairs={{0,2},{1,3},{2,0},{3,1},{4,6},{5,7},{6,4},{7,5},{8,10},{9,11},{10,... | collective-permute-start | bytes 4718600 | tf_op jit(solution)/shard_map/ppermute | solution.py:902
  305.1 1.4 copy-start.14
  305.1 65.5 %collective-permute-start.5 = (bf16[512,1536]{1,0:T(8,128)(2,1)}, bf16[512,1536]{1,0:T(8,128)(2,1)}, u32[]{:S(2)}, u32[]{:S(2)}) collective-permute-start(bf16[512,1536]{1,0:T(8,128)(2,1)} %add_convert_fusion), channel_id=1, source_target_pairs={{0,2},{1,3},{2,0},{3,1},{4,6},{5,7},{6,4},{7,5},{8,10},{9,11},{10,... | collective-permute-start | bytes 4718600 | tf_op jit(solution)/shard_map/ppermute | solution.py:902
  306.5 31.3 %copy-start.12 = (bf16[192,1024]{1,0:T(8,128)(2,1)S(1)}, bf16[192,1024]{1,0:T(8,128)(2,1)}, u32[]{:S(2)}) copy-start(bf16[192,1024]{1,0:T(8,128)(2,1)} %param.27) | copy-start | bytes 1179652
  336.8 33.9 %copy-start = (f32[512,1536]{1,0:T(8,128)S(1)}, f32[512,1536]{1,0:T(8,128)}, u32[]{:S(2)}) copy-start(f32[512,1536]{1,0:T(8,128)} %get-tuple-element.27) | copy-start | bytes 9437188
  370.7 3.7 copy-start.2
  370.7 4.3 copy-start.5
  370.7 4.7 copy-start.10
  512.4 5.2 copy-start.13
  512.4 5.4 %copy-start.16 = (bf16[192]{0:T(256)(128)(2,1)S(1)}, bf16[192]{0:T(256)(128)(2,1)}, u32[]{:S(2)}) copy-start(bf16[192]{0:T(256)(128)(2,1)} %param.25) | copy-start | bytes 1156
  512.4 6.0 %copy-start.17 = (bf16[192]{0:T(256)(128)(2,1)S(1)}, bf16[192]{0:T(256)(128)(2,1)}, u32[]{:S(2)}) copy-start(bf16[192]{0:T(256)(128)(2,1)} %param.20) | copy-start | bytes 1156
  512.4 9.0 %copy-start.11 = (bf16[512,1536]{1,0:T(8,128)(2,1)S(1)}, bf16[512,1536]{1,0:T(8,128)(2,1)}, u32[]{:S(2)}) copy-start(bf16[512,1536]{1,0:T(8,128)(2,1)} %get-tuple-element.98) | copy-start | bytes 4718596
  517.6 5.0 copy-start.15
